TPU v7x, 128 devices: a whole 4x4x4 slice. The times are simulated.
128 devices in a mesh: section: 8 (over x, core), tensor: 16 (over y, z).
Axes of the slice: x: 4, y: 4, z: 4, core: 2. Of those that a mesh axis runs over, the one named last changes fastest.
Arguments:
- hidden: bfloat16 [512, 4608], P(('section', 'tensor')), may hold values from -0.59765625 to 0.59765625
- norm_gain: float32 [4608], replicated, may hold values from 0.5 to 1.5
- head_weight: bfloat16 [128000, 4608], P(('section', 'tensor')), as said below
- targets: int32 [512], replicated, may hold values from 0 to 127999
Outputs:
- token_loss: float32 [512], P(('section', 'tensor'))
- grad_gain: float32 [4608], replicated
- grad_hidden: float32 [512, 4608], P(('section', 'tensor'))
- grad_head: bfloat16 [128000, 4608], P(('section', 'tensor'))
Inputs may be any that keep to these rules, and one draw needn't show every extreme that they name: head_weight entries are finite and at most 19.5 times 4608^-0.5 in magnitude.
All inputs are finite; a program needn't handle non-finite values.
Results may differ from a plain program's by a relative error of at most 0.0054.
Values may be sent and summed in bfloat16 or wider, within the bound.
No kernel may reach another device: no remote copies, remote signals or barrier semaphores. Data moves between devices by JAX's collectives and lax.ppermute only.
A program may use at most 128 MiB of HBM per device.

v0:
```python
import jax
import jax.numpy as jnp
from jax import lax
from jax.sharding import PartitionSpec as P

soft_cap = 30.0
norm_eps = 1e-06


def normalize(values):
    root_mean = jnp.sqrt(jnp.mean(values * values, axis=1, keepdims=True) + norm_eps)
    return (root_mean, values / root_mean)


def norm_backward(grad_normed, unit_rows, root_mean, norm_gain):
    grad_unit = grad_normed * norm_gain[None, :]
    inner_mean = jnp.mean(grad_unit * unit_rows, axis=1, keepdims=True)
    return (grad_unit - unit_rows * inner_mean) / root_mean


def body(hidden, norm_gain, head_weight, targets):
    rows_dev = hidden.shape[0]
    vocab_dev = head_weight.shape[0]
    device = lax.axis_index("section") * lax.axis_size("tensor") + lax.axis_index("tensor")
    gathered = lax.all_gather(hidden, ("section", "tensor"), axis=0, tiled=True)
    root_mean, unit_rows = normalize(gathered.astype(jnp.float32))
    normed = (unit_rows * norm_gain[None, :]).astype(jnp.bfloat16)
    raw_logits = lax.dot_general(
        normed, head_weight, (((1,), (1,)), ((), ())), preferred_element_type=jnp.float32
    )
    capped = soft_cap * jnp.tanh(raw_logits / soft_cap)
    scaled_exp = jnp.exp(capped)
    columns = lax.iota(jnp.int32, vocab_dev) + device * vocab_dev
    onehot = columns[None, :] == targets[:, None]
    local_total = jnp.sum(scaled_exp, axis=1)
    local_picked = jnp.sum(jnp.where(onehot, capped, jnp.zeros_like(capped)), axis=1)
    exp_total, picked = lax.psum((local_total, local_picked), ("section", "tensor"))
    row_start = device * rows_dev
    token_loss = lax.dynamic_slice_in_dim(jnp.log(exp_total) - picked, row_start, rows_dev, 0)
    cap_slope = 1.0 - (capped / soft_cap) ** 2
    dlogit = ((scaled_exp / exp_total[:, None] - onehot.astype(jnp.float32)) * cap_slope).astype(
        jnp.bfloat16
    )
    grad_head = lax.dot_general(
        dlogit, normed, (((0,), (0,)), ((), ())), preferred_element_type=jnp.float32
    ).astype(jnp.bfloat16)
    local_grad = jnp.dot(dlogit, head_weight, preferred_element_type=jnp.float32)
    grad_normed = lax.psum(local_grad, ("section", "tensor"))
    grad_gain = jnp.sum(grad_normed * unit_rows, axis=0)
    every_grad = norm_backward(grad_normed, unit_rows, root_mean, norm_gain)
    grad_hidden = lax.dynamic_slice_in_dim(every_grad, row_start, rows_dev, 0)
    return (token_loss, grad_gain, grad_hidden, grad_head)


def solution(mesh):
    placed = (P(("section", "tensor"), None), P(), P(("section", "tensor"), None), P())
    return jax.shard_map(
        body,
        mesh=mesh,
        in_specs=placed,
        out_specs=(
            P(("section", "tensor")),
            P(),
            P(("section", "tensor"), None),
            P(("section", "tensor"), None),
        ),
        check_vma=False,
    )
```

profile of v0, /device:TPU:1, one launch (start us, length us, event | category | flops | bytes accessed | tf_op | source)
XLA Modules:
  0.0 363.6 jit_solution(14939950825926150857)
XLA Ops:
  7.2 0.0 all-gather.3.cloned.1.call-start
  7.2 0.7 all-gather.3.cloned.1.call-update
  7.9 0.0 all-reduce.3.cloned.1.call-start
  8.0 73.9 %all-gather.3.cloned.1.call-done = bf16[128,4,4608]{2,1,0:T(4,128)(2,1)} async-done(((bf16[1,4,4608]{2,1,0:T(4,128)(2,1)}), bf16[128,4,4608]{2,1,0:T(4,128)(2,1)}) %all-gather.3.cloned.1.call-update) | async-done | bytes 4718608 | tf_op jit(solution)/shard_map/all_gather | solution.py:25
  81.8 7.7 %reshape.29 = f32[512,4608]{1,0:T(8,128)} reshape(bf16[128,4,4608]{2,1,0:T(4,128)(2,1)} %all-gather.3.cloned.1.call-done) | data formatting | bytes 14155776 | tf_op jit(solution)/shard_map/convert_element_type | solution.py:26
  89.5 0.0 copy-start
  89.5 4.5 %multiply_reduce_fusion.2 = f32[512]{0:T(512)S(1)} fusion(f32[512,4608]{1,0:T(8,128)} %reshape.29), kind=kLoop, calls=%fused_computation.3 | loop fusion | flops 4718080 | bytes 9439232 | tf_op jit(solution)/shard_map/reduce_sum | solution.py:11
  94.1 1.8 copy-done
  95.9 0.0 copy-start.2
  95.9 0.0 copy-start.3
  95.9 1.2 broadcast_divide_fusion
  97.1 0.0 copy-done.2
  97.1 0.0 copy-done.3
  97.1 0.0 copy-start.1
  97.1 13.7 %exponential_reduce_fusion = (f32[512]{0:T(512)S(1)}, f32[512]{0:T(512)S(1)}, f32[512,1000]{0,1:T(8,128)}) fusion(s32[512]{0:T(512)S(1)} %copy-done.3, s32[1000]{0:T(1024)S(1)} %iota_add_fusion, bf16[1000,4608]{1,0:T(8,128)(2,1)} %param.6, f32[512,4608]{1,0:T(8,128)S(1)} %broadcast_divide_fusion, f32[4608]{0:T(1024)S(1)} %copy-done.2), kind=kOutput, calls=%fused_computation.14 | convolution fusion | flops 4726381568 | bytes 20729760 | tf_op jit(solution)/shard_map/dot_general | solution.py:28
  110.8 0.0 copy-done.1
  110.8 62.5 %all-reduce = (f32[512]{0:T(512)S(1)}, f32[512]{0:T(512)S(1)}) all-reduce(f32[512]{0:T(512)S(1)} %get-tuple-element.7, f32[512]{0:T(512)S(1)} %get-tuple-element.6), channel_id=1, replica_groups=mesh['section'=8,'tensor'=16] {'section','tensor'}, use_global_device_ids=true, to_apply=%region_4.5 | all-reduce | flops 1024 | bytes 8192 | tf_op jit(solution)/shard_map/psum | solution.py:37
  173.3 11.2 %fusion.7 = f32[512,4608]{1,0:T(8,128)} fusion(bf16[1000,4608]{1,0:T(8,128)(2,1)} %param.6, f32[512,1000]{0,1:T(8,128)} %get-tuple-element.11, f32[512]{0:T(512)S(1)} %get-tuple-element.9, s32[512]{0:T(512)S(1)} %copy-done.3, s32[1000]{0:T(1024)S(1)} %iota_add_fusion), kind=kOutput, calls=%fused_computation.23 | convolution fusion | flops 4723200000 | bytes 20709280 | tf_op jit(solution)/shard_map/dot_general | solution.py:47
  184.5 0.0 copy-start.4
  184.5 0.0 all-reduce.3.cloned.1.call-update
  184.5 0.1 dynamic-slice.1
  184.6 0.6 dynamic_slice.6
  185.2 0.9 copy-done.4
  186.1 11.7 %convolution_convert_fusion = bf16[1000,4608]{1,0:T(8,128)(2,1)} fusion(f32[512,4608]{1,0:T(8,128)} %copy-done.1, f32[4608]{0:T(1024)S(1)} %copy-done.2, f32[512,1000]{0,1:T(8,128)S(1)} %copy-done.4, f32[512]{0:T(512)S(1)} %get-tuple-element.9, s32[512]{0:T(512)S(1)} %copy-done.3, s32[1000]{0:T(1024)S(1)} %iota_add_fusion), kind=kOutput, calls=%fused_computation.4 | convolution fusion | flops 4732526592 | bytes 20727712 | tf_op jit(solution)/shard_map/dot_general | solution.py:44
  197.8 148.1 %all-reduce.3.cloned.1.call-done = f32[512,4608]{1,0:T(8,128)} async-done(((f32[512,4608]{1,0:T(8,128)}), f32[512,4608]{1,0:T(8,128)}) %all-reduce.3.cloned.1.call-update) | async-done | bytes 9437200 | tf_op jit(solution)/shard_map/psum | solution.py:48
  345.8 9.2 %multiply_reduce_fusion = (f32[512]{0:T(512)S(1)}, f32[4608]{0:T(1024)}, f32[512,4608]{1,0:T(8,128)S(1)}) fusion(f32[512,4608]{1,0:T(8,128)} %all-reduce.3.cloned.1.call-done, f32[4608]{0:T(1024)S(1)} %copy-done.2, f32[512,4608]{1,0:T(8,128)} %reshape.29, f32[512]{0:T(512)S(1)} %add_sqrt_fusion), kind=kLoop, calls=%fused_computation | loop fusion | flops 14150656 | bytes 28352512 | tf_op jit(solution)/shard_map/reduce_sum | solution.py:17
  355.1 0.1 dynamic-slice
  355.2 1.6 fusion.5
  (4 shorter events, 0.0 us)
Async XLA Ops:
  7.2 74.7 %all-gather.3.cloned.1.call-start = ((), (), s32[]{:S(2)}) async-start(), calls=%async_computation.1 | async-start | bytes 4755456 | tf_op jit(solution)/shard_map/all_gather | solution.py:25
  7.9 337.9 %all-reduce.3.cloned.1.call-start = ((), (), s32[]{:S(2)}) async-start(), calls=%async_computation | async-start | bytes 18874368 | tf_op jit(solution)/shard_map/psum | solution.py:48
  89.5 6.4 %copy-start = (f32[512,4608]{1,0:T(8,128)S(1)}, f32[512,4608]{1,0:T(8,128)}, u32[]{:S(2)}) copy-start(f32[512,4608]{1,0:T(8,128)} %reshape.29) | copy-start | bytes 28311556
  95.9 1.2 copy-start.2
  95.9 1.2 copy-start.3
  97.1 13.7 %copy-start.1 = (f32[512,4608]{1,0:T(8,128)}, f32[512,4608]{1,0:T(8,128)S(1)}, u32[]{:S(2)}) copy-start(f32[512,4608]{1,0:T(8,128)S(1)} %broadcast_divide_fusion) | copy-start | bytes 28311556
  184.5 1.6 copy-start.4
Sparse Core Ops, SparseCore 0:
  11.1 70.6 all-gather.2
  184.7 161.1 all-reduce.2
where the time goes:
time: 364 us
  waiting for transfers between devices  223 us (61%)
  blocking collectives  62.5 us (17%)
  matrix products  36.5 us (10%)
  other arithmetic  16.6 us (5%)
  between operations  14.1 us (4%)
  local copies, waits for them, and re-layouts  11.2 us (3%)
    psum x1, waiting for transfers between devices, body(): grad_normed = lax.psum(local_grad, ('section', 'tensor'))  148 us
    all_gather x1, waiting for transfers between devices, body(): gathered = lax.all_gather(hidden, ('section', 'tensor'), axis=0, tiled=True)  73.9 us
    psum x1, blocking collectives, body(): lax.psum((local_total, local_picked), ('section', 'tensor'))  62.5 us
    dot_general x1, matrix products, body(): lax.dot_general(normed, head_weight, (((1,), (1,)), ((), ())), preferred_...  13.7 us
    dot_general x1, matrix products, body(): lax.dot_general(dlogit, normed, (((0,), (0,)), ((), ())), preferred_eleme...  11.7 us
    dot_general x1, matrix products, body(): jnp.dot(dlogit, head_weight, preferred_element_type=jnp.float32)  11.2 us
    reduce_sum x1, other arithmetic, norm_backward(): inner_mean = jnp.mean(grad_unit * unit_rows, axis=1, keepdims=True)  9.23 us
    convert_element_type x1, local copies, waits for them, and re-layouts, body(): root_mean, unit_rows = normalize(gathered.astype(jnp.float32))  7.7 us
  transfers between devices with their start and end apart: 2, of which 2 were waited for; matrix products, arithmetic and copies ran while one was open for 3% of the time, Pallas kernels for 0%

commit v1 on v0

v1 whole, which is shorter than its diff:
```python
import functools

import jax
import jax.numpy as jnp
from jax import lax
from jax.experimental import pallas as pl
from jax.experimental.pallas import tpu as pltpu
from jax.sharding import Mesh
from jax.sharding import PartitionSpec as P

soft_cap = 30.0
norm_eps = 1e-06
f32 = jnp.float32
bf16 = jnp.bfloat16
every = ("x", "c", "y", "z")
chips = ("x", "y", "z")
n_chips = 64
tokens = 512
width = 4608
half = width // 2
tile = 768
tiles = half // tile
wide = tile + 128
vocab_tile = 256

swap_cores = [
    (((x * 2 + c) * 4 + y) * 4 + z, ((x * 2 + 1 - c) * 4 + y) * 4 + z)
    for x in range(4)
    for c in range(2)
    for y in range(4)
    for z in range(4)
]


def other_core(array):
    return lax.ppermute(array, every, swap_cores)


def params(flops=0, bytes_accessed=0, transcendentals=0):
    return dict(
        compiler_params=pltpu.CompilerParams(vmem_limit_bytes=48 << 20),
        cost_estimate=pl.CostEstimate(
            flops=flops, bytes_accessed=bytes_accessed, transcendentals=transcendentals
        ),
    )


def norm_kernel(core, mine, theirs, gain, spread, unit_out, root_out):
    first = core[0] == 0
    own = mine[...].astype(f32)
    far = theirs[...].astype(f32)
    rows = jnp.concatenate([jnp.where(first, own, far), jnp.where(first, far, own)], axis=0)
    root = jnp.sqrt(jnp.mean(rows * rows, axis=1, keepdims=True) + norm_eps)
    unit = rows / root
    normed = unit * gain[...]
    part = jnp.where(first, normed[:, :half], normed[:, half:]).astype(bf16)
    spread[...] = jnp.broadcast_to(part[None], spread.shape)
    unit_out[...] = jnp.where(first, unit[:4], unit[4:])
    root_out[...] = jnp.broadcast_to(jnp.where(first, root[:4], root[4:]), root_out.shape)


def logits_first_kernel(core, own, weight, out):
    out[...] = lax.dot_general(
        weight[...], own[...], (((1,), (1,)), ((), ())), preferred_element_type=f32
    )


def logits_kernel(vocab, core, other, weight, part, picks, capped_out, stats):
    step = pl.program_id(0)
    raw = part[...] + lax.dot_general(
        weight[...], other[...], (((1,), (1,)), ((), ())), preferred_element_type=f32
    )
    capped = soft_cap * jnp.tanh(raw / soft_cap)
    capped_out[...] = capped
    row = lax.broadcasted_iota(jnp.int32, capped.shape, 0) + step * vocab_tile
    total = jnp.sum(jnp.where(row < vocab, jnp.exp(capped), 0.0), axis=0, keepdims=True)
    hit = (row == picks[...]) & (row < vocab)
    picked = jnp.sum(jnp.where(hit, capped, 0.0), axis=0, keepdims=True)

    @pl.when(step == 0)
    def _():
        stats[...] = jnp.zeros_like(stats)

    for j in range(4):
        lanes = slice(128 * j, 128 * (j + 1))
        stats[j : j + 1, :] += total[:, lanes]
        stats[4 + j : 5 + j, :] += picked[:, lanes]


def far_grad_kernel(core, capped, total, picks, weight, normed, gain, grad_out, dlogit_out, gain_out):
    @pl.when(pl.program_id(0) == 0)
    def _():
        value = capped[...]
        row = lax.broadcasted_iota(jnp.int32, value.shape, 0)
        onehot = (row == picks[...]).astype(f32)
        slope = 1.0 - (value / soft_cap) ** 2
        dlogit_out[...] = ((jnp.exp(value) / total[...] - onehot) * slope).astype(bf16)

    grad = lax.dot_general(
        dlogit_out[...], weight[...], (((0,), (0,)), ((), ())), preferred_element_type=f32
    )
    grad_out[...] = grad.astype(bf16)
    gain_out[...] = jnp.sum(grad * normed[...].astype(f32), axis=0, keepdims=True) / gain[...]


def head_kernel(core, dlogit, own, other, out):
    near = pl.program_id(0) // tiles == core[0]

    @pl.when(near)
    def _():
        out[...] = jnp.dot(dlogit[...], own[...], preferred_element_type=f32).astype(bf16)

    @pl.when(jnp.logical_not(near))
    def _():
        out[...] = jnp.dot(dlogit[...], other[...], preferred_element_type=f32).astype(bf16)


def near_grad_kernel(core, dlogit, weight, normed, gain, received, received_gain, out):
    grad = lax.dot_general(
        dlogit[...], weight[...], (((0,), (0,)), ((), ())), preferred_element_type=f32
    )
    out[:, :tile] = (grad + received[...].astype(f32)).astype(bf16)
    part = jnp.sum(grad * normed[...].astype(f32), axis=0, keepdims=True) / gain[...]
    part = part + received_gain[...]
    rows = [part[:, 128 * j : 128 * (j + 1)] for j in range(tile // 128)]
    rows = jnp.concatenate(rows + [jnp.zeros((8 - len(rows), 128), f32)], axis=0)
    rows = jnp.broadcast_to(rows[None], (n_chips, 8, 128)).reshape(n_chips * 8, 128)
    out[:, tile:] = rows.astype(bf16)


def sum_kernel(core, blocks, keep, send):
    total = jnp.sum(blocks[...].astype(f32), axis=0)
    first = core[0] == 0
    keep[...] = jnp.zeros_like(keep)
    send[...] = jnp.zeros_like(send)
    for j in range(tiles):
        lanes = slice(tile * j, tile * (j + 1))
        grad = total[:, wide * j : wide * j + tile]
        keep[0:4, lanes] = jnp.where(first, grad[:4], grad[4:])
        send[0:4, lanes] = jnp.where(first, grad[4:], grad[:4])
        for k in range(tile // 128):
            row = total[k : k + 1, wide * j + tile : wide * (j + 1)]
            lane = slice(tile * j + 128 * k, tile * j + 128 * (k + 1))
            keep[4:5, lane] = row
            send[4:5, lane] = row


def final_kernel(core, keep, received, unit, root, gain, grad_out, gain_out):
    first = core[0] == 0
    near, far = keep[...], received[...]
    both = jnp.concatenate([jnp.where(first, near, far), jnp.where(first, far, near)], axis=1)
    gain_out[...] = both[4:5]
    grad_unit = both[0:4] * gain[...]
    rows = unit[...]
    inner = jnp.mean(grad_unit * rows, axis=1, keepdims=True)
    grad_out[...] = (grad_unit - rows * inner) / root[:, 0:1]


def call(kernel, core, args, grid, in_specs, out_specs, out_shape, scratch=(), **cost):
    return pl.pallas_call(
        kernel,
        grid_spec=pltpu.PrefetchScalarGridSpec(
            num_scalar_prefetch=1,
            grid=grid,
            in_specs=in_specs,
            out_specs=out_specs,
            scratch_shapes=scratch,
        ),
        out_shape=out_shape,
        **params(**cost),
    )(core, *args)


def shape(dims, dtype):
    return jax.ShapeDtypeStruct(dims, dtype)


def whole(*dims):
    return pl.BlockSpec(dims, lambda *_: (0,) * len(dims))


def body(hidden, norm_gain, head_weight, targets):
    vocab = head_weight.shape[0]
    place = [lax.axis_index(name) for name in every]
    device = ((place[0] * 2 + place[1]) * 4 + place[2]) * 4 + place[3]
    core = place[1][None]
    gain = norm_gain[None, :]
    picks = targets.reshape(4, 2, 16, 4).transpose(0, 2, 1, 3).reshape(1, tokens) - device * vocab

    spread, unit, root = call(
        norm_kernel,
        core,
        (hidden, other_core(hidden), gain),
        (1,),
        [whole(4, width), whole(4, width), whole(1, width)],
        [whole(n_chips, 8, half), whole(4, width), whole(4, 128)],
        [shape((n_chips, 8, half), bf16), shape((4, width), f32), shape((4, 128), f32)],
    )
    own = lax.all_to_all(spread, chips, 0, 0, tiled=True).reshape(tokens, half)
    other = other_core(own)

    blocks = pl.cdiv(vocab, vocab_tile)
    logit_flops = 2 * tokens * vocab * half
    part = call(
        logits_first_kernel,
        core,
        (own, head_weight),
        (blocks,),
        [whole(tokens, half), pl.BlockSpec((vocab_tile, half), lambda i, c: (i, c[0]))],
        pl.BlockSpec((vocab_tile, tokens), lambda i, c: (i, 0)),
        shape((vocab, tokens), f32),
        flops=logit_flops,
        bytes_accessed=9 << 20,
    )
    capped, stats = call(
        functools.partial(logits_kernel, vocab),
        core,
        (other, head_weight, part, picks),
        (blocks,),
        [
            whole(tokens, half),
            pl.BlockSpec((vocab_tile, half), lambda i, c: (i, 1 - c[0])),
            pl.BlockSpec((vocab_tile, tokens), lambda i, c: (i, 0)),
            whole(1, tokens),
        ],
        [pl.BlockSpec((vocab_tile, tokens), lambda i, c: (i, 0)), whole(8, 128)],
        [shape((vocab, tokens), f32), shape((8, 128), f32)],
        flops=logit_flops,
        bytes_accessed=11 << 20,
    )
    stats = stats + other_core(stats)
    stats = jnp.broadcast_to(stats[None], (n_chips, 8, 128))
    stats = jnp.sum(lax.all_to_all(stats, chips, 0, 0, tiled=True), axis=0)
    total = stats[:4].reshape(1, tokens)
    loss = (jnp.log(stats[:4]) - stats[4:]).reshape(n_chips, 2, 4)
    chip = (place[0] * 4 + place[2]) * 4 + place[3]
    token_loss = lax.dynamic_slice(loss, (chip, place[1], 0), (1, 1, 4)).reshape(4)

    far_grad, dlogit, far_gain = call(
        far_grad_kernel,
        core,
        (capped, total, picks, head_weight, other, gain),
        (tiles,),
        [
            whole(vocab, tokens),
            whole(1, tokens),
            whole(1, tokens),
            pl.BlockSpec((vocab, tile), lambda j, c: (0, (1 - c[0]) * tiles + j)),
            pl.BlockSpec((tokens, tile), lambda j, c: (0, j)),
            pl.BlockSpec((1, tile), lambda j, c: (0, (1 - c[0]) * tiles + j)),
        ],
        [
            pl.BlockSpec((tokens, tile), lambda j, c: (0, j)),
            whole(vocab, tokens),
            pl.BlockSpec((1, tile), lambda j, c: (0, j)),
        ],
        [shape((tokens, half), bf16), shape((vocab, tokens), bf16), shape((1, half), f32)],
        flops=logit_flops,
        bytes_accessed=12 << 20,
    )
    received = other_core(far_grad)
    received_gain = other_core(far_gain)
    grad_head = call(
        head_kernel,
        core,
        (dlogit, own, other),
        (2 * tiles,),
        [
            whole(vocab, tokens),
            pl.BlockSpec((tokens, tile), lambda j, c: (0, jnp.clip(j - c[0] * tiles, 0, tiles - 1))),
            pl.BlockSpec(
                (tokens, tile), lambda j, c: (0, jnp.clip(j - (1 - c[0]) * tiles, 0, tiles - 1))
            ),
        ],
        pl.BlockSpec((vocab, tile), lambda j, c: (0, j)),
        shape((vocab, width), bf16),
        flops=2 * logit_flops,
        bytes_accessed=15 << 20,
    )
    packed = call(
        near_grad_kernel,
        core,
        (dlogit, head_weight, own, gain, received, received_gain),
        (tiles,),
        [
            whole(vocab, tokens),
            pl.BlockSpec((vocab, tile), lambda j, c: (0, c[0] * tiles + j)),
            pl.BlockSpec((tokens, tile), lambda j, c: (0, j)),
            pl.BlockSpec((1, tile), lambda j, c: (0, c[0] * tiles + j)),
            pl.BlockSpec((tokens, tile), lambda j, c: (0, j)),
            pl.BlockSpec((1, tile), lambda j, c: (0, j)),
        ],
        pl.BlockSpec((tokens, wide), lambda j, c: (0, j)),
        shape((tokens, tiles * wide), bf16),
        flops=logit_flops,
        bytes_accessed=13 << 20,
    )
    packed = packed.reshape(n_chips, 8, tiles * wide)
    packed = lax.all_to_all(packed, chips, 0, 0, tiled=True)
    keep, send = call(
        sum_kernel,
        core,
        (packed,),
        (1,),
        [whole(n_chips, 8, tiles * wide)],
        [whole(8, half), whole(8, half)],
        [shape((8, half), f32), shape((8, half), f32)],
    )
    grad_hidden, grad_gain = call(
        final_kernel,
        core,
        (keep, other_core(send), unit, root, gain),
        (1,),
        [whole(8, half), whole(8, half), whole(4, width), whole(4, 128), whole(1, width)],
        [whole(4, width), whole(1, width)],
        [shape((4, width), f32), shape((1, width), f32)],
    )
    return (token_loss, grad_gain.reshape(width), grad_hidden, grad_head)


def solution(mesh):
    fine = Mesh(mesh.devices.reshape(4, 2, 4, 4), every)
    rows = P(every, None)
    return jax.shard_map(
        body,
        mesh=fine,
        in_specs=(rows, P(), rows, P()),
        out_specs=(P(every), P(), rows, rows),
        check_vma=False,
    )
```

time: 364 us -> 147 us (0.40)
  waiting for transfers between devices: 223 us -> 32.7 us
  Pallas kernels: 0 us -> 36.8 us
  matrix products: 36.5 us -> 0 us
  other arithmetic: 16.6 us -> 0.73 us
  between operations: 14.1 us -> 0.76 us
  starting transfers between devices: 0.08 us -> 12.1 us
  local copies, waits for them, and re-layouts: 11.2 us -> 5.33 us
  blocking collectives: 62.5 us -> 57.9 us
    psum x1 -> x0, waiting for transfers between devices: 148 us -> none  [body(): grad_normed = lax.psum(local_grad, ('section', 'tensor'))]
    all_gather x1 -> x0, waiting for transfers between devices: 73.9 us -> none  [body(): gathered = lax.all_gather(hidden, ('section', 'tensor'), axis=0, tiled=True)]
    psum x1 -> x0, blocking collectives: 62.5 us -> none  [body(): lax.psum((local_total, local_picked), ('section', 'tensor'))]
    all_to_all x0 -> x2, blocking collectives: none -> 57.9 us  [the longest x1 42.9 us: body(): own = lax.all_to_all(spread, chips, 0, 0, tiled=True).reshape(tokens, half)]
    pallas_call x0 -> x8, Pallas kernels: none -> 36.8 us  [call(): pl.pallas_call(kernel, grid_spec=pltpu.PrefetchScalarGridSpec(num_scalar_...]
    dot_general x3 -> x0, matrix products: 36.5 us -> none  [the longest x1 13.7 us: body(): lax.dot_general(normed, head_weight, (((1,), (1,)), ((), ())), preferred_...]
    all_to_all x0 -> x1, waiting for transfers between devices: none -> 26.7 us  [body(): packed = lax.all_to_all(packed, chips, 0, 0, tiled=True)]
    reduce_sum x2 -> x1, other arithmetic: 13.8 us -> 0.07 us  [body(): stats = jnp.sum(lax.all_to_all(stats, chips, 0, 0, tiled=True), axis=0)]
  transfers between devices with their start and end apart: 2 -> 7, of which waited for: 2 -> 5; matrix products, arithmetic and copies ran while one was open for 3% -> 1% of each run, Pallas kernels for 0% -> 10%
where the time goes in v1:
time: 147 us; the launch traced here: 146 us
  blocking collectives  57.9 us (39%)
  Pallas kernels  36.8 us (25%)
  waiting for transfers between devices  32.7 us (22%)
  starting transfers between devices  12.1 us (8%)
  local copies, waits for them, and re-layouts  5.33 us (4%)
    all_to_all x1, blocking collectives, body(): own = lax.all_to_all(spread, chips, 0, 0, tiled=True).reshape(tokens, half)  42.9 us
    pallas_call x8, Pallas kernels, call(): pl.pallas_call(kernel, grid_spec=pltpu.PrefetchScalarGridSpec(num_scalar_...  36.8 us
    all_to_all x1, waiting for transfers between devices, body(): packed = lax.all_to_all(packed, chips, 0, 0, tiled=True)  26.7 us
    all_to_all x1, blocking collectives, body(): stats = jnp.sum(lax.all_to_all(stats, chips, 0, 0, tiled=True), axis=0)  15 us
    ppermute x6, starting transfers between devices, other_core(): return lax.ppermute(array, every, swap_cores)  6.56 us
    ppermute x6, waiting for transfers between devices, other_core(): return lax.ppermute(array, every, swap_cores)  5.98 us
    all_to_all x1, starting transfers between devices, body(): packed = lax.all_to_all(packed, chips, 0, 0, tiled=True)  5.57 us
    unnamed x8, local copies, waits for them, and re-layouts  3.64 us
  transfers between devices with their start and end apart: 7, of which 5 were waited for; matrix products, arithmetic and copies ran while one was open for 1% of the time, Pallas kernels for 10%

profile of v1, /device:TPU:1, one launch (start us, length us, event | category | flops | bytes accessed | tf_op | source)
XLA Modules:
  0.0 146.2 jit_solution(4107747003835056455)
XLA Ops:
  0.6 1.5 %collective-permute-start = (bf16[4,4608]{1,0:T(4,128)(2,1)}, bf16[4,4608]{1,0:T(4,128)(2,1)S(1)}, u32[]{:S(2)}, u32[]{:S(2)}) collective-permute-start(bf16[4,4608]{1,0:T(4,128)(2,1)} %mine.1), channel_id=1, source_target_pairs={{0,16},{1,17},{2,18},{3,19},{4,20},{5,21},{6,22},{7,23},{8,24},{9,... | collective-permute-start | bytes 110600 | tf_op jit(solution)/shard_map/ppermute | solution.py:36
  2.1 0.7 broadcast_in_dim.13.gain
  2.9 0.3 collective-permute-done.theirs
  3.2 0.0 copy-start.2
  3.2 0.8 copy-done.2
  4.0 0.3 shard_map.75
  4.3 0.0 copy-start.3
  4.3 42.9 %all_to_all.15 = bf16[64,8,2304]{2,1,0:T(8,128)(2,1)S(1)} all-to-all(bf16[64,8,2304]{2,1,0:T(8,128)(2,1)S(1)} %get-tuple-element.16), channel_id=1, replica_groups=mesh['x'=4,'c'=2,'y'=4,'z'=4] {'x','y','z'}, dimensions={0} | all-to-all | bytes 4718592 | tf_op jit(solution)/shard_map/all_to_all | solution.py:199
  47.2 2.0 %collective-permute-start.1 = (bf16[512,2304]{1,0:T(8,128)(2,1)S(1)}, bf16[512,2304]{1,0:T(8,128)(2,1)}, u32[]{:S(2)}, u32[]{:S(2)}) collective-permute-start(bf16[512,2304]{1,0:T(8,128)(2,1)S(1)} %bitcast.7), channel_id=1, source_target_pairs={{0,16},{1,17},{2,18},{3,19},{4,20},{5,21},{6,22},{7,23},{8,24},{9,... | collective-permute-start | bytes 7077896 | tf_op jit(solution)/shard_map/ppermute | solution.py:36
  49.2 0.0 copy-done.3
  49.2 0.1 sub.17
  49.3 0.1 sub.19.picks
  49.5 5.3 %shard_map.76.part = f32[1000,512]{1,0:T(8,128)S(1)} custom-call(s32[1]{0:T(128)} %bitcast.core, bf16[512,2304]{1,0:T(8,128)(2,1)S(1)} %bitcast.8, bf16[1000,4608]{1,0:T(8,128)(2,1)} %weight.7), custom_call_target="tpu_custom_call" | custom-call | flops 2359296000 | bytes 9437184 | tf_op jit(solution)/shard_map/pallas_call | solution.py:160
  54.7 0.0 collective-permute-done.1.other.normed
  54.7 6.5 %shard_map.77 = (f32[1000,512]{1,0:T(8,128)S(1)}, f32[8,128]{1,0:T(8,128)S(1)}) custom-call(s32[1]{0:T(128)} %bitcast.core, bf16[512,2304]{1,0:T(8,128)(2,1)} %collective-permute-done.1.other.normed, bf16[1000,4608]{1,0:T(8,128)(2,1)} %weight.7, f32[1000,512]{1,0:T(8,128)S(1)} %shard_map.76.part, s32[1,512]{1,0:T(1,128)S(1)} %sub.19.picks), custom_call_target="tpu_custom_call" | custom-call | flops 2359296000 | bytes 11534336 | tf_op jit(solution)/shard_map/pallas_call | solution.py:160
  61.3 0.0 copy-start
  61.3 1.3 copy-done
  62.6 0.0 collective-permute-start.2
  62.6 1.2 collective-permute-done.2
  63.8 15.0 %all_to_all.16 = f32[64,8,128]{2,1,0:T(8,128)S(1)} all-to-all(f32[64,8,128]{2,1,0:T(8,128)S(1)} %broadcast_in_dim.14), channel_id=1, replica_groups=mesh['x'=4,'c'=2,'y'=4,'z'=4] {'x','y','z'}, dimensions={0} | all-to-all | bytes 524288 | tf_op jit(solution)/shard_map/all_to_all | solution.py:233
  78.8 0.1 reduce_sum.9
  78.8 0.0 copy-start.1
  78.9 1.6 %copy-done.1 = f32[1000,512]{1,0:T(8,128)S(1)} copy-done((f32[1000,512]{1,0:T(8,128)S(1)}, f32[1000,512]{1,0:T(8,128)}, u32[]{:S(2)}) %copy-start.1) | copy-done | bytes 2048024
  80.4 6.1 %shard_map.78 = (bf16[512,2304]{1,0:T(8,128)(2,1)S(1)}, bf16[1000,512]{1,0:T(8,128)(2,1)S(1)}, f32[1,2304]{1,0:T(1,128)S(1)}) custom-call(s32[1]{0:T(128)} %bitcast.core, f32[1000,512]{1,0:T(8,128)S(1)} %copy-done.1, f32[1,512]{1,0:T(1,128)S(1)} %bitcast.11, s32[1,512]{1,0:T(1,128)S(1)} %sub.19.picks, bf16[1000,4608]{1,0:T(8,128)(2,1)} %weight.7, ...), custom_call_target="tpu_custom_call" | custom-call | flops 2359296000 | bytes 12582912 | tf_op jit(solution)/shard_map/pallas_call | solution.py:160
  86.6 1.6 %collective-permute-start.3 = (bf16[512,2304]{1,0:T(8,128)(2,1)S(1)}, bf16[512,2304]{1,0:T(8,128)(2,1)S(1)}, u32[]{:S(2)}, u32[]{:S(2)}) collective-permute-start(bf16[512,2304]{1,0:T(8,128)(2,1)S(1)} %get-tuple-element.20), channel_id=1, source_target_pairs={{0,16},{1,17},{2,18},{3,19},{4,20},{5,21},{6,22},{7,23},{8,24},{9,... | collective-permute-start | bytes 7077896 | tf_op jit(solution)/shard_map/ppermute | solution.py:36
  88.1 0.1 collective-permute-start.4
  88.2 4.1 %collective-permute-done.4.received_gain = f32[1,2304]{1,0:T(1,128)S(1)} collective-permute-done((f32[1,2304]{1,0:T(1,128)S(1)}, f32[1,2304]{1,0:T(1,128)S(1)}, u32[]{:S(2)}, u32[]{:S(2)}) %collective-permute-start.4) | collective-permute-done | bytes 9248 | tf_op jit(solution)/shard_map/ppermute | solution.py:36
  92.3 0.0 collective-permute-done.3.received
  92.3 6.3 %shard_map.79 = bf16[512,2688]{1,0:T(8,128)(2,1)} custom-call(s32[1]{0:T(128)} %bitcast.core, bf16[1000,512]{1,0:T(8,128)(2,1)S(1)} %get-tuple-element.19.dlogit, bf16[1000,4608]{1,0:T(8,128)(2,1)} %weight.7, bf16[512,2304]{1,0:T(8,128)(2,1)S(1)} %bitcast.9, f32[1,4608]{1,0:T(1,128)S(1)} %broadcast_in_dim.13.gain, ...), custom_call_target="tpu_custom_call" | custom-call | flops 2359296000 | bytes 13631488 | tf_op jit(solution)/shard_map/pallas_call | solution.py:160
  98.7 5.6 %all-to-all-start.2 = ((bf16[64,8,2688]{2,1,0:T(8,128)(2,1)}), bf16[64,8,2688]{2,1,0:T(8,128)(2,1)}, u32[]{:S(2)}, u32[]{:S(2)}) async-start(bf16[64,8,2688]{2,1,0:T(8,128)(2,1)} %bitcast.12), calls=%async_computation.2 | async-start | bytes 5505024 | tf_op jit(solution)/shard_map/all_to_all | solution.py:299
  104.3 0.1 reshape.46
  104.4 9.2 %shard_map.82 = bf16[1000,4608]{1,0:T(8,128)(2,1)} custom-call(s32[1]{0:T(128)} %bitcast.core, bf16[1000,512]{1,0:T(8,128)(2,1)S(1)} %get-tuple-element.19.dlogit, bf16[512,2304]{1,0:T(8,128)(2,1)S(1)} %bitcast.10, bf16[512,2304]{1,0:T(8,128)(2,1)} %collective-permute-done.1.other.normed), custom_call_target="tpu_custom_call" | custom-call | flops 4718592000 | bytes 15728640 | tf_op jit(solution)/shard_map/pallas_call | solution.py:160
  113.6 26.7 %all-to-all-done.2.blocks = bf16[64,8,2688]{2,1,0:T(8,128)(2,1)} async-done(((bf16[64,8,2688]{2,1,0:T(8,128)(2,1)}), bf16[64,8,2688]{2,1,0:T(8,128)(2,1)}, u32[]{:S(2)}, u32[]{:S(2)}) %all-to-all-start.2) | async-done | bytes 2752544 | tf_op jit(solution)/shard_map/all_to_all | solution.py:299
  140.3 2.2 %shard_map.80 = (f32[8,2304]{1,0:T(8,128)S(1)}, f32[8,2304]{1,0:T(8,128)S(1)}) custom-call(s32[1]{0:T(128)} %bitcast.core, bf16[64,8,2688]{2,1,0:T(8,128)(2,1)} %all-to-all-done.2.blocks), custom_call_target="tpu_custom_call" | custom-call | tf_op jit(solution)/shard_map/pallas_call | solution.py:160
  142.5 1.4 collective-permute-start.5
  143.9 0.5 dynamic-slice_bitcast_fusion
  144.4 0.4 collective-permute-done.5.received
  144.8 0.8 shard_map.81
  145.5 0.7 reduce
  (5 shorter events, 0.1 us)
Async XLA Ops:
  0.6 2.6 %collective-permute-start = (bf16[4,4608]{1,0:T(4,128)(2,1)}, bf16[4,4608]{1,0:T(4,128)(2,1)S(1)}, u32[]{:S(2)}, u32[]{:S(2)}) collective-permute-start(bf16[4,4608]{1,0:T(4,128)(2,1)} %mine.1), channel_id=1, source_target_pairs={{0,16},{1,17},{2,18},{3,19},{4,20},{5,21},{6,22},{7,23},{8,24},{9,... | collective-permute-start | bytes 110600 | tf_op jit(solution)/shard_map/ppermute | solution.py:36
  3.2 0.8 copy-start.2
  4.3 44.9 %copy-start.3 = (s32[512]{0:T(512)S(1)}, s32[512]{0:T(512)}, u32[]{:S(2)}) copy-start(s32[512]{0:T(512)} %param.7) | copy-start | bytes 6148
  47.2 7.6 %collective-permute-start.1 = (bf16[512,2304]{1,0:T(8,128)(2,1)S(1)}, bf16[512,2304]{1,0:T(8,128)(2,1)}, u32[]{:S(2)}, u32[]{:S(2)}) collective-permute-start(bf16[512,2304]{1,0:T(8,128)(2,1)S(1)} %bitcast.7), channel_id=1, source_target_pairs={{0,16},{1,17},{2,18},{3,19},{4,20},{5,21},{6,22},{7,23},{8,24},{9,... | collective-permute-start | bytes 7077896 | tf_op jit(solution)/shard_map/ppermute | solution.py:36
  61.3 1.3 copy-start
  62.6 1.2 collective-permute-start.2
  78.8 1.6 %copy-start.1 = (f32[1000,512]{1,0:T(8,128)S(1)}, f32[1000,512]{1,0:T(8,128)}, u32[]{:S(2)}) copy-start(f32[1000,512]{1,0:T(8,128)} %copy-done) | copy-start | bytes 6144004
  86.6 5.8 %collective-permute-start.3 = (bf16[512,2304]{1,0:T(8,128)(2,1)S(1)}, bf16[512,2304]{1,0:T(8,128)(2,1)S(1)}, u32[]{:S(2)}, u32[]{:S(2)}) collective-permute-start(bf16[512,2304]{1,0:T(8,128)(2,1)S(1)} %get-tuple-element.20), channel_id=1, source_target_pairs={{0,16},{1,17},{2,18},{3,19},{4,20},{5,21},{6,22},{7,23},{8,24},{9,... | collective-permute-start | bytes 7077896 | tf_op jit(solution)/shard_map/ppermute | solution.py:36
  88.1 4.2 %collective-permute-start.4 = (f32[1,2304]{1,0:T(1,128)S(1)}, f32[1,2304]{1,0:T(1,128)S(1)}, u32[]{:S(2)}, u32[]{:S(2)}) collective-permute-start(f32[1,2304]{1,0:T(1,128)S(1)} %get-tuple-element.21), channel_id=1, source_target_pairs={{0,16},{1,17},{2,18},{3,19},{4,20},{5,21},{6,22},{7,23},{8,24},{9,... | collective-permute-start | bytes 27656 | tf_op jit(solution)/shard_map/ppermute | solution.py:36
  98.7 41.6 %all-to-all-start.2 = ((bf16[64,8,2688]{2,1,0:T(8,128)(2,1)}), bf16[64,8,2688]{2,1,0:T(8,128)(2,1)}, u32[]{:S(2)}, u32[]{:S(2)}) async-start(bf16[64,8,2688]{2,1,0:T(8,128)(2,1)} %bitcast.12), calls=%async_computation.2 | async-start | bytes 5505024 | tf_op jit(solution)/shard_map/all_to_all | solution.py:299
  142.5 2.3 %collective-permute-start.5 = (f32[8,2304]{1,0:T(8,128)S(1)}, f32[8,2304]{1,0:T(8,128)S(1)}, u32[]{:S(2)}, u32[]{:S(2)}) collective-permute-start(f32[8,2304]{1,0:T(8,128)S(1)} %get-tuple-element.23), channel_id=1, source_target_pairs={{0,16},{1,17},{2,18},{3,19},{4,20},{5,21},{6,22},{7,23},{8,24},{9,... | collective-permute-start | bytes 221192 | tf_op jit(solution)/shard_map/ppermute | solution.py:36

commit v2 on v0

v2 whole, which is shorter than its diff:
```python
import jax
import jax.numpy as jnp
from jax import lax
from jax.experimental import pallas as pl
from jax.experimental.pallas import tpu as pltpu
from jax.sharding import Mesh
from jax.sharding import PartitionSpec as P

soft_cap = 30.0
norm_eps = 1e-06
f32 = jnp.float32
bf16 = jnp.bfloat16
every = ("x", "c", "y", "z")
chips = ("x", "y", "z")
n_chips = 64
tokens = 512
width = 4608
half = width // 2
tile = 768
tiles = half // tile
wide = tile + 128

plane = 16
block = tokens // 4
chunk = 32
chunks = tokens // chunk
groups = ((0, 3), (1, 2))


def index(x, c, y, z):
    return ((x % 4 * 2 + c % 2) * 4 + y % 4) * 4 + z % 4


places = [(x, c, y, z) for x in range(4) for c in range(2) for y in range(4) for z in range(4)]
swap_cores = [(index(x, c, y, z), index(x, c + 1, y, z)) for x, c, y, z in places]
planes = [[index(x, 0, y, z) for y in range(4) for z in range(4)] for x in range(4)]
planes += [[index(x, 1, y, z) for x in range(4) for z in range(4)] for y in range(4)]


def other_core(array):
    return lax.ppermute(array, every, swap_cores)


def along_line(array, step):
    pairs = [
        (index(x, c, y, z), index(x + step * (1 - c), c, y + step * c, z)) for x, c, y, z in places
    ]
    return lax.ppermute(array, every, pairs)


def over_plane(array):
    return lax.all_to_all(array, every, 0, 0, axis_index_groups=planes, tiled=True)


def lane_rows(part):
    rows = [part[:, 128 * j : 128 * (j + 1)] for j in range(tile // 128)]
    return jnp.concatenate(rows + [jnp.zeros((8 - len(rows), 128), f32)], axis=0)


def assemble(table, blocks, out):
    for d in range(4):
        for k in range(4):
            row = pl.multiple_of(table(4 * d + k) * chunk, chunk)
            out[pl.ds(row, chunk), :] = blocks[d][chunk * k : chunk * (k + 1), :]


def params(room):
    return dict(
        compiler_params=pltpu.CompilerParams(vmem_limit_bytes=room << 20),
        cost_estimate=pl.CostEstimate(flops=1000, bytes_accessed=1000, transcendentals=0),
    )


def norm_kernel(core, mine, theirs, gain, spread, unit_out, root_out):
    first = core[0] == 0
    own = mine[...].astype(f32)
    far = theirs[...].astype(f32)
    rows = jnp.concatenate([jnp.where(first, own, far), jnp.where(first, far, own)], axis=0)
    root = jnp.sqrt(jnp.mean(rows * rows, axis=1, keepdims=True) + norm_eps)
    unit = rows / root
    normed = unit * gain[...]
    part = jnp.where(first, normed[:, :half], normed[:, half:]).astype(bf16)
    spread[...] = jnp.broadcast_to(part[None], spread.shape)
    unit_out[...] = jnp.where(first, unit[:4], unit[4:])
    root_out[...] = jnp.broadcast_to(jnp.where(first, root[:4], root[4:]), root_out.shape)


def half_of(weight, which):
    return weight[:, pl.ds(pl.multiple_of(which * half, half), half)]


def near_logits_kernel(core, b0, b1, weight, out, rows):
    rows[:block, :] = b0[...]
    rows[block:, :] = b1[...]
    out[...] = lax.dot_general(
        rows[...], half_of(weight, core[0]), (((1,), (1,)), ((), ())), preferred_element_type=f32
    )


def logits_kernel(core, b0, b1, b2, b3, weight, part0, part1, picks, out, stats, rows):
    assemble(lambda i: core[1 + chunks + i], (b0, b1, b2, b3), rows)
    out[...] = lax.dot_general(
        rows[...], half_of(weight, 1 - core[0]), (((1,), (1,)), ((), ())), preferred_element_type=f32
    )
    for g, part in enumerate((part0, part1)):
        for d in range(2):
            for k in range(4):
                row = pl.multiple_of(core[1 + 4 * groups[g][d] + k] * chunk, chunk)
                at = chunk * (4 * d + k)
                out[pl.ds(row, chunk), :] += part[at : at + chunk, :]
    for j in range(4):
        lines = slice(128 * j, 128 * (j + 1))
        capped = soft_cap * jnp.tanh(out[lines, :] / soft_cap)
        out[lines, :] = capped
        column = lax.broadcasted_iota(jnp.int32, capped.shape, 1)
        total = jnp.sum(jnp.exp(capped), axis=1, keepdims=True)
        picked = jnp.sum(jnp.where(column == picks[lines, :], capped, 0.0), axis=1, keepdims=True)
        stats[j : j + 1, :] = jnp.broadcast_to(total, (128, 128)).T[0:1, :]
        stats[4 + j : 5 + j, :] = jnp.broadcast_to(picked, (128, 128)).T[0:1, :]


def far_grad_kernel(core, capped, totals, picks, weight, out, dlogit):
    total = jnp.sum(totals[...], axis=0)
    for j in range(4):
        lines = slice(128 * j, 128 * (j + 1))
        column = jnp.broadcast_to(total[j : j + 1, :], (128, 128)).T[:, 0:1]
        value = capped[lines, :]
        onehot = (lax.broadcasted_iota(jnp.int32, value.shape, 1) == picks[lines, :]).astype(f32)
        slope = 1.0 - (value / soft_cap) ** 2
        dlogit[lines, :] = ((jnp.exp(value) / column - onehot) * slope).astype(bf16)
    out[...] = jnp.dot(
        dlogit[...], half_of(weight, 1 - core[0]), preferred_element_type=f32
    ).astype(bf16)


def near_grad_kernel(core, dlogit, weight, out):
    out[...] = jnp.dot(dlogit[...], half_of(weight, core[0]), preferred_element_type=f32)


def combine_kernel(core, grad, received, n0, n1, n2, n3, gain, o0, o1, o2, o3):
    for j in range(tiles):
        lanes = slice(tile * j, tile * (j + 1))
        part = jnp.zeros((8, tile), f32)
        for d, (out, normed) in enumerate(((o0, n0), (o1, n1), (o2, n2), (o3, n3))):
            for k in range(4):
                at = pl.ds(pl.multiple_of(core[1 + 4 * d + k] * chunk, chunk), chunk)
                rows = slice(chunk * k, chunk * (k + 1))
                value = grad[at, lanes] + received[at, lanes].astype(f32)
                out[rows, wide * j : wide * j + tile] = value.astype(bf16)
                value = value * normed[rows, lanes].astype(f32)
                part += jnp.sum(value.reshape(4, 8, tile), axis=0)
        spread = gain[:, pl.ds(pl.multiple_of(core[0] * half + tile * j, tile), tile)]
        sent = lane_rows(jnp.sum(part, axis=0, keepdims=True) / spread)
        sent = jnp.broadcast_to(sent[None], (plane, 8, 128)).reshape(block, 128).astype(bf16)
        for out in (o0, o1, o2, o3):
            out[:, wide * j + tile : wide * (j + 1)] = sent


def head_kernel(core, dlogit, n0, n1, n2, n3, m0, m1, m2, m3, out, turned, own, other):
    step = pl.program_id(0)

    @pl.when(step == 0)
    def _():
        turned[...] = dlogit[...].astype(f32).T.astype(bf16)
        for first, blocks, rows in ((1, (n0, n1, n2, n3), own), (1 + chunks, (m0, m1, m2, m3), other)):
            for d in range(4):
                for k in range(4):
                    row = pl.multiple_of(core[first + 4 * d + k] * chunk, chunk)
                    for j in range(tiles):
                        part = blocks[d][chunk * k : chunk * (k + 1), tile * j : tile * (j + 1)]
                        rows[j, pl.ds(row, chunk), :] = part

    near = step // tiles == core[0]

    @pl.when(near)
    def _():
        out[...] = jnp.dot(turned[...], own[step % tiles], preferred_element_type=f32).astype(bf16)

    @pl.when(jnp.logical_not(near))
    def _():
        out[...] = jnp.dot(turned[...], other[step % tiles], preferred_element_type=f32).astype(bf16)


def add_kernel(core, b0, b1, b2, b3, out):
    total = b0[...].astype(f32) + b1[...].astype(f32) + (b2[...].astype(f32) + b3[...].astype(f32))
    out[...] = total.astype(bf16)


def sum_kernel(core, blocks, keep, send):
    total = jnp.sum(blocks[...].astype(f32), axis=0)
    first = core[0] == 0
    keep[...] = jnp.zeros_like(keep)
    send[...] = jnp.zeros_like(send)
    for j in range(tiles):
        lanes = slice(tile * j, tile * (j + 1))
        grad = total[:, wide * j : wide * j + tile]
        keep[0:4, lanes] = jnp.where(first, grad[:4], grad[4:])
        send[0:4, lanes] = jnp.where(first, grad[4:], grad[:4])
        for k in range(tile // 128):
            row = total[k : k + 1, wide * j + tile : wide * (j + 1)]
            lane = slice(tile * j + 128 * k, tile * j + 128 * (k + 1))
            keep[4:5, lane] = row
            send[4:5, lane] = row


def final_kernel(core, keep, received, unit, root, gain, grad_out, gain_out):
    first = core[0] == 0
    near, far = keep[...], received[...]
    both = jnp.concatenate([jnp.where(first, near, far), jnp.where(first, far, near)], axis=1)
    gain_out[...] = both[4:5]
    grad_unit = both[0:4] * gain[...]
    rows = unit[...]
    inner = jnp.mean(grad_unit * rows, axis=1, keepdims=True)
    grad_out[...] = (grad_unit - rows * inner) / root[:, 0:1]


def call(kernel, core, args, out_shape, scratch=(), grid=(1,), out_specs=None, room=24):
    here = pl.BlockSpec(memory_space=pltpu.VMEM)
    return pl.pallas_call(
        kernel,
        grid_spec=pltpu.PrefetchScalarGridSpec(
            num_scalar_prefetch=1,
            grid=grid,
            in_specs=[here] * len(args),
            out_specs=out_specs or jax.tree.map(lambda _: here, out_shape),
            scratch_shapes=scratch,
        ),
        out_shape=out_shape,
        **params(room),
    )(core, *args)


def shape(dims, dtype):
    return jax.ShapeDtypeStruct(dims, dtype)


def body(hidden, norm_gain, head_weight, targets):
    vocab = head_weight.shape[0]
    place = [lax.axis_index(name) for name in every]
    device = ((place[0] * 2 + place[1]) * 4 + place[2]) * 4 + place[3]
    steps = jnp.arange(4, dtype=jnp.int32)
    by_x = ((place[0] + steps) % 4 * 4)[:, None] + steps[None, :]
    by_y = steps[None, :] * 4 + ((place[2] + steps) % 4)[:, None]
    first = place[1] == 0
    core = jnp.concatenate(
        [
            place[1][None],
            jnp.where(first, by_x, by_y).reshape(chunks),
            jnp.where(first, by_y, by_x).reshape(chunks),
        ]
    )
    gain = norm_gain[None, :]

    spread, unit, root = call(
        norm_kernel,
        core,
        (hidden, other_core(hidden), gain),
        [shape((plane, 8, half), bf16), shape((4, width), f32), shape((4, 128), f32)],
    )
    near = over_plane(spread).reshape(block, half)
    near = [near, *(along_line(near, -d) for d in (1, 2, 3))]
    local, late = lax.optimization_barrier((near[0], targets))
    picks = late.reshape(4, 2, 16, 4).transpose(0, 2, 1, 3).reshape(tokens, 1) - device * vocab
    local, picks = lax.optimization_barrier((local, picks))

    parts = []
    far = [None] * 4
    for group in groups:
        for d in group:
            far[d] = other_core(near[d])
        part = call(
            near_logits_kernel,
            core,
            (local if group[0] == 0 else near[group[0]], near[group[1]], head_weight),
            shape((2 * block, vocab), f32),
            [pltpu.VMEM((2 * block, half), bf16)],
        )
        parts.append(part)
        if group[0] == 0:
            parts[0], near[1], near[2] = lax.optimization_barrier((part, near[1], near[2]))
    capped, stats = call(
        logits_kernel,
        core,
        (*far, head_weight, *parts, picks),
        [shape((tokens, vocab), f32), shape((8, 128), f32)],
        [pltpu.VMEM((tokens, half), bf16)],
    )
    stats = stats + other_core(stats)
    stats = jnp.broadcast_to(stats[None], (n_chips, 8, 128))
    stats = lax.all_to_all(stats, chips, 0, 0, tiled=True)

    far_grad, dlogit = call(
        far_grad_kernel,
        core,
        (capped, stats, picks, head_weight),
        [shape((tokens, half), bf16), shape((tokens, vocab), bf16)],
    )
    received = other_core(far_grad)
    near_grad = call(near_grad_kernel, core, (dlogit, head_weight), shape((tokens, half), f32))
    sums = call(
        combine_kernel,
        core,
        (near_grad, received, *near, gain),
        [shape((block, tiles * wide), bf16)] * 4,
    )
    arrived = [along_line(sums[d], d) for d in (1, 2, 3)]
    dlogit, local = lax.optimization_barrier((dlogit, sums[0]))
    grad_head = call(
        head_kernel,
        core,
        (dlogit, *near, *far),
        shape((vocab, width), bf16),
        [
            pltpu.VMEM((vocab, tokens), bf16),
            pltpu.VMEM((tiles, tokens, tile), bf16),
            pltpu.VMEM((tiles, tokens, tile), bf16),
        ],
        grid=(2 * tiles,),
        out_specs=pl.BlockSpec((vocab, tile), lambda j, c: (0, j)),
    )
    grad_head, local = lax.optimization_barrier((grad_head, local))
    packed = call(add_kernel, core, (local, *arrived), shape((block, tiles * wide), bf16))
    packed = over_plane(packed.reshape(plane, 8, tiles * wide))

    stats = jnp.sum(stats, axis=0)
    loss = (jnp.log(stats[:4]) - stats[4:]).reshape(n_chips, 2, 4)
    chip = (place[0] * 4 + place[2]) * 4 + place[3]
    token_loss = lax.dynamic_slice(loss, (chip, place[1], 0), (1, 1, 4)).reshape(4)
    keep, send = call(sum_kernel, core, (packed,), [shape((8, half), f32)] * 2)
    grad_hidden, grad_gain = call(
        final_kernel,
        core,
        (keep, other_core(send), unit, root, gain),
        [shape((4, width), f32), shape((1, width), f32)],
    )
    return (token_loss, grad_gain.reshape(width), grad_hidden, grad_head)


def solution(mesh):
    fine = Mesh(mesh.devices.reshape(4, 2, 4, 4), every)
    rows = P(every, None)
    return jax.shard_map(
        body,
        mesh=fine,
        in_specs=(rows, P(), rows, P()),
        out_specs=(P(every), P(), rows, rows),
        check_vma=False,
    )
```

time: 364 us -> 129 us (0.35)
  waiting for transfers between devices: 223 us -> 24.3 us
  matrix products: 36.5 us -> 0 us
  Pallas kernels: 0 us -> 33.1 us
  blocking collectives: 62.5 us -> 36.1 us
  starting transfers between devices: 0.08 us -> 21.3 us
  other arithmetic: 16.6 us -> 1.59 us
  between operations: 14.1 us -> 0.81 us
    psum x1 -> x0, waiting for transfers between devices: 148 us -> none  [body(): grad_normed = lax.psum(local_grad, ('section', 'tensor'))]
    all_gather x1 -> x0, waiting for transfers between devices: 73.9 us -> none  [body(): gathered = lax.all_gather(hidden, ('section', 'tensor'), axis=0, tiled=True)]
    psum x1 -> x0, blocking collectives: 62.5 us -> none  [body(): lax.psum((local_total, local_picked), ('section', 'tensor'))]
    dot_general x3 -> x0, matrix products: 36.5 us -> none  [the longest x1 13.7 us: body(): lax.dot_general(normed, head_weight, (((1,), (1,)), ((), ())), preferred_...]
    all_to_all x0 -> x2, blocking collectives: none -> 36.1 us  [the longest x1 18.1 us: body(): stats = lax.all_to_all(stats, chips, 0, 0, tiled=True)]
    pallas_call x0 -> x11, Pallas kernels: none -> 33.1 us  [call(): pl.pallas_call(kernel, grid_spec=pltpu.PrefetchScalarGridSpec(num_scalar_...]
    ppermute x0 -> x14, starting transfers between devices: none -> 17.7 us  [the longest x8 10.1 us: other_core(): return lax.ppermute(array, every, swap_cores)]
    reduce_sum x2 -> x1, other arithmetic: 13.8 us -> 0.07 us  [body(): stats = jnp.sum(stats, axis=0)]
  transfers between devices with their start and end apart: 2 -> 15, of which waited for: 2 -> 8; matrix products, arithmetic and copies ran while one was open for 3% -> 3% of each run, Pallas kernels for 0% -> 13%
where the time goes in v2:
time: 129 us; the launch traced here: 128 us
  blocking collectives  36.1 us (28%)
  Pallas kernels  33.1 us (26%)
  waiting for transfers between devices  24.3 us (19%)
  starting transfers between devices  21.3 us (17%)
  local copies, waits for them, and re-layouts  10.7 us (8%)
  other arithmetic  1.59 us (1%)
    pallas_call x11, Pallas kernels, call(): pl.pallas_call(kernel, grid_spec=pltpu.PrefetchScalarGridSpec(num_scalar_...  33.1 us
    all_to_all x1, blocking collectives, body(): stats = lax.all_to_all(stats, chips, 0, 0, tiled=True)  18.1 us
    all_to_all x1, blocking collectives, over_plane(): lax.all_to_all(array, every, 0, 0, axis_index_groups=planes, tiled=True)  18 us
    ppermute x6, waiting for transfers between devices, along_line(): return lax.ppermute(array, every, pairs)  11 us
    all_to_all x1, waiting for transfers between devices, over_plane(): lax.all_to_all(array, every, 0, 0, axis_index_groups=planes, tiled=True)  10.7 us
    ppermute x8, starting transfers between devices, other_core(): return lax.ppermute(array, every, swap_cores)  10.1 us
    unnamed x8, local copies, waits for them, and re-layouts  8 us
    ppermute x6, starting transfers between devices, along_line(): return lax.ppermute(array, every, pairs)  7.66 us
  transfers between devices with their start and end apart: 15, of which 8 were waited for; matrix products, arithmetic and copies ran while one was open for 3% of the time, Pallas kernels for 13%

profile of v2, /device:TPU:1, one launch (start us, length us, event | category | flops | bytes accessed | tf_op | source)
XLA Modules:
  0.0 128.0 jit_solution(3422430280843480341)
XLA Ops:
  0.6 1.5 %collective-permute-start = (bf16[4,4608]{1,0:T(4,128)(2,1)}, bf16[4,4608]{1,0:T(4,128)(2,1)S(1)}, u32[]{:S(2)}, u32[]{:S(2)}) collective-permute-start(bf16[4,4608]{1,0:T(4,128)(2,1)} %mine.1), channel_id=1, source_target_pairs={{0,16},{1,17},{2,18},{3,19},{4,20},{5,21},{6,22},{7,23},{8,24},{9,... | collective-permute-start | bytes 110600 | tf_op jit(solution)/shard_map/ppermute | solution.py:41
  2.1 0.1 add_select_fusion.1
  2.2 0.1 select_n.49
  2.3 0.1 select_n.51
  2.4 0.1 pad_add_fusion.core
  2.5 0.7 broadcast_in_dim.7.gain
  3.2 0.0 collective-permute-done.theirs
  3.2 0.0 copy-start.3
  3.2 0.8 copy-done.3
  4.0 0.7 shard_map.75
  4.7 18.0 %all_to_all.15 = bf16[16,8,2304]{2,1,0:T(8,128)(2,1)S(1)} all-to-all(bf16[16,8,2304]{2,1,0:T(8,128)(2,1)S(1)} %get-tuple-element.30), channel_id=1, replica_groups={{0,1,2,3,4,5,6,7,8,9,10,11,12,13,14,15},{32,33,34,35,36,37,38,39,40,41,..., dimensions={0} | all-to-all | bytes 1179648 | tf_op jit(solution)/shard_map/all_to_all | solution.py:52
  22.7 1.2 collective-permute-start.2
  24.0 2.4 %collective-permute-start.4 = (bf16[128,2304]{1,0:T(8,128)(2,1)S(1)}, bf16[128,2304]{1,0:T(8,128)(2,1)S(1)}, u32[]{:S(2)}, u32[]{:S(2)}) collective-permute-start(bf16[128,2304]{1,0:T(8,128)(2,1)S(1)} %bitcast.7), channel_id=1, source_target_pairs={{0,64},{1,65},{2,66},{3,67},{4,68},{5,69},{6,70},{7,71},{8,72},{9,... | collective-permute-start | bytes 1769480 | tf_op jit(solution)/shard_map/ppermute | solution.py:48
  26.4 1.1 collective-permute-start.3
  27.6 1.6 %collective-permute-start.1 = (bf16[128,2304]{1,0:T(8,128)(2,1)S(1)}, bf16[128,2304]{1,0:T(8,128)(2,1)}, u32[]{:S(2)}, u32[]{:S(2)}) collective-permute-start(bf16[128,2304]{1,0:T(8,128)(2,1)S(1)} %bitcast.9), channel_id=1, source_target_pairs={{0,16},{1,17},{2,18},{3,19},{4,20},{5,21},{6,22},{7,23},{8,24},{9,... | collective-permute-start | bytes 1769480 | tf_op jit(solution)/shard_map/ppermute | solution.py:41
  29.1 0.7 broadcast_subtract_fusion
  29.8 0.1 sub.28
  30.0 0.1 sub.30
  30.1 2.9 %collective-permute-done.2.b1.n3 = bf16[128,2304]{1,0:T(8,128)(2,1)S(1)} collective-permute-done((bf16[128,2304]{1,0:T(8,128)(2,1)S(1)}, bf16[128,2304]{1,0:T(8,128)(2,1)S(1)}, u32[]{:S(2)}, u32[]{:S(2)}) %collective-permute-start.2) | collective-permute-done | bytes 589856 | tf_op jit(solution)/shard_map/ppermute | solution.py:48
  33.0 0.0 copy-start
  33.0 3.6 %copy-done = bf16[1000,4608]{1,0:T(8,128)(2,1)S(1)} copy-done((bf16[1000,4608]{1,0:T(8,128)(2,1)S(1)}, bf16[1000,4608]{1,0:T(8,128)(2,1)}, u32[]{:S(2)}) %copy-start) | copy-done | bytes 9216024
  36.6 1.9 %shard_map.76.part0 = f32[256,1000]{1,0:T(8,128)S(1)} custom-call(s32[33]{0:T(128)S(1)} %pad_add_fusion.core, bf16[128,2304]{1,0:T(8,128)(2,1)S(1)} %bitcast.10, bf16[128,2304]{1,0:T(8,128)(2,1)S(1)} %collective-permute-done.2.b1.n3, bf16[1000,4608]{1,0:T(8,128)(2,1)S(1)} %copy-done), custom_call_target="tpu_custom_call" | custom-call | flops 1000 | bytes 1000 | tf_op jit(solution)/shard_map/pallas_call | solution.py:219
  38.5 1.8 %collective-permute-done.4.b1.n2 = bf16[128,2304]{1,0:T(8,128)(2,1)S(1)} collective-permute-done((bf16[128,2304]{1,0:T(8,128)(2,1)S(1)}, bf16[128,2304]{1,0:T(8,128)(2,1)S(1)}, u32[]{:S(2)}, u32[]{:S(2)}) %collective-permute-start.4) | collective-permute-done | bytes 589856 | tf_op jit(solution)/shard_map/ppermute | solution.py:48
  40.3 0.0 collective-permute-done.3.b0.n1
  40.3 2.1 %collective-permute-start.5 = (bf16[128,2304]{1,0:T(8,128)(2,1)S(1)}, bf16[128,2304]{1,0:T(8,128)(2,1)}, u32[]{:S(2)}, u32[]{:S(2)}) collective-permute-start(bf16[128,2304]{1,0:T(8,128)(2,1)S(1)} %collective-permute-done.3.b0.n1), channel_id=1, source_target_pairs={{0,16},{1,17},{2,18},{3,19},{4,20},{5,21},{6,22},{7,23},{8,24},{9,... | collective-permute-start | bytes 1769480 | tf_op jit(solution)/shard_map/ppermute | solution.py:41
  42.4 0.0 collective-permute-start.7
  42.4 0.5 collective-permute-start.6
  42.9 0.9 copy.9.picks
  43.8 0.0 copy-start.1
  43.8 3.6 %copy-done.1 = bf16[1000,4608]{1,0:T(8,128)(2,1)S(1)} copy-done((bf16[1000,4608]{1,0:T(8,128)(2,1)S(1)}, bf16[1000,4608]{1,0:T(8,128)(2,1)}, u32[]{:S(2)}) %copy-start.1) | copy-done | bytes 9216024
  47.4 0.0 copy-start.2
  47.4 2.0 %shard_map.77.part1 = f32[256,1000]{1,0:T(8,128)S(1)} custom-call(s32[33]{0:T(128)S(1)} %pad_add_fusion.core, bf16[128,2304]{1,0:T(8,128)(2,1)S(1)} %collective-permute-done.3.b0.n1, bf16[128,2304]{1,0:T(8,128)(2,1)S(1)} %collective-permute-done.4.b1.n2, bf16[1000,4608]{1,0:T(8,128)(2,1)S(1)} %copy-done.1), custom_call_target="tpu_custom_call" | custom-call | flops 1000 | bytes 1000 | tf_op jit(solution)/shard_map/pallas_call | solution.py:219
  49.4 0.0 collective-permute-done.1.b0.m0
  49.4 0.0 collective-permute-done.7.b3.m3
  49.4 0.0 collective-permute-done.5.b1.m1
  49.4 0.0 collective-permute-done.6.b2.m2
  49.4 0.0 copy-done.2
  49.4 6.0 %shard_map.78 = (f32[512,1000]{1,0:T(8,128)S(1)}, f32[8,128]{1,0:T(8,128)S(1)}) custom-call(s32[33]{0:T(128)S(1)} %pad_add_fusion.core, bf16[128,2304]{1,0:T(8,128)(2,1)} %collective-permute-done.1.b0.m0, bf16[128,2304]{1,0:T(8,128)(2,1)} %collective-permute-done.5.b1.m1, bf16[128,2304]{1,0:T(8,128)(2,1)} %collective-permute-done.6.b2.m2, ...), custom_call_target="tpu_custom_call" | custom-call | flops 1000 | bytes 1000 | tf_op jit(solution)/shard_map/pallas_call | solution.py:219
  55.5 0.1 collective-permute-start.8
  55.5 1.2 collective-permute-done.8
  56.7 18.1 %all_to_all.16.totals = f32[64,8,128]{2,1,0:T(8,128)S(1)} all-to-all(f32[64,8,128]{2,1,0:T(8,128)S(1)} %broadcast_in_dim.8), channel_id=1, replica_groups=mesh['x'=4,'c'=2,'y'=4,'z'=4] {'x','y','z'}, dimensions={0} | all-to-all | bytes 524288 | tf_op jit(solution)/shard_map/all_to_all | solution.py:290
  74.8 3.9 %shard_map.79 = (bf16[512,2304]{1,0:T(8,128)(2,1)S(1)}, bf16[512,1000]{1,0:T(8,128)(2,1)S(1)}) custom-call(s32[33]{0:T(128)S(1)} %pad_add_fusion.core, f32[512,1000]{1,0:T(8,128)S(1)} %get-tuple-element.39.capped, f32[64,8,128]{2,1,0:T(8,128)S(1)} %all_to_all.16.totals, s32[512,1]{1,0:T(8,128)S(1)} %copy-done.2, bf16[1000,4608]{1,0:T(8,128)(2,1)S(1)} %copy-done.1), custom_call_target="tpu_custom_call" | custom-call | flops 1000 | bytes 1000 | tf_op jit(solution)/shard_map/pallas_call | solution.py:219
  78.8 2.2 %collective-permute-start.9 = (bf16[512,2304]{1,0:T(8,128)(2,1)S(1)}, bf16[512,2304]{1,0:T(8,128)(2,1)S(1)}, u32[]{:S(2)}, u32[]{:S(2)}) collective-permute-start(bf16[512,2304]{1,0:T(8,128)(2,1)S(1)} %get-tuple-element.41), channel_id=1, source_target_pairs={{0,16},{1,17},{2,18},{3,19},{4,20},{5,21},{6,22},{7,23},{8,24},{9,... | collective-permute-start | bytes 7077896 | tf_op jit(solution)/shard_map/ppermute | solution.py:41
  80.9 3.1 %shard_map.80.grad = f32[512,2304]{1,0:T(8,128)S(1)} custom-call(s32[33]{0:T(128)S(1)} %pad_add_fusion.core, bf16[512,1000]{1,0:T(8,128)(2,1)S(1)} %get-tuple-element.43.dlogit, bf16[1000,4608]{1,0:T(8,128)(2,1)S(1)} %copy-done.1), custom_call_target="tpu_custom_call" | custom-call | flops 1000 | bytes 1000 | tf_op jit(solution)/shard_map/pallas_call | solution.py:219
  84.1 1.0 collective-permute-done.9.received
  85.1 1.5 %shard_map.81 = (bf16[128,2688]{1,0:T(8,128)(2,1)S(1)}, bf16[128,2688]{1,0:T(8,128)(2,1)S(1)}, bf16[128,2688]{1,0:T(8,128)(2,1)S(1)}, bf16[128,2688]{1,0:T(8,128)(2,1)S(1)}) custom-call(s32[33]{0:T(128)S(1)} %pad_add_fusion.core, f32[512,2304]{1,0:T(8,128)S(1)} %shard_map.80.grad, bf16[512,2304]{1,0:T(8,128)(2,1)S(1)} %collective-permute-done.9.received, ...), custom_call_target="tpu_custom_call" | custom-call | flops 1000 | bytes 1000 | tf_op jit(solution)/shard_map/pallas_call | solution.py:219
  86.6 0.3 collective-permute-start.10
  87.0 1.4 %collective-permute-start.11 = (bf16[128,2688]{1,0:T(8,128)(2,1)S(1)}, bf16[128,2688]{1,0:T(8,128)(2,1)S(1)}, u32[]{:S(2)}, u32[]{:S(2)}) collective-permute-start(bf16[128,2688]{1,0:T(8,128)(2,1)S(1)} %get-tuple-element.47), channel_id=1, source_target_pairs={{0,64},{1,65},{2,66},{3,67},{4,68},{5,69},{6,70},{7,71},{8,72},{9,... | collective-permute-start | bytes 2064392 | tf_op jit(solution)/shard_map/ppermute | solution.py:48
  88.4 1.0 collective-permute-start.12
  89.4 10.1 %shard_map.82 = bf16[1000,4608]{1,0:T(8,128)(2,1)} custom-call(s32[33]{0:T(128)S(1)} %pad_add_fusion.core, bf16[512,1000]{1,0:T(8,128)(2,1)S(1)} %get-tuple-element.43.dlogit, bf16[128,2304]{1,0:T(8,128)(2,1)S(1)} %bitcast.12, bf16[128,2304]{1,0:T(8,128)(2,1)S(1)} %collective-permute-done.3.b0.n1, bf16[128,2304]{1,0:T(8,128)(2,1)S(1)} %collective-permute-done.4.b1.n2, ...), custom_call_target="tpu_custom_call" | custom-call | flops 1000 | bytes 1000 | tf_op jit(solution)/shard_map/pallas_call | solution.py:219
  99.6 5.8 %collective-permute-done.10.b1 = bf16[128,2688]{1,0:T(8,128)(2,1)S(1)} collective-permute-done((bf16[128,2688]{1,0:T(8,128)(2,1)S(1)}, bf16[128,2688]{1,0:T(8,128)(2,1)S(1)}, u32[]{:S(2)}, u32[]{:S(2)}) %collective-permute-start.10) | collective-permute-done | bytes 688160 | tf_op jit(solution)/shard_map/ppermute | solution.py:48
  105.3 0.0 collective-permute-done.11.b2
  105.4 0.6 collective-permute-done.12.b3
  106.0 1.7 %shard_map.83 = bf16[128,2688]{1,0:T(8,128)(2,1)} custom-call(s32[33]{0:T(128)S(1)} %pad_add_fusion.core, bf16[128,2688]{1,0:T(8,128)(2,1)S(1)} %get-tuple-element.45.b0, bf16[128,2688]{1,0:T(8,128)(2,1)S(1)} %collective-permute-done.10.b1, bf16[128,2688]{1,0:T(8,128)(2,1)S(1)} %collective-permute-done.11.b2, bf16[128,2688]{1,0:T(8,128)(2,1)S(1)} %collective-permute-done.12.b3), custom_call_target="tpu_custom_call" | custom-call | flops 1000 | bytes 1000 | tf_op jit(solution)/shard_map/pallas_call | solution.py:219
  107.7 3.6 %all-to-all-start.2 = ((bf16[16,8,2688]{2,1,0:T(8,128)(2,1)}), bf16[16,8,2688]{2,1,0:T(8,128)(2,1)S(1)}, u32[]{:S(2)}, u32[]{:S(2)}) async-start(bf16[16,8,2688]{2,1,0:T(8,128)(2,1)} %bitcast.4), calls=%async_computation.2 | async-start | bytes 1376256 | tf_op jit(solution)/shard_map/all_to_all | solution.py:52
  111.3 0.1 reduce_sum.9
  111.4 0.2 reshape.95
  111.6 10.7 %all-to-all-done.2.blocks = bf16[16,8,2688]{2,1,0:T(8,128)(2,1)S(1)} async-done(((bf16[16,8,2688]{2,1,0:T(8,128)(2,1)}), bf16[16,8,2688]{2,1,0:T(8,128)(2,1)S(1)}, u32[]{:S(2)}, u32[]{:S(2)}) %all-to-all-start.2) | async-done | bytes 688160 | tf_op jit(solution)/shard_map/all_to_all | solution.py:52
  122.3 0.6 shard_map.84
  122.9 2.2 %collective-permute-start.13 = (f32[8,2304]{1,0:T(8,128)S(1)}, f32[8,2304]{1,0:T(8,128)S(1)}, u32[]{:S(2)}, u32[]{:S(2)}) collective-permute-start(f32[8,2304]{1,0:T(8,128)S(1)} %get-tuple-element.50), channel_id=1, source_target_pairs={{0,16},{1,17},{2,18},{3,19},{4,20},{5,21},{6,22},{7,23},{8,24},{9,... | collective-permute-start | bytes 221192 | tf_op jit(solution)/shard_map/ppermute | solution.py:41
  125.1 0.5 dynamic-slice_bitcast_fusion
  125.6 0.4 collective-permute-done.13.received
  126.0 1.3 %shard_map.85 = (f32[4,4608]{1,0:T(4,128)}, f32[1,4608]{1,0:T(1,128)S(1)}) custom-call(s32[33]{0:T(128)S(1)} %pad_add_fusion.core, f32[8,2304]{1,0:T(8,128)S(1)} %get-tuple-element.49.keep, f32[8,2304]{1,0:T(8,128)S(1)} %collective-permute-done.13.received, f32[4,4608]{1,0:T(4,128)S(1)} %get-tuple-element.51.unit, f32[4,128]{1,0:T(4,128)S(1)} %get-tuple-element.52.root, ...), custom_call_target="tpu_custom_call" | custom-call | flops 1000 | bytes 1000 | tf_op jit(solution)/shard_map/pallas_call | solution.py:219
  127.3 0.7 reduce
  (6 shorter events, 0.1 us)
Async XLA Ops:
  0.6 2.6 %collective-permute-start = (bf16[4,4608]{1,0:T(4,128)(2,1)}, bf16[4,4608]{1,0:T(4,128)(2,1)S(1)}, u32[]{:S(2)}, u32[]{:S(2)}) collective-permute-start(bf16[4,4608]{1,0:T(4,128)(2,1)} %mine.1), channel_id=1, source_target_pairs={{0,16},{1,17},{2,18},{3,19},{4,20},{5,21},{6,22},{7,23},{8,24},{9,... | collective-permute-start | bytes 110600 | tf_op jit(solution)/shard_map/ppermute | solution.py:41
  3.2 0.8 copy-start.3
  22.7 10.2 %collective-permute-start.2 = (bf16[128,2304]{1,0:T(8,128)(2,1)S(1)}, bf16[128,2304]{1,0:T(8,128)(2,1)S(1)}, u32[]{:S(2)}, u32[]{:S(2)}) collective-permute-start(bf16[128,2304]{1,0:T(8,128)(2,1)S(1)} %bitcast.6), channel_id=1, source_target_pairs={{0,32},{1,33},{2,34},{3,35},{4,36},{5,37},{6,38},{7,39},{8,40},{9,... | collective-permute-start | bytes 1769480 | tf_op jit(solution)/shard_map/ppermute | solution.py:48
  24.0 16.3 %collective-permute-start.4 = (bf16[128,2304]{1,0:T(8,128)(2,1)S(1)}, bf16[128,2304]{1,0:T(8,128)(2,1)S(1)}, u32[]{:S(2)}, u32[]{:S(2)}) collective-permute-start(bf16[128,2304]{1,0:T(8,128)(2,1)S(1)} %bitcast.7), channel_id=1, source_target_pairs={{0,64},{1,65},{2,66},{3,67},{4,68},{5,69},{6,70},{7,71},{8,72},{9,... | collective-permute-start | bytes 1769480 | tf_op jit(solution)/shard_map/ppermute | solution.py:48
  26.4 13.9 %collective-permute-start.3 = (bf16[128,2304]{1,0:T(8,128)(2,1)S(1)}, bf16[128,2304]{1,0:T(8,128)(2,1)S(1)}, u32[]{:S(2)}, u32[]{:S(2)}) collective-permute-start(bf16[128,2304]{1,0:T(8,128)(2,1)S(1)} %bitcast.8), channel_id=1, source_target_pairs={{0,96},{1,97},{2,98},{3,99},{4,100},{5,101},{6,102},{7,103},{8,104... | collective-permute-start | bytes 1769480 | tf_op jit(solution)/shard_map/ppermute | solution.py:48
  27.6 21.8 %collective-permute-start.1 = (bf16[128,2304]{1,0:T(8,128)(2,1)S(1)}, bf16[128,2304]{1,0:T(8,128)(2,1)}, u32[]{:S(2)}, u32[]{:S(2)}) collective-permute-start(bf16[128,2304]{1,0:T(8,128)(2,1)S(1)} %bitcast.9), channel_id=1, source_target_pairs={{0,16},{1,17},{2,18},{3,19},{4,20},{5,21},{6,22},{7,23},{8,24},{9,... | collective-permute-start | bytes 1769480 | tf_op jit(solution)/shard_map/ppermute | solution.py:41
  33.0 3.6 %copy-start = (bf16[1000,4608]{1,0:T(8,128)(2,1)S(1)}, bf16[1000,4608]{1,0:T(8,128)(2,1)}, u32[]{:S(2)}) copy-start(bf16[1000,4608]{1,0:T(8,128)(2,1)} %weight.9) | copy-start | bytes 27648004
  40.3 9.1 %collective-permute-start.5 = (bf16[128,2304]{1,0:T(8,128)(2,1)S(1)}, bf16[128,2304]{1,0:T(8,128)(2,1)}, u32[]{:S(2)}, u32[]{:S(2)}) collective-permute-start(bf16[128,2304]{1,0:T(8,128)(2,1)S(1)} %collective-permute-done.3.b0.n1), channel_id=1, source_target_pairs={{0,16},{1,17},{2,18},{3,19},{4,20},{5,21},{6,22},{7,23},{8,24},{9,... | collective-permute-start | bytes 1769480 | tf_op jit(solution)/shard_map/ppermute | solution.py:41
  42.4 7.0 %collective-permute-start.7 = (bf16[128,2304]{1,0:T(8,128)(2,1)S(1)}, bf16[128,2304]{1,0:T(8,128)(2,1)}, u32[]{:S(2)}, u32[]{:S(2)}) collective-permute-start(bf16[128,2304]{1,0:T(8,128)(2,1)S(1)} %collective-permute-done.2.b1.n3), channel_id=1, source_target_pairs={{0,16},{1,17},{2,18},{3,19},{4,20},{5,21},{6,22},{7,23},{8,24},{9,... | collective-permute-start | bytes 1769480 | tf_op jit(solution)/shard_map/ppermute | solution.py:41
  42.4 7.0 %collective-permute-start.6 = (bf16[128,2304]{1,0:T(8,128)(2,1)S(1)}, bf16[128,2304]{1,0:T(8,128)(2,1)}, u32[]{:S(2)}, u32[]{:S(2)}) collective-permute-start(bf16[128,2304]{1,0:T(8,128)(2,1)S(1)} %collective-permute-done.4.b1.n2), channel_id=1, source_target_pairs={{0,16},{1,17},{2,18},{3,19},{4,20},{5,21},{6,22},{7,23},{8,24},{9,... | collective-permute-start | bytes 1769480 | tf_op jit(solution)/shard_map/ppermute | solution.py:41
  43.8 3.6 %copy-start.1 = (bf16[1000,4608]{1,0:T(8,128)(2,1)S(1)}, bf16[1000,4608]{1,0:T(8,128)(2,1)}, u32[]{:S(2)}) copy-start(bf16[1000,4608]{1,0:T(8,128)(2,1)} %weight.9) | copy-start | bytes 27648004
  47.4 2.0 %copy-start.2 = (s32[512,1]{1,0:T(8,128)S(1)}, s32[512,1]{1,0:T(8,128)}, u32[]{:S(2)}) copy-start(s32[512,1]{1,0:T(8,128)} %copy.9.picks) | copy-start | bytes 6148
  55.5 1.2 collective-permute-start.8
  78.8 6.3 %collective-permute-start.9 = (bf16[512,2304]{1,0:T(8,128)(2,1)S(1)}, bf16[512,2304]{1,0:T(8,128)(2,1)S(1)}, u32[]{:S(2)}, u32[]{:S(2)}) collective-permute-start(bf16[512,2304]{1,0:T(8,128)(2,1)S(1)} %get-tuple-element.41), channel_id=1, source_target_pairs={{0,16},{1,17},{2,18},{3,19},{4,20},{5,21},{6,22},{7,23},{8,24},{9,... | collective-permute-start | bytes 7077896 | tf_op jit(solution)/shard_map/ppermute | solution.py:41
  86.6 18.7 %collective-permute-start.10 = (bf16[128,2688]{1,0:T(8,128)(2,1)S(1)}, bf16[128,2688]{1,0:T(8,128)(2,1)S(1)}, u32[]{:S(2)}, u32[]{:S(2)}) collective-permute-start(bf16[128,2688]{1,0:T(8,128)(2,1)S(1)} %get-tuple-element.46), channel_id=1, source_target_pairs={{0,32},{1,33},{2,34},{3,35},{4,36},{5,37},{6,38},{7,39},{8,40},{9,... | collective-permute-start | bytes 2064392 | tf_op jit(solution)/shard_map/ppermute | solution.py:48
  87.0 18.4 %collective-permute-start.11 = (bf16[128,2688]{1,0:T(8,128)(2,1)S(1)}, bf16[128,2688]{1,0:T(8,128)(2,1)S(1)}, u32[]{:S(2)}, u32[]{:S(2)}) collective-permute-start(bf16[128,2688]{1,0:T(8,128)(2,1)S(1)} %get-tuple-element.47), channel_id=1, source_target_pairs={{0,64},{1,65},{2,66},{3,67},{4,68},{5,69},{6,70},{7,71},{8,72},{9,... | collective-permute-start | bytes 2064392 | tf_op jit(solution)/shard_map/ppermute | solution.py:48
  88.4 17.6 %collective-permute-start.12 = (bf16[128,2688]{1,0:T(8,128)(2,1)S(1)}, bf16[128,2688]{1,0:T(8,128)(2,1)S(1)}, u32[]{:S(2)}, u32[]{:S(2)}) collective-permute-start(bf16[128,2688]{1,0:T(8,128)(2,1)S(1)} %get-tuple-element.48), channel_id=1, source_target_pairs={{0,96},{1,97},{2,98},{3,99},{4,100},{5,101},{6,102},{7,103},{8,104... | collective-permute-start | bytes 2064392 | tf_op jit(solution)/shard_map/ppermute | solution.py:48
  107.7 14.5 %all-to-all-start.2 = ((bf16[16,8,2688]{2,1,0:T(8,128)(2,1)}), bf16[16,8,2688]{2,1,0:T(8,128)(2,1)S(1)}, u32[]{:S(2)}, u32[]{:S(2)}) async-start(bf16[16,8,2688]{2,1,0:T(8,128)(2,1)} %bitcast.4), calls=%async_computation.2 | async-start | bytes 1376256 | tf_op jit(solution)/shard_map/all_to_all | solution.py:52
  122.9 3.1 %collective-permute-start.13 = (f32[8,2304]{1,0:T(8,128)S(1)}, f32[8,2304]{1,0:T(8,128)S(1)}, u32[]{:S(2)}, u32[]{:S(2)}) collective-permute-start(f32[8,2304]{1,0:T(8,128)S(1)} %get-tuple-element.50), channel_id=1, source_target_pairs={{0,16},{1,17},{2,18},{3,19},{4,20},{5,21},{6,22},{7,23},{8,24},{9,... | collective-permute-start | bytes 221192 | tf_op jit(solution)/shard_map/ppermute | solution.py:41

commit v3 on v2

v3 whole, which is shorter than its diff:
```python
import jax
import jax.numpy as jnp
from jax import lax
from jax.experimental import pallas as pl
from jax.experimental.pallas import tpu as pltpu
from jax.sharding import Mesh
from jax.sharding import PartitionSpec as P

soft_cap = 30.0
norm_eps = 1e-06
f32 = jnp.float32
bf16 = jnp.bfloat16
every = ("x", "c", "y", "z")
chips = ("x", "y", "z")
n_chips = 64
tokens = 512
width = 4608
half = width // 2
tile = 768
tiles = half // tile
wide = tile + 128

plane = 16
block = tokens // 4
chunk = 32
chunks = tokens // chunk


def index(x, c, y, z):
    return ((x % 4 * 2 + c % 2) * 4 + y % 4) * 4 + z % 4


places = [(x, c, y, z) for x in range(4) for c in range(2) for y in range(4) for z in range(4)]
swap_cores = [(index(x, c, y, z), index(x, c + 1, y, z)) for x, c, y, z in places]
planes = [[index(x, 0, y, z) for y in range(4) for z in range(4)] for x in range(4)]
planes += [[index(x, 1, y, z) for x in range(4) for z in range(4)] for y in range(4)]


def other_core(array):
    return lax.ppermute(array, every, swap_cores)


def along_line(array, step):
    pairs = [
        (index(x, c, y, z), index(x + step * (1 - c), c, y + step * c, z)) for x, c, y, z in places
    ]
    return lax.ppermute(array, every, pairs)


def over_plane(array):
    return lax.all_to_all(array, every, 0, 0, axis_index_groups=planes, tiled=True)


def lane_rows(part):
    rows = [part[:, 128 * j : 128 * (j + 1)] for j in range(tile // 128)]
    return jnp.concatenate(rows + [jnp.zeros((8 - len(rows), 128), f32)], axis=0)


def assemble(table, blocks, out):
    for d in range(4):
        for k in range(4):
            row = pl.multiple_of(table(4 * d + k) * chunk, chunk)
            out[pl.ds(row, chunk), :] = blocks[d][chunk * k : chunk * (k + 1), :]


def params(room):
    return dict(
        compiler_params=pltpu.CompilerParams(vmem_limit_bytes=room << 20),
        cost_estimate=pl.CostEstimate(flops=1000, bytes_accessed=1000, transcendentals=0),
    )


def norm_kernel(core, mine, theirs, gain, spread, unit_out, root_out, row):
    first = core[0] == 0
    own = mine[...].astype(f32)
    far = theirs[...].astype(f32)
    rows = jnp.concatenate([jnp.where(first, own, far), jnp.where(first, far, own)], axis=0)
    root = jnp.sqrt(jnp.mean(rows * rows, axis=1, keepdims=True) + norm_eps)
    unit = rows / root
    normed = unit * gain[...].reshape(1, width)
    part = jnp.where(first, normed[:, :half], normed[:, half:]).astype(bf16)
    row[...] = gain[...].reshape(1, width)
    spread[...] = jnp.broadcast_to(part[None], spread.shape)
    unit_out[...] = jnp.where(first, unit[:4], unit[4:])
    root_out[...] = jnp.broadcast_to(jnp.where(first, root[:4], root[4:]), root_out.shape)


def half_of(weight, which):
    return weight[:, pl.ds(pl.multiple_of(which * half, half), half)]


def turned_column(row):
    return jnp.broadcast_to(row, (128, 128)).T[:, 0:1]


def hits_of(labels, j, dims):
    label = turned_column(labels[j : j + 1, :].astype(f32)).astype(jnp.int32)
    return lax.broadcasted_iota(jnp.int32, dims, 1) == label


def onehot_rows(labels, vocab):
    rows = [hits_of(labels, j, (128, vocab)).astype(f32).astype(bf16) for j in range(4)]
    return jnp.concatenate(rows, axis=0)


def far_target_kernel(core, weight, labels, out):
    onehot = onehot_rows(labels, weight.shape[0])
    out[...] = jnp.dot(
        onehot, half_of(weight, 1 - core[0]), preferred_element_type=f32
    ).astype(bf16)


def near_logits_kernel(core, *refs):
    *blocks, weight, out, rows = refs
    for d, ref in enumerate(blocks):
        rows[block * d : block * (d + 1), :] = ref[...]
    out[...] = lax.dot_general(
        rows[...], half_of(weight, core[0]), (((1,), (1,)), ((), ())), preferred_element_type=f32
    )


def logits_kernel(core, b0, b1, b2, b3, weight, part0, part1, labels, out, stats, others, rows):
    assemble(lambda i: core[1 + chunks + i], (b0, b1, b2, b3), rows)
    out[...] = lax.dot_general(
        rows[...], half_of(weight, 1 - core[0]), (((1,), (1,)), ((), ())), preferred_element_type=f32
    )
    for i in range(chunks):
        row = pl.multiple_of(core[1 + i] * chunk, chunk)
        part = part0[chunk * i : chunk * (i + 1), :] if i < 4 else part1[chunk * (i - 4) : chunk * (i - 3), :]
        out[pl.ds(row, chunk), :] += part
    for j in range(4):
        lines = slice(128 * j, 128 * (j + 1))
        capped = soft_cap * jnp.tanh(out[lines, :] / soft_cap)
        out[lines, :] = capped
        hit = hits_of(labels, j, capped.shape)
        exps = jnp.exp(capped)
        slope = 1.0 - (capped / soft_cap) ** 2
        others[lines, :] = jnp.where(hit, 0.0, exps * slope).astype(bf16)
        total = jnp.sum(exps, axis=1, keepdims=True)
        picked = jnp.sum(jnp.where(hit, capped, 0.0), axis=1, keepdims=True)
        stats[j : j + 1, :] = jnp.broadcast_to(total, (128, 128)).T[0:1, :]
        stats[4 + j : 5 + j, :] = jnp.broadcast_to(picked, (128, 128)).T[0:1, :]


def far_grad_kernel(core, others, weight, out):
    grad = jnp.dot(others[...], half_of(weight, 1 - core[0]), preferred_element_type=f32)
    out[...] = grad.astype(bf16)


def combine_kernel(
    core, capped, stats, labels, weight, received, target, n0, n1, n2, n3, gain,
    o0, o1, o2, o3, loss, totals, dlogit, held, inverse, factor
):
    sums = jnp.sum(stats[...], axis=0)
    total, picked = sums[0:4, :], sums[4:8, :]
    totals[...] = total
    loss[...] = jnp.log(total) - picked
    slack = (jnp.exp(picked) / total - 1.0) * (1.0 - (picked / soft_cap) ** 2)
    scale = 1.0 / total
    for j in range(4):
        lines = slice(128 * j, 128 * (j + 1))
        inverse[lines, :] = turned_column(scale[j : j + 1, :])
        factor[lines, :] = turned_column(slack[j : j + 1, :])
        value = capped[lines, :]
        onehot = hits_of(labels, j, value.shape).astype(f32)
        slope = 1.0 - (value / soft_cap) ** 2
        share = jnp.exp(value) / turned_column(total[j : j + 1, :])
        dlogit[lines, :] = ((share - onehot) * slope).astype(bf16)
    for out in (o0, o1, o2, o3):
        out[:, half:] = jnp.zeros((block, 128), bf16)
    for j in range(tiles):
        lanes = slice(tile * j, tile * (j + 1))
        from_start = pl.ds(pl.multiple_of(core[0] * half + tile * j, tile), tile)
        held[...] = jnp.dot(dlogit[...], weight[:, from_start], preferred_element_type=f32)
        part = jnp.zeros((8, tile), f32)
        for d, (out, normed) in enumerate(((o0, n0), (o1, n1), (o2, n2), (o3, n3))):
            for k in range(4):
                at = pl.ds(pl.multiple_of(core[1 + 4 * d + k] * chunk, chunk), chunk)
                rows = slice(chunk * k, chunk * (k + 1))
                value = held[at, :] + received[at, lanes].astype(f32) * inverse[at, :]
                value += target[at, lanes].astype(f32) * factor[at, :]
                out[rows, lanes] = value.astype(bf16)
                value = value * normed[rows, lanes].astype(f32)
                part += jnp.sum(value.reshape(4, 8, tile), axis=0)
        sent = lane_rows(jnp.sum(part, axis=0, keepdims=True) / gain[:, from_start])
        high = sent.astype(bf16).astype(f32)
        sent = jnp.concatenate([high, sent - high], axis=0).astype(bf16)
        for out in (o0, o1, o2, o3):
            out[16 * j : 16 * (j + 1), half:] = sent


def head_kernel(core, capped, stats, labels, n0, n1, n2, n3, m0, m1, m2, m3, out, turned, own, other):
    step = pl.program_id(0)

    @pl.when(step == 0)
    def _():
        for j in range(4):
            lines = slice(128 * j, 128 * (j + 1))
            value = capped[lines, :].T
            row = lax.broadcasted_iota(jnp.int32, value.shape, 0)
            onehot = (row == labels[j : j + 1, :]).astype(f32)
            slope = 1.0 - (value / soft_cap) ** 2
            dlogit = (jnp.exp(value) / stats[j : j + 1, :] - onehot) * slope
            turned[:, lines] = dlogit.astype(bf16)
        for first, blocks, rows in ((1, (n0, n1, n2, n3), own), (1 + chunks, (m0, m1, m2, m3), other)):
            for d in range(4):
                for k in range(4):
                    row = pl.multiple_of(core[first + 4 * d + k] * chunk, chunk)
                    for j in range(tiles):
                        part = blocks[d][chunk * k : chunk * (k + 1), tile * j : tile * (j + 1)]
                        rows[j, pl.ds(row, chunk), :] = part

    near = step // tiles == core[0]

    @pl.when(near)
    def _():
        out[...] = jnp.dot(turned[...], own[step % tiles], preferred_element_type=f32).astype(bf16)

    @pl.when(jnp.logical_not(near))
    def _():
        out[...] = jnp.dot(turned[...], other[step % tiles], preferred_element_type=f32).astype(bf16)


def add_kernel(core, b0, b1, b2, b3, out):
    total = b0[...].astype(f32) + b1[...].astype(f32) + (b2[...].astype(f32) + b3[...].astype(f32))
    for j in range(tiles):
        out[:, wide * j : wide * j + tile] = total[:, tile * j : tile * (j + 1)].astype(bf16)
        rows = total[16 * j : 16 * j + 8, half:] + total[16 * j + 8 : 16 * j + 16, half:]
        rows = jnp.broadcast_to(rows[None], (plane, 8, 128)).reshape(block, 128)
        out[:, wide * j + tile : wide * (j + 1)] = rows.astype(bf16)


def sum_kernel(core, blocks, keep, send):
    total = jnp.sum(blocks[...].astype(f32), axis=0)
    first = core[0] == 0
    keep[...] = jnp.zeros_like(keep)
    send[...] = jnp.zeros_like(send)
    for j in range(tiles):
        lanes = slice(tile * j, tile * (j + 1))
        grad = total[:, wide * j : wide * j + tile]
        keep[0:4, lanes] = jnp.where(first, grad[:4], grad[4:])
        send[0:4, lanes] = jnp.where(first, grad[4:], grad[:4])
        for k in range(tile // 128):
            row = total[k : k + 1, wide * j + tile : wide * (j + 1)]
            lane = slice(tile * j + 128 * k, tile * j + 128 * (k + 1))
            keep[4:5, lane] = row
            send[4:5, lane] = row


def final_kernel(core, keep, received, unit, root, gain, loss, loss_out, grad_out, gain_out):
    line = loss[pl.ds(core[1 + 2 * chunks], 1), :]
    loss_out[...] = pltpu.roll(line, core[2 + 2 * chunks], 1)[0, :4]
    first = core[0] == 0
    near, far = keep[...], received[...]
    both = jnp.concatenate([jnp.where(first, near, far), jnp.where(first, far, near)], axis=1)
    gain_out[...] = both[4:5].reshape(width)
    grad_unit = both[0:4] * gain[...]
    rows = unit[...]
    inner = jnp.mean(grad_unit * rows, axis=1, keepdims=True)
    grad_out[...] = (grad_unit - rows * inner) / root[:, 0:1]


def call(kernel, core, args, out_shape, scratch=(), grid=(1,), out_specs=None, room=16):
    here = pl.BlockSpec(memory_space=pltpu.VMEM)
    return pl.pallas_call(
        kernel,
        grid_spec=pltpu.PrefetchScalarGridSpec(
            num_scalar_prefetch=1,
            grid=grid,
            in_specs=[here] * len(args),
            out_specs=out_specs or jax.tree.map(lambda _: here, out_shape),
            scratch_shapes=scratch,
        ),
        out_shape=out_shape,
        **params(room),
    )(core, *args)


def shape(dims, dtype):
    return jax.ShapeDtypeStruct(dims, dtype)


def body(hidden, norm_gain, weight, targets):
    vocab = weight.shape[0]
    place = [lax.axis_index(name) for name in every]
    device = ((place[0] * 2 + place[1]) * 4 + place[2]) * 4 + place[3]
    token = ((place[0] * 4 + place[2]) * 4 + place[3]) * 8 + place[1] * 4
    steps = jnp.arange(4, dtype=jnp.int32)
    by_x = ((place[0] + steps) % 4 * 4)[:, None] + steps[None, :]
    by_y = steps[None, :] * 4 + ((place[2] + steps) % 4)[:, None]
    first = place[1] == 0
    core = jnp.concatenate(
        [
            place[1][None],
            jnp.where(first, by_x, by_y).reshape(chunks),
            jnp.where(first, by_y, by_x).reshape(chunks),
            (token // 128)[None],
            ((128 - token % 128) % 128)[None],
        ]
    )
    gain = norm_gain

    labels = targets.reshape(4, 2, 16, 4).transpose(0, 2, 1, 3).reshape(4, 128) - device * vocab
    spread, unit, root, gain = call(
        norm_kernel,
        core,
        (hidden, other_core(hidden), gain),
        [
            shape((plane, 8, half), bf16),
            shape((4, width), f32),
            shape((4, 128), f32),
            shape((1, width), f32),
        ],
    )
    spread, labels = lax.optimization_barrier((spread, labels))
    near = over_plane(spread).reshape(block, half)
    near = [near, *(along_line(near, -d) for d in (1, 2, 3))]
    local, late = lax.optimization_barrier((near[0], labels))
    target = call(far_target_kernel, core, (weight, late), shape((tokens, half), bf16))
    local, target = lax.optimization_barrier((local, target))
    target = other_core(target)
    parts = []
    far = [None] * 4
    for group in ((0,), (1, 2, 3)):
        for d in group:
            far[d] = other_core(near[d])
        part = call(
            near_logits_kernel,
            core,
            (*(near[d] if d else local for d in group), weight),
            shape((len(group) * block, vocab), f32),
            [pltpu.VMEM((len(group) * block, half), bf16)],
        )
        if group[0] == 0:
            part, near[1], near[2], near[3] = lax.optimization_barrier((part, *near[1:]))
        parts.append(part)
    capped, stats, others = call(
        logits_kernel,
        core,
        (*far, weight, *parts, labels),
        [shape((tokens, vocab), f32), shape((8, 128), f32), shape((tokens, vocab), bf16)],
        [pltpu.VMEM((tokens, half), bf16)],
    )
    stats = stats + other_core(stats)
    far_grad = call(far_grad_kernel, core, (others, weight), shape((tokens, half), bf16))
    stats, far_grad = lax.optimization_barrier((stats, far_grad))
    received = other_core(far_grad)
    stats = jnp.broadcast_to(stats[None], (n_chips, 8, 128))
    stats = lax.all_to_all(stats, chips, 0, 0, tiled=True)
    *sums, loss, totals = call(
        combine_kernel,
        core,
        (capped, stats, labels, weight, received, target, *near, gain),
        [shape((block, half + 128), bf16)] * 4 + [shape((4, 128), f32)] * 2,
        [
            pltpu.VMEM((tokens, vocab), bf16),
            pltpu.VMEM((tokens, tile), f32),
            pltpu.VMEM((tokens, 1), f32),
            pltpu.VMEM((tokens, 1), f32),
        ],
    )
    arrived = [along_line(sums[d], d) for d in (1, 2, 3)]
    local = sums[0]
    grad_head = call(
        head_kernel,
        core,
        (capped, totals, labels, *near, *far),
        shape((vocab, width), bf16),
        [
            pltpu.VMEM((vocab, tokens), bf16),
            pltpu.VMEM((tiles, tokens, tile), bf16),
            pltpu.VMEM((tiles, tokens, tile), bf16),
        ],
        grid=(2 * tiles,),
        out_specs=pl.BlockSpec((vocab, tile), lambda j, c: (0, j)),
    )
    grad_head, local = lax.optimization_barrier((grad_head, local))
    packed = call(add_kernel, core, (local, *arrived), shape((block, tiles * wide), bf16))
    packed = over_plane(packed.reshape(plane, 8, tiles * wide))

    keep, send = call(sum_kernel, core, (packed,), [shape((8, half), f32)] * 2)
    token_loss, grad_hidden, grad_gain = call(
        final_kernel,
        core,
        (keep, other_core(send), unit, root, gain, loss),
        [shape((4,), f32), shape((4, width), f32), shape((width,), f32)],
    )
    return (token_loss, grad_gain, grad_hidden, grad_head)


def solution(mesh):
    fine = Mesh(mesh.devices.reshape(4, 2, 4, 4), every)
    rows = P(every, None)
    return jax.shard_map(
        body,
        mesh=fine,
        in_specs=(rows, P(), rows, P()),
        out_specs=(P(every), P(), rows, rows),
        check_vma=False,
    )
```

time: 129 us -> 117 us (0.907)
  waiting for transfers between devices: 24.3 us -> 9.17 us
  blocking collectives: 36.1 us -> 47.9 us
  local copies, waits for them, and re-layouts: 10.7 us -> 5.78 us
  starting transfers between devices: 21.3 us -> 18.1 us
    all_to_all x1 -> x2, blocking collectives: 18 us -> 30.8 us  [over_plane(): lax.all_to_all(array, every, 0, 0, axis_index_groups=planes, tiled=True)]
    all_to_all x1 -> x0, waiting for transfers between devices: 10.7 us -> none  [over_plane(): lax.all_to_all(array, every, 0, 0, axis_index_groups=planes, tiled=True)]
    all_to_all x1 -> x0, starting transfers between devices: 3.6 us -> none  [over_plane(): lax.all_to_all(array, every, 0, 0, axis_index_groups=planes, tiled=True)]
    ppermute x6, waiting for transfers between devices: 11 us -> 8.03 us  [along_line(): return lax.ppermute(array, every, pairs)]
    unnamed x8, local copies, waits for them, and re-layouts: 8 us -> 5.24 us
    ppermute x8 -> x9, waiting for transfers between devices: 2.57 us -> 1.15 us  [other_core(): return lax.ppermute(array, every, swap_cores)]
    ppermute x8 -> x9, starting transfers between devices: 10.1 us -> 10.7 us  [other_core(): return lax.ppermute(array, every, swap_cores)]
  transfers between devices with their start and end apart: 15 -> 15, of which waited for: 8 -> 5; matrix products, arithmetic and copies ran while one was open for 3% -> 1% of each run, Pallas kernels for 13% -> 17%
where the time goes in v3:
time: 117 us
  blocking collectives  47.9 us (41%)
  Pallas kernels  34 us (29%)
  starting transfers between devices  18.1 us (15%)
  waiting for transfers between devices  9.17 us (8%)
  local copies, waits for them, and re-layouts  5.78 us (5%)
    pallas_call x11, Pallas kernels, call(): pl.pallas_call(kernel, grid_spec=pltpu.PrefetchScalarGridSpec(num_scalar_...  34 us
    all_to_all x2, blocking collectives, over_plane(): lax.all_to_all(array, every, 0, 0, axis_index_groups=planes, tiled=True)  30.8 us
    all_to_all x1, blocking collectives, body(): stats = lax.all_to_all(stats, chips, 0, 0, tiled=True)  17.1 us
    ppermute x9, starting transfers between devices, other_core(): return lax.ppermute(array, every, swap_cores)  10.7 us
    ppermute x6, waiting for transfers between devices, along_line(): return lax.ppermute(array, every, pairs)  8.03 us
    ppermute x6, starting transfers between devices, along_line(): return lax.ppermute(array, every, pairs)  7.41 us
    unnamed x8, local copies, waits for them, and re-layouts  5.24 us
  transfers between devices with their start and end apart: 15, of which 5 were waited for; matrix products, arithmetic and copies ran while one was open for 1% of the time, Pallas kernels for 17%

profile of v3, /device:TPU:1, one launch (start us, length us, event | category | flops | bytes accessed | tf_op | source)
XLA Modules:
  0.0 116.5 jit_solution(16215548950781562235)
XLA Ops:
  0.6 1.5 %collective-permute-start = (bf16[4,4608]{1,0:T(4,128)(2,1)}, bf16[4,4608]{1,0:T(4,128)(2,1)S(1)}, u32[]{:S(2)}, u32[]{:S(2)}) collective-permute-start(bf16[4,4608]{1,0:T(4,128)(2,1)} %mine.1), channel_id=1, source_target_pairs={{0,16},{1,17},{2,18},{3,19},{4,20},{5,21},{6,22},{7,23},{8,24},{9,... | collective-permute-start | bytes 110600 | tf_op jit(solution)/shard_map/ppermute | solution.py:40
  2.2 0.1 add_select_fusion
  2.2 0.7 broadcast_subtract_fusion
  2.9 0.1 select_n.59
  3.0 0.1 select_n.57
  3.1 0.1 sub.26
  3.2 0.1 sub.28.labels
  3.4 0.1 concatenate.3.core
  3.5 0.0 collective-permute-done.theirs
  3.5 0.0 copy-start.2
  3.5 0.8 copy-done.2
  4.2 0.0 copy-start.3
  4.2 0.7 copy-done.3
  5.0 0.7 shard_map.75
  5.7 17.9 %all_to_all.15 = bf16[16,8,2304]{2,1,0:T(8,128)(2,1)S(1)} all-to-all(bf16[16,8,2304]{2,1,0:T(8,128)(2,1)S(1)} %get-tuple-element.37), channel_id=1, replica_groups={{0,1,2,3,4,5,6,7,8,9,10,11,12,13,14,15},{32,33,34,35,36,37,38,39,40,41,..., dimensions={0} | all-to-all | bytes 1179648 | tf_op jit(solution)/shard_map/all_to_all | solution.py:51
  23.7 1.2 %collective-permute-start.4 = (bf16[128,2304]{1,0:T(8,128)(2,1)S(1)}, bf16[128,2304]{1,0:T(8,128)(2,1)S(1)}, u32[]{:S(2)}, u32[]{:S(2)}) collective-permute-start(bf16[128,2304]{1,0:T(8,128)(2,1)S(1)} %bitcast.6), channel_id=1, source_target_pairs={{0,32},{1,33},{2,34},{3,35},{4,36},{5,37},{6,38},{7,39},{8,40},{9,... | collective-permute-start | bytes 1769480 | tf_op jit(solution)/shard_map/ppermute | solution.py:47
  24.9 2.3 %collective-permute-start.3 = (bf16[128,2304]{1,0:T(8,128)(2,1)S(1)}, bf16[128,2304]{1,0:T(8,128)(2,1)S(1)}, u32[]{:S(2)}, u32[]{:S(2)}) collective-permute-start(bf16[128,2304]{1,0:T(8,128)(2,1)S(1)} %bitcast.7), channel_id=1, source_target_pairs={{0,64},{1,65},{2,66},{3,67},{4,68},{5,69},{6,70},{7,71},{8,72},{9,... | collective-permute-start | bytes 1769480 | tf_op jit(solution)/shard_map/ppermute | solution.py:47
  27.2 1.1 collective-permute-start.2
  28.3 1.6 %collective-permute-start.1 = (bf16[128,2304]{1,0:T(8,128)(2,1)S(1)}, bf16[128,2304]{1,0:T(8,128)(2,1)S(1)}, u32[]{:S(2)}, u32[]{:S(2)}) collective-permute-start(bf16[128,2304]{1,0:T(8,128)(2,1)S(1)} %bitcast.9), channel_id=1, source_target_pairs={{0,16},{1,17},{2,18},{3,19},{4,20},{5,21},{6,22},{7,23},{8,24},{9,... | collective-permute-start | bytes 1769480 | tf_op jit(solution)/shard_map/ppermute | solution.py:40
  29.9 0.0 copy-start
  29.9 3.6 %copy-done = bf16[1000,4608]{1,0:T(8,128)(2,1)S(1)} copy-done((bf16[1000,4608]{1,0:T(8,128)(2,1)S(1)}, bf16[1000,4608]{1,0:T(8,128)(2,1)}, u32[]{:S(2)}) %copy-start) | copy-done | bytes 9216024
  33.5 0.0 copy-start.1
  33.5 3.5 %shard_map.76 = bf16[512,2304]{1,0:T(8,128)(2,1)S(1)} custom-call(s32[35]{0:T(128)S(1)} %concatenate.3.core, bf16[1000,4608]{1,0:T(8,128)(2,1)S(1)} %copy-done, s32[4,128]{1,0:T(4,128)S(1)} %sub.28.labels), custom_call_target="tpu_custom_call" | custom-call | flops 1000 | bytes 1000 | tf_op jit(solution)/shard_map/pallas_call | solution.py:265
  37.0 0.1 copy-done.1
  37.1 2.1 %shard_map.77.part0 = f32[128,1000]{1,0:T(8,128)S(1)} custom-call(s32[35]{0:T(128)S(1)} %concatenate.3.core, bf16[128,2304]{1,0:T(8,128)(2,1)S(1)} %bitcast.10, bf16[1000,4608]{1,0:T(8,128)(2,1)S(1)} %copy-done.1), custom_call_target="tpu_custom_call" | custom-call | flops 1000 | bytes 1000 | tf_op jit(solution)/shard_map/pallas_call | solution.py:265
  39.2 0.0 collective-permute-done.4.refs_2_.n3
  39.2 1.8 %collective-permute-done.3.refs_1_.n2 = bf16[128,2304]{1,0:T(8,128)(2,1)S(1)} collective-permute-done((bf16[128,2304]{1,0:T(8,128)(2,1)S(1)}, bf16[128,2304]{1,0:T(8,128)(2,1)S(1)}, u32[]{:S(2)}, u32[]{:S(2)}) %collective-permute-start.3) | collective-permute-done | bytes 589856 | tf_op jit(solution)/shard_map/ppermute | solution.py:47
  41.0 0.0 collective-permute-done.2.refs_0_.n1
  41.0 2.1 %collective-permute-start.5 = (bf16[128,2304]{1,0:T(8,128)(2,1)S(1)}, bf16[128,2304]{1,0:T(8,128)(2,1)S(1)}, u32[]{:S(2)}, u32[]{:S(2)}) collective-permute-start(bf16[128,2304]{1,0:T(8,128)(2,1)S(1)} %collective-permute-done.2.refs_0_.n1), channel_id=1, source_target_pairs={{0,16},{1,17},{2,18},{3,19},{4,20},{5,21},{6,22},{7,23},{8,24},{9,... | collective-permute-start | bytes 1769480 | tf_op jit(solution)/shard_map/ppermute | solution.py:40
  43.2 0.0 collective-permute-start.6
  43.2 0.5 collective-permute-start.7
  43.7 2.6 %shard_map.78.part1 = f32[384,1000]{1,0:T(8,128)S(1)} custom-call(s32[35]{0:T(128)S(1)} %concatenate.3.core, bf16[128,2304]{1,0:T(8,128)(2,1)S(1)} %collective-permute-done.2.refs_0_.n1, bf16[128,2304]{1,0:T(8,128)(2,1)S(1)} %collective-permute-done.3.refs_1_.n2, bf16[128,2304]{1,0:T(8,128)(2,1)S(1)} %collective-permute-done.4.refs_2_.n3, ...), custom_call_target="tpu_custom_call" | custom-call | flops 1000 | bytes 1000 | tf_op jit(solution)/shard_map/pallas_call | solution.py:265
  46.3 0.0 collective-permute-done.1.b0.m0
  46.3 0.0 collective-permute-done.5.b1.m1
  46.3 0.0 collective-permute-done.6.b2.m2
  46.3 0.2 collective-permute-done.7.b3.m3
  46.5 4.8 %shard_map.79 = (f32[512,1000]{1,0:T(8,128)S(1)}, f32[8,128]{1,0:T(8,128)S(1)}, bf16[512,1000]{1,0:T(8,128)(2,1)S(1)}) custom-call(s32[35]{0:T(128)S(1)} %concatenate.3.core, bf16[128,2304]{1,0:T(8,128)(2,1)S(1)} %collective-permute-done.1.b0.m0, bf16[128,2304]{1,0:T(8,128)(2,1)S(1)} %collective-permute-done.5.b1.m1, ...), custom_call_target="tpu_custom_call" | custom-call | flops 1000 | bytes 1000 | tf_op jit(solution)/shard_map/pallas_call | solution.py:265
  51.3 0.4 collective-permute-start.8
  51.8 0.3 collective-permute-start.10
  52.0 3.2 %shard_map.80 = bf16[512,2304]{1,0:T(8,128)(2,1)S(1)} custom-call(s32[35]{0:T(128)S(1)} %concatenate.3.core, bf16[512,1000]{1,0:T(8,128)(2,1)S(1)} %get-tuple-element.48.others, bf16[1000,4608]{1,0:T(8,128)(2,1)S(1)} %copy-done.1), custom_call_target="tpu_custom_call" | custom-call | flops 1000 | bytes 1000 | tf_op jit(solution)/shard_map/pallas_call | solution.py:265
  55.2 0.0 collective-permute-done.8
  55.2 0.3 collective-permute-start.9
  55.5 17.1 %all_to_all.16.stats = f32[64,8,128]{2,1,0:T(8,128)S(1)} all-to-all(f32[64,8,128]{2,1,0:T(8,128)S(1)} %broadcast_in_dim.22), channel_id=1, replica_groups=mesh['x'=4,'c'=2,'y'=4,'z'=4] {'x','y','z'}, dimensions={0} | all-to-all | bytes 524288 | tf_op jit(solution)/shard_map/all_to_all | solution.py:349
  72.7 0.0 collective-permute-done.10.target
  72.7 0.0 collective-permute-done.9.received
  72.7 5.4 %shard_map.81 = (bf16[128,2432]{1,0:T(8,128)(2,1)S(1)}, bf16[128,2432]{1,0:T(8,128)(2,1)S(1)}, bf16[128,2432]{1,0:T(8,128)(2,1)S(1)}, bf16[128,2432]{1,0:T(8,128...) custom-call(s32[35]{0:T(128)S(1)} %concatenate.3.core, f32[512,1000]{1,0:T(8,128)S(1)} %get-tuple-element.46.capped, ...), custom_call_target="tpu_custom_call" | custom-call | flops 1000 | bytes 1000 | tf_op jit(solution)/shard_map/pallas_call | solution.py:265
  78.0 0.3 collective-permute-start.11
  78.3 1.1 collective-permute-start.12
  79.4 1.4 %collective-permute-start.13 = (bf16[128,2432]{1,0:T(8,128)(2,1)S(1)}, bf16[128,2432]{1,0:T(8,128)(2,1)S(1)}, u32[]{:S(2)}, u32[]{:S(2)}) collective-permute-start(bf16[128,2432]{1,0:T(8,128)(2,1)S(1)} %get-tuple-element.58), channel_id=1, source_target_pairs={{0,96},{1,97},{2,98},{3,99},{4,100},{5,101},{6,102},{7,103},{8,104... | collective-permute-start | bytes 1867784 | tf_op jit(solution)/shard_map/ppermute | solution.py:47
  80.8 9.0 %shard_map.82 = bf16[1000,4608]{1,0:T(8,128)(2,1)} custom-call(s32[35]{0:T(128)S(1)} %concatenate.3.core, f32[512,1000]{1,0:T(8,128)S(1)} %get-tuple-element.46.capped, f32[4,128]{1,0:T(4,128)S(1)} %get-tuple-element.53.stats, s32[4,128]{1,0:T(4,128)S(1)} %sub.28.labels, bf16[128,2304]{1,0:T(8,128)(2,1)S(1)} %bitcast.12, ...), custom_call_target="tpu_custom_call" | custom-call | flops 1000 | bytes 1000 | tf_op jit(solution)/shard_map/pallas_call | solution.py:265
  89.8 5.6 %collective-permute-done.11.b1 = bf16[128,2432]{1,0:T(8,128)(2,1)S(1)} collective-permute-done((bf16[128,2432]{1,0:T(8,128)(2,1)S(1)}, bf16[128,2432]{1,0:T(8,128)(2,1)S(1)}, u32[]{:S(2)}, u32[]{:S(2)}) %collective-permute-start.11) | collective-permute-done | bytes 622624 | tf_op jit(solution)/shard_map/ppermute | solution.py:47
  95.4 0.0 collective-permute-done.12.b2
  95.4 0.6 collective-permute-done.13.b3
  96.0 0.8 shard_map.83
  96.8 12.8 %all_to_all.17.blocks = bf16[16,8,2688]{2,1,0:T(8,128)(2,1)S(1)} all-to-all(bf16[16,8,2688]{2,1,0:T(8,128)(2,1)S(1)} %bitcast.13), channel_id=1, replica_groups={{0,1,2,3,4,5,6,7,8,9,10,11,12,13,14,15},{32,33,34,35,36,37,38,39,40,41,..., dimensions={0} | all-to-all | bytes 1376256 | tf_op jit(solution)/shard_map/all_to_all | solution.py:51
  109.7 0.6 shard_map.84
  110.3 4.0 %collective-permute-start.14 = (f32[8,2304]{1,0:T(8,128)S(1)}, f32[8,2304]{1,0:T(8,128)S(1)}, u32[]{:S(2)}, u32[]{:S(2)}) collective-permute-start(f32[8,2304]{1,0:T(8,128)S(1)} %get-tuple-element.60), channel_id=1, source_target_pairs={{0,16},{1,17},{2,18},{3,19},{4,20},{5,21},{6,22},{7,23},{8,24},{9,... | collective-permute-start | bytes 221192 | tf_op jit(solution)/shard_map/ppermute | solution.py:40
  114.3 0.9 collective-permute-done.14.received
  115.2 1.3 %shard_map.85 = (f32[4]{0:T(128)}, f32[4,4608]{1,0:T(4,128)}, f32[4608]{0:T(1024)}) custom-call(s32[35]{0:T(128)S(1)} %concatenate.3.core, f32[8,2304]{1,0:T(8,128)S(1)} %get-tuple-element.59.keep, f32[8,2304]{1,0:T(8,128)S(1)} %collective-permute-done.14.received, f32[4,4608]{1,0:T(4,128)S(1)} %get-tuple-element.61.unit, ...), custom_call_target="tpu_custom_call" | custom-call | flops 1000 | bytes 1000 | tf_op jit(solution)/shard_map/pallas_call | solution.py:265
  (5 shorter events, 0.1 us)
Async XLA Ops:
  0.6 2.8 %collective-permute-start = (bf16[4,4608]{1,0:T(4,128)(2,1)}, bf16[4,4608]{1,0:T(4,128)(2,1)S(1)}, u32[]{:S(2)}, u32[]{:S(2)}) collective-permute-start(bf16[4,4608]{1,0:T(4,128)(2,1)} %mine.1), channel_id=1, source_target_pairs={{0,16},{1,17},{2,18},{3,19},{4,20},{5,21},{6,22},{7,23},{8,24},{9,... | collective-permute-start | bytes 110600 | tf_op jit(solution)/shard_map/ppermute | solution.py:40
  3.5 0.8 copy-start.2
  4.2 0.7 copy-start.3
  23.7 15.5 %collective-permute-start.4 = (bf16[128,2304]{1,0:T(8,128)(2,1)S(1)}, bf16[128,2304]{1,0:T(8,128)(2,1)S(1)}, u32[]{:S(2)}, u32[]{:S(2)}) collective-permute-start(bf16[128,2304]{1,0:T(8,128)(2,1)S(1)} %bitcast.6), channel_id=1, source_target_pairs={{0,32},{1,33},{2,34},{3,35},{4,36},{5,37},{6,38},{7,39},{8,40},{9,... | collective-permute-start | bytes 1769480 | tf_op jit(solution)/shard_map/ppermute | solution.py:47
  24.9 16.1 %collective-permute-start.3 = (bf16[128,2304]{1,0:T(8,128)(2,1)S(1)}, bf16[128,2304]{1,0:T(8,128)(2,1)S(1)}, u32[]{:S(2)}, u32[]{:S(2)}) collective-permute-start(bf16[128,2304]{1,0:T(8,128)(2,1)S(1)} %bitcast.7), channel_id=1, source_target_pairs={{0,64},{1,65},{2,66},{3,67},{4,68},{5,69},{6,70},{7,71},{8,72},{9,... | collective-permute-start | bytes 1769480 | tf_op jit(solution)/shard_map/ppermute | solution.py:47
  27.2 13.9 %collective-permute-start.2 = (bf16[128,2304]{1,0:T(8,128)(2,1)S(1)}, bf16[128,2304]{1,0:T(8,128)(2,1)S(1)}, u32[]{:S(2)}, u32[]{:S(2)}) collective-permute-start(bf16[128,2304]{1,0:T(8,128)(2,1)S(1)} %bitcast.8), channel_id=1, source_target_pairs={{0,96},{1,97},{2,98},{3,99},{4,100},{5,101},{6,102},{7,103},{8,104... | collective-permute-start | bytes 1769480 | tf_op jit(solution)/shard_map/ppermute | solution.py:47
  28.3 18.0 %collective-permute-start.1 = (bf16[128,2304]{1,0:T(8,128)(2,1)S(1)}, bf16[128,2304]{1,0:T(8,128)(2,1)S(1)}, u32[]{:S(2)}, u32[]{:S(2)}) collective-permute-start(bf16[128,2304]{1,0:T(8,128)(2,1)S(1)} %bitcast.9), channel_id=1, source_target_pairs={{0,16},{1,17},{2,18},{3,19},{4,20},{5,21},{6,22},{7,23},{8,24},{9,... | collective-permute-start | bytes 1769480 | tf_op jit(solution)/shard_map/ppermute | solution.py:40
  29.9 3.6 %copy-start = (bf16[1000,4608]{1,0:T(8,128)(2,1)S(1)}, bf16[1000,4608]{1,0:T(8,128)(2,1)}, u32[]{:S(2)}) copy-start(bf16[1000,4608]{1,0:T(8,128)(2,1)} %weight.7) | copy-start | bytes 27648004
  33.5 3.6 %copy-start.1 = (bf16[1000,4608]{1,0:T(8,128)(2,1)S(1)}, bf16[1000,4608]{1,0:T(8,128)(2,1)}, u32[]{:S(2)}) copy-start(bf16[1000,4608]{1,0:T(8,128)(2,1)} %weight.7) | copy-start | bytes 27648004
  41.0 5.2 %collective-permute-start.5 = (bf16[128,2304]{1,0:T(8,128)(2,1)S(1)}, bf16[128,2304]{1,0:T(8,128)(2,1)S(1)}, u32[]{:S(2)}, u32[]{:S(2)}) collective-permute-start(bf16[128,2304]{1,0:T(8,128)(2,1)S(1)} %collective-permute-done.2.refs_0_.n1), channel_id=1, source_target_pairs={{0,16},{1,17},{2,18},{3,19},{4,20},{5,21},{6,22},{7,23},{8,24},{9,... | collective-permute-start | bytes 1769480 | tf_op jit(solution)/shard_map/ppermute | solution.py:40
  43.2 3.1 %collective-permute-start.6 = (bf16[128,2304]{1,0:T(8,128)(2,1)S(1)}, bf16[128,2304]{1,0:T(8,128)(2,1)S(1)}, u32[]{:S(2)}, u32[]{:S(2)}) collective-permute-start(bf16[128,2304]{1,0:T(8,128)(2,1)S(1)} %collective-permute-done.3.refs_1_.n2), channel_id=1, source_target_pairs={{0,16},{1,17},{2,18},{3,19},{4,20},{5,21},{6,22},{7,23},{8,24},{9,... | collective-permute-start | bytes 1769480 | tf_op jit(solution)/shard_map/ppermute | solution.py:40
  43.2 3.3 %collective-permute-start.7 = (bf16[128,2304]{1,0:T(8,128)(2,1)S(1)}, bf16[128,2304]{1,0:T(8,128)(2,1)S(1)}, u32[]{:S(2)}, u32[]{:S(2)}) collective-permute-start(bf16[128,2304]{1,0:T(8,128)(2,1)S(1)} %collective-permute-done.4.refs_2_.n3), channel_id=1, source_target_pairs={{0,16},{1,17},{2,18},{3,19},{4,20},{5,21},{6,22},{7,23},{8,24},{9,... | collective-permute-start | bytes 1769480 | tf_op jit(solution)/shard_map/ppermute | solution.py:40
  51.3 3.9 %collective-permute-start.8 = (f32[8,128]{1,0:T(8,128)S(1)}, f32[8,128]{1,0:T(8,128)S(1)}, u32[]{:S(2)}, u32[]{:S(2)}) collective-permute-start(f32[8,128]{1,0:T(8,128)S(1)} %get-tuple-element.47), channel_id=1, source_target_pairs={{0,16},{1,17},{2,18},{3,19},{4,20},{5,21},{6,22},{7,23},{8,24},{9,... | collective-permute-start | bytes 12296 | tf_op jit(solution)/shard_map/ppermute | solution.py:40
  51.8 20.9 %collective-permute-start.10 = (bf16[512,2304]{1,0:T(8,128)(2,1)S(1)}, bf16[512,2304]{1,0:T(8,128)(2,1)S(1)}, u32[]{:S(2)}, u32[]{:S(2)}) collective-permute-start(bf16[512,2304]{1,0:T(8,128)(2,1)S(1)} %shard_map.76), channel_id=1, source_target_pairs={{0,16},{1,17},{2,18},{3,19},{4,20},{5,21},{6,22},{7,23},{8,24},{9,... | collective-permute-start | bytes 7077896 | tf_op jit(solution)/shard_map/ppermute | solution.py:40
  55.2 17.4 %collective-permute-start.9 = (bf16[512,2304]{1,0:T(8,128)(2,1)S(1)}, bf16[512,2304]{1,0:T(8,128)(2,1)S(1)}, u32[]{:S(2)}, u32[]{:S(2)}) collective-permute-start(bf16[512,2304]{1,0:T(8,128)(2,1)S(1)} %shard_map.80), channel_id=1, source_target_pairs={{0,16},{1,17},{2,18},{3,19},{4,20},{5,21},{6,22},{7,23},{8,24},{9,... | collective-permute-start | bytes 7077896 | tf_op jit(solution)/shard_map/ppermute | solution.py:40
  78.0 17.3 %collective-permute-start.11 = (bf16[128,2432]{1,0:T(8,128)(2,1)S(1)}, bf16[128,2432]{1,0:T(8,128)(2,1)S(1)}, u32[]{:S(2)}, u32[]{:S(2)}) collective-permute-start(bf16[128,2432]{1,0:T(8,128)(2,1)S(1)} %get-tuple-element.56), channel_id=1, source_target_pairs={{0,32},{1,33},{2,34},{3,35},{4,36},{5,37},{6,38},{7,39},{8,40},{9,... | collective-permute-start | bytes 1867784 | tf_op jit(solution)/shard_map/ppermute | solution.py:47
  78.3 17.0 %collective-permute-start.12 = (bf16[128,2432]{1,0:T(8,128)(2,1)S(1)}, bf16[128,2432]{1,0:T(8,128)(2,1)S(1)}, u32[]{:S(2)}, u32[]{:S(2)}) collective-permute-start(bf16[128,2432]{1,0:T(8,128)(2,1)S(1)} %get-tuple-element.57), channel_id=1, source_target_pairs={{0,64},{1,65},{2,66},{3,67},{4,68},{5,69},{6,70},{7,71},{8,72},{9,... | collective-permute-start | bytes 1867784 | tf_op jit(solution)/shard_map/ppermute | solution.py:47
  79.4 16.6 %collective-permute-start.13 = (bf16[128,2432]{1,0:T(8,128)(2,1)S(1)}, bf16[128,2432]{1,0:T(8,128)(2,1)S(1)}, u32[]{:S(2)}, u32[]{:S(2)}) collective-permute-start(bf16[128,2432]{1,0:T(8,128)(2,1)S(1)} %get-tuple-element.58), channel_id=1, source_target_pairs={{0,96},{1,97},{2,98},{3,99},{4,100},{5,101},{6,102},{7,103},{8,104... | collective-permute-start | bytes 1867784 | tf_op jit(solution)/shard_map/ppermute | solution.py:47
  110.3 4.9 %collective-permute-start.14 = (f32[8,2304]{1,0:T(8,128)S(1)}, f32[8,2304]{1,0:T(8,128)S(1)}, u32[]{:S(2)}, u32[]{:S(2)}) collective-permute-start(f32[8,2304]{1,0:T(8,128)S(1)} %get-tuple-element.60), channel_id=1, source_target_pairs={{0,16},{1,17},{2,18},{3,19},{4,20},{5,21},{6,22},{7,23},{8,24},{9,... | collective-permute-start | bytes 221192 | tf_op jit(solution)/shard_map/ppermute | solution.py:40

commit v4 on v3

--- a/solution.py
+++ b/solution.py
@@ -21,6 +21,7 @@
 wide = tile + 128
 
 plane = 16
+vocab_tile = 256
 block = tokens // 4
 chunk = 32
 chunks = tokens // chunk
@@ -119,27 +120,39 @@
     )
 
 
-def logits_kernel(core, b0, b1, b2, b3, weight, part0, part1, labels, out, stats, others, rows):
+def logits_kernel(
+    core, b0, b1, b2, b3, weight, part0, part1, labels, out, stats, others, rows
+):
     assemble(lambda i: core[1 + chunks + i], (b0, b1, b2, b3), rows)
-    out[...] = lax.dot_general(
-        rows[...], half_of(weight, 1 - core[0]), (((1,), (1,)), ((), ())), preferred_element_type=f32
-    )
-    for i in range(chunks):
-        row = pl.multiple_of(core[1 + i] * chunk, chunk)
-        part = part0[chunk * i : chunk * (i + 1), :] if i < 4 else part1[chunk * (i - 4) : chunk * (i - 3), :]
-        out[pl.ds(row, chunk), :] += part
+    vocab = weight.shape[0]
+    from_start = pl.ds(pl.multiple_of((1 - core[0]) * half, half), half)
+    marks = [turned_column(labels[j : j + 1, :].astype(f32)).astype(jnp.int32) for j in range(4)]
+    totals = [jnp.zeros((128, 1), f32)] * 4
+    picks = [jnp.zeros((128, 1), f32)] * 4
+    for start in range(0, vocab, vocab_tile):
+        some = slice(start, min(start + vocab_tile, vocab))
+        out[:, some] = lax.dot_general(
+            rows[...], weight[some, from_start], (((1,), (1,)), ((), ())), preferred_element_type=f32
+        )
+        for i in range(chunks):
+            row = pl.multiple_of(core[1 + i] * chunk, chunk)
+            part, at = (part0, i) if i < 4 else (part1, i - 4)
+            out[pl.ds(row, chunk), some] += part[chunk * at : chunk * (at + 1), some]
+        for j in range(4):
+            lines = slice(128 * j, 128 * (j + 1))
+            capped = soft_cap * jnp.tanh(out[lines, some] / soft_cap)
+            hit = lax.broadcasted_iota(jnp.int32, capped.shape, 1) + start == marks[j]
+            exps = jnp.exp(capped)
+            slope = 1.0 - (capped / soft_cap) ** 2
+            rest = jnp.where(hit, 0.0, exps * slope)
+            out[lines, some] = rest
+            others[lines, some] = rest.astype(bf16)
+            totals[j] = totals[j] + jnp.sum(exps, axis=1, keepdims=True)
+            picked = jnp.where(hit, capped, 0.0)
+            picks[j] = picks[j] + jnp.sum(picked, axis=1, keepdims=True)
     for j in range(4):
-        lines = slice(128 * j, 128 * (j + 1))
-        capped = soft_cap * jnp.tanh(out[lines, :] / soft_cap)
-        out[lines, :] = capped
-        hit = hits_of(labels, j, capped.shape)
-        exps = jnp.exp(capped)
-        slope = 1.0 - (capped / soft_cap) ** 2
-        others[lines, :] = jnp.where(hit, 0.0, exps * slope).astype(bf16)
-        total = jnp.sum(exps, axis=1, keepdims=True)
-        picked = jnp.sum(jnp.where(hit, capped, 0.0), axis=1, keepdims=True)
-        stats[j : j + 1, :] = jnp.broadcast_to(total, (128, 128)).T[0:1, :]
-        stats[4 + j : 5 + j, :] = jnp.broadcast_to(picked, (128, 128)).T[0:1, :]
+        stats[j : j + 1, :] = jnp.broadcast_to(totals[j], (128, 128)).T[0:1, :]
+        stats[4 + j : 5 + j, :] = jnp.broadcast_to(picks[j], (128, 128)).T[0:1, :]
 
 
 def far_grad_kernel(core, others, weight, out):
@@ -148,36 +161,35 @@
 
 
 def combine_kernel(
-    core, capped, stats, labels, weight, received, target, n0, n1, n2, n3, gain,
-    o0, o1, o2, o3, loss, totals, dlogit, held, inverse, factor
+    core, others, stats, labels, weight, received, target, n0, n1, n2, n3, gain,
+    o0, o1, o2, o3, loss, marks, dlogit, held, inverse, factor
 ):
     sums = jnp.sum(stats[...], axis=0)
     total, picked = sums[0:4, :], sums[4:8, :]
-    totals[...] = total
     loss[...] = jnp.log(total) - picked
     slack = (jnp.exp(picked) / total - 1.0) * (1.0 - (picked / soft_cap) ** 2)
     scale = 1.0 / total
+    marks[0:4, :] = scale
+    marks[4:8, :] = slack
     for j in range(4):
         lines = slice(128 * j, 128 * (j + 1))
         inverse[lines, :] = turned_column(scale[j : j + 1, :])
         factor[lines, :] = turned_column(slack[j : j + 1, :])
-        value = capped[lines, :]
-        onehot = hits_of(labels, j, value.shape).astype(f32)
-        slope = 1.0 - (value / soft_cap) ** 2
-        share = jnp.exp(value) / turned_column(total[j : j + 1, :])
-        dlogit[lines, :] = ((share - onehot) * slope).astype(bf16)
+        hit = hits_of(labels, j, (128, weight.shape[0]))
+        rest = others[lines, :] * turned_column(scale[j : j + 1, :])
+        dlogit[lines, :] = jnp.where(hit, turned_column(slack[j : j + 1, :]), rest).astype(bf16)
     for out in (o0, o1, o2, o3):
         out[:, half:] = jnp.zeros((block, 128), bf16)
     for j in range(tiles):
         lanes = slice(tile * j, tile * (j + 1))
         from_start = pl.ds(pl.multiple_of(core[0] * half + tile * j, tile), tile)
-        held[...] = jnp.dot(dlogit[...], weight[:, from_start], preferred_element_type=f32)
+        held[j] = jnp.dot(dlogit[...], weight[:, from_start], preferred_element_type=f32)
         part = jnp.zeros((8, tile), f32)
         for d, (out, normed) in enumerate(((o0, n0), (o1, n1), (o2, n2), (o3, n3))):
             for k in range(4):
                 at = pl.ds(pl.multiple_of(core[1 + 4 * d + k] * chunk, chunk), chunk)
                 rows = slice(chunk * k, chunk * (k + 1))
-                value = held[at, :] + received[at, lanes].astype(f32) * inverse[at, :]
+                value = held[j, at, :] + received[at, lanes].astype(f32) * inverse[at, :]
                 value += target[at, lanes].astype(f32) * factor[at, :]
                 out[rows, lanes] = value.astype(bf16)
                 value = value * normed[rows, lanes].astype(f32)
@@ -189,19 +201,16 @@
             out[16 * j : 16 * (j + 1), half:] = sent
 
 
-def head_kernel(core, capped, stats, labels, n0, n1, n2, n3, m0, m1, m2, m3, out, turned, own, other):
+def head_kernel(core, others, marks, labels, n0, n1, n2, n3, m0, m1, m2, m3, out, turned, own, other):
     step = pl.program_id(0)
 
     @pl.when(step == 0)
     def _():
         for j in range(4):
             lines = slice(128 * j, 128 * (j + 1))
-            value = capped[lines, :].T
-            row = lax.broadcasted_iota(jnp.int32, value.shape, 0)
-            onehot = (row == labels[j : j + 1, :]).astype(f32)
-            slope = 1.0 - (value / soft_cap) ** 2
-            dlogit = (jnp.exp(value) / stats[j : j + 1, :] - onehot) * slope
-            turned[:, lines] = dlogit.astype(bf16)
+            rest = others[lines, :].T * marks[j : j + 1, :]
+            hit = lax.broadcasted_iota(jnp.int32, rest.shape, 0) == labels[j : j + 1, :]
+            turned[:, lines] = jnp.where(hit, marks[4 + j : 5 + j, :], rest).astype(bf16)
         for first, blocks, rows in ((1, (n0, n1, n2, n3), own), (1 + chunks, (m0, m1, m2, m3), other)):
             for d in range(4):
                 for k in range(4):
@@ -314,7 +323,8 @@
     )
     spread, labels = lax.optimization_barrier((spread, labels))
     near = over_plane(spread).reshape(block, half)
-    near = [near, *(along_line(near, -d) for d in (1, 2, 3))]
+    sent = {d: along_line(near, -d) for d in (2, 1, 3)}
+    near = [near, sent[1], sent[2], sent[3]]
     local, late = lax.optimization_barrier((near[0], labels))
     target = call(far_target_kernel, core, (weight, late), shape((tokens, half), bf16))
     local, target = lax.optimization_barrier((local, target))
@@ -322,7 +332,7 @@
     parts = []
     far = [None] * 4
     for group in ((0,), (1, 2, 3)):
-        for d in group:
+        for d in (0,) if group == (0,) else (2, 1, 3):
             far[d] = other_core(near[d])
         part = call(
             near_logits_kernel,
@@ -332,9 +342,11 @@
             [pltpu.VMEM((len(group) * block, half), bf16)],
         )
         if group[0] == 0:
-            part, near[1], near[2], near[3] = lax.optimization_barrier((part, *near[1:]))
+            part, near[2], near[1], near[3] = lax.optimization_barrier(
+                (part, near[2], near[1], near[3])
+            )
         parts.append(part)
-    capped, stats, others = call(
+    rest, stats, others = call(
         logits_kernel,
         core,
         (*far, weight, *parts, labels),
@@ -347,24 +359,24 @@
     received = other_core(far_grad)
     stats = jnp.broadcast_to(stats[None], (n_chips, 8, 128))
     stats = lax.all_to_all(stats, chips, 0, 0, tiled=True)
-    *sums, loss, totals = call(
+    *sums, loss, marks = call(
         combine_kernel,
         core,
-        (capped, stats, labels, weight, received, target, *near, gain),
-        [shape((block, half + 128), bf16)] * 4 + [shape((4, 128), f32)] * 2,
+        (rest, stats, labels, weight, received, target, *near, gain),
+        [shape((block, half + 128), bf16)] * 4 + [shape((4, 128), f32), shape((8, 128), f32)],
         [
             pltpu.VMEM((tokens, vocab), bf16),
-            pltpu.VMEM((tokens, tile), f32),
+            pltpu.VMEM((tiles, tokens, tile), f32),
             pltpu.VMEM((tokens, 1), f32),
             pltpu.VMEM((tokens, 1), f32),
         ],
     )
-    arrived = [along_line(sums[d], d) for d in (1, 2, 3)]
+    arrived = [along_line(sums[d], d) for d in (1, 3, 2)]
     local = sums[0]
     grad_head = call(
         head_kernel,
         core,
-        (capped, totals, labels, *near, *far),
+        (rest, marks, labels, *near, *far),
         shape((vocab, width), bf16),
         [
             pltpu.VMEM((vocab, tokens), bf16),

time: 117 us -> 115 us (0.983)
  starting transfers between devices: 18.1 us -> 16.6 us
  transfers between devices with their start and end apart: 15 -> 15, of which waited for: 5 -> 4; matrix products, arithmetic and copies ran while one was open for 1% -> 1% of each run, Pallas kernels for 17% -> 17%
where the time goes in v4:
time: 115 us
  blocking collectives  47.9 us (42%)
  Pallas kernels  33.2 us (29%)
  starting transfers between devices  16.6 us (14%)
  waiting for transfers between devices  9.42 us (8%)
  local copies, waits for them, and re-layouts  5.78 us (5%)
    pallas_call x11, Pallas kernels, call(): pl.pallas_call(kernel, grid_spec=pltpu.PrefetchScalarGridSpec(num_scalar_...  33.2 us
    all_to_all x2, blocking collectives, over_plane(): lax.all_to_all(array, every, 0, 0, axis_index_groups=planes, tiled=True)  30.8 us
    all_to_all x1, blocking collectives, body(): stats = lax.all_to_all(stats, chips, 0, 0, tiled=True)  17.1 us
    ppermute x9, starting transfers between devices, other_core(): return lax.ppermute(array, every, swap_cores)  9.82 us
    ppermute x6, waiting for transfers between devices, along_line(): return lax.ppermute(array, every, pairs)  8.28 us
    ppermute x6, starting transfers between devices, along_line(): return lax.ppermute(array, every, pairs)  6.77 us
    unnamed x8, local copies, waits for them, and re-layouts  5.24 us
  transfers between devices with their start and end apart: 15, of which 4 were waited for; matrix products, arithmetic and copies ran while one was open for 1% of the time, Pallas kernels for 17%

profile of v4, /device:TPU:1, one launch (start us, length us, event | category | flops | bytes accessed | tf_op | source)
XLA Modules:
  0.0 114.5 jit_solution(13168911724196777068)
XLA Ops:
  0.6 1.5 %collective-permute-start = (bf16[4,4608]{1,0:T(4,128)(2,1)}, bf16[4,4608]{1,0:T(4,128)(2,1)S(1)}, u32[]{:S(2)}, u32[]{:S(2)}) collective-permute-start(bf16[4,4608]{1,0:T(4,128)(2,1)} %mine.1), channel_id=1, source_target_pairs={{0,16},{1,17},{2,18},{3,19},{4,20},{5,21},{6,22},{7,23},{8,24},{9,... | collective-permute-start | bytes 110600 | tf_op jit(solution)/shard_map/ppermute | solution.py:41
  2.2 0.1 add_select_fusion
  2.2 0.7 broadcast_subtract_fusion
  2.9 0.1 select_n.59
  3.0 0.1 select_n.57
  3.1 0.1 sub.26
  3.2 0.1 sub.28.labels
  3.4 0.1 concatenate.3.core
  3.5 0.0 collective-permute-done.theirs
  3.5 0.0 copy-start.2
  3.5 0.8 copy-done.2
  4.2 0.0 copy-start.3
  4.2 0.7 copy-done.3
  5.0 0.7 shard_map.75
  5.7 17.9 %all_to_all.15 = bf16[16,8,2304]{2,1,0:T(8,128)(2,1)S(1)} all-to-all(bf16[16,8,2304]{2,1,0:T(8,128)(2,1)S(1)} %get-tuple-element.37), channel_id=1, replica_groups={{0,1,2,3,4,5,6,7,8,9,10,11,12,13,14,15},{32,33,34,35,36,37,38,39,40,41,..., dimensions={0} | all-to-all | bytes 1179648 | tf_op jit(solution)/shard_map/all_to_all | solution.py:52
  23.7 1.2 %collective-permute-start.4 = (bf16[128,2304]{1,0:T(8,128)(2,1)S(1)}, bf16[128,2304]{1,0:T(8,128)(2,1)S(1)}, u32[]{:S(2)}, u32[]{:S(2)}) collective-permute-start(bf16[128,2304]{1,0:T(8,128)(2,1)S(1)} %bitcast.6), channel_id=1, source_target_pairs={{0,32},{1,33},{2,34},{3,35},{4,36},{5,37},{6,38},{7,39},{8,40},{9,... | collective-permute-start | bytes 1769480 | tf_op jit(solution)/shard_map/ppermute | solution.py:48
  24.9 1.5 %collective-permute-start.3 = (bf16[128,2304]{1,0:T(8,128)(2,1)S(1)}, bf16[128,2304]{1,0:T(8,128)(2,1)S(1)}, u32[]{:S(2)}, u32[]{:S(2)}) collective-permute-start(bf16[128,2304]{1,0:T(8,128)(2,1)S(1)} %bitcast.7), channel_id=1, source_target_pairs={{0,96},{1,97},{2,98},{3,99},{4,100},{5,101},{6,102},{7,103},{8,104... | collective-permute-start | bytes 1769480 | tf_op jit(solution)/shard_map/ppermute | solution.py:48
  26.3 1.3 %collective-permute-start.2 = (bf16[128,2304]{1,0:T(8,128)(2,1)S(1)}, bf16[128,2304]{1,0:T(8,128)(2,1)S(1)}, u32[]{:S(2)}, u32[]{:S(2)}) collective-permute-start(bf16[128,2304]{1,0:T(8,128)(2,1)S(1)} %bitcast.8), channel_id=1, source_target_pairs={{0,64},{1,65},{2,66},{3,67},{4,68},{5,69},{6,70},{7,71},{8,72},{9,... | collective-permute-start | bytes 1769480 | tf_op jit(solution)/shard_map/ppermute | solution.py:48
  27.7 1.6 %collective-permute-start.1 = (bf16[128,2304]{1,0:T(8,128)(2,1)S(1)}, bf16[128,2304]{1,0:T(8,128)(2,1)S(1)}, u32[]{:S(2)}, u32[]{:S(2)}) collective-permute-start(bf16[128,2304]{1,0:T(8,128)(2,1)S(1)} %bitcast.9), channel_id=1, source_target_pairs={{0,16},{1,17},{2,18},{3,19},{4,20},{5,21},{6,22},{7,23},{8,24},{9,... | collective-permute-start | bytes 1769480 | tf_op jit(solution)/shard_map/ppermute | solution.py:41
  29.3 0.0 copy-start
  29.3 3.6 %copy-done = bf16[1000,4608]{1,0:T(8,128)(2,1)S(1)} copy-done((bf16[1000,4608]{1,0:T(8,128)(2,1)S(1)}, bf16[1000,4608]{1,0:T(8,128)(2,1)}, u32[]{:S(2)}) %copy-start) | copy-done | bytes 9216024
  32.9 0.0 copy-start.1
  32.9 3.5 %shard_map.76 = bf16[512,2304]{1,0:T(8,128)(2,1)S(1)} custom-call(s32[35]{0:T(128)S(1)} %concatenate.3.core, bf16[1000,4608]{1,0:T(8,128)(2,1)S(1)} %copy-done, s32[4,128]{1,0:T(4,128)S(1)} %sub.28.labels), custom_call_target="tpu_custom_call" | custom-call | flops 1000 | bytes 1000 | tf_op jit(solution)/shard_map/pallas_call | solution.py:274
  36.4 0.1 copy-done.1
  36.5 2.1 %shard_map.77.part0 = f32[128,1000]{1,0:T(8,128)S(1)} custom-call(s32[35]{0:T(128)S(1)} %concatenate.3.core, bf16[128,2304]{1,0:T(8,128)(2,1)S(1)} %bitcast.10, bf16[1000,4608]{1,0:T(8,128)(2,1)S(1)} %copy-done.1), custom_call_target="tpu_custom_call" | custom-call | flops 1000 | bytes 1000 | tf_op jit(solution)/shard_map/pallas_call | solution.py:274
  38.6 0.0 collective-permute-done.4.refs_2_.n3
  38.6 0.0 collective-permute-done.3.refs_0_.n1
  38.6 2.4 %collective-permute-done.2.refs_1_.n2 = bf16[128,2304]{1,0:T(8,128)(2,1)S(1)} collective-permute-done((bf16[128,2304]{1,0:T(8,128)(2,1)S(1)}, bf16[128,2304]{1,0:T(8,128)(2,1)S(1)}, u32[]{:S(2)}, u32[]{:S(2)}) %collective-permute-start.2) | collective-permute-done | bytes 589856 | tf_op jit(solution)/shard_map/ppermute | solution.py:48
  41.0 1.6 %collective-permute-start.5 = (bf16[128,2304]{1,0:T(8,128)(2,1)S(1)}, bf16[128,2304]{1,0:T(8,128)(2,1)S(1)}, u32[]{:S(2)}, u32[]{:S(2)}) collective-permute-start(bf16[128,2304]{1,0:T(8,128)(2,1)S(1)} %collective-permute-done.3.refs_0_.n1), channel_id=1, source_target_pairs={{0,16},{1,17},{2,18},{3,19},{4,20},{5,21},{6,22},{7,23},{8,24},{9,... | collective-permute-start | bytes 1769480 | tf_op jit(solution)/shard_map/ppermute | solution.py:41
  42.6 0.0 collective-permute-start.6
  42.6 0.5 collective-permute-start.7
  43.1 2.6 %shard_map.78.part1 = f32[384,1000]{1,0:T(8,128)S(1)} custom-call(s32[35]{0:T(128)S(1)} %concatenate.3.core, bf16[128,2304]{1,0:T(8,128)(2,1)S(1)} %collective-permute-done.3.refs_0_.n1, bf16[128,2304]{1,0:T(8,128)(2,1)S(1)} %collective-permute-done.2.refs_1_.n2, bf16[128,2304]{1,0:T(8,128)(2,1)S(1)} %collective-permute-done.4.refs_2_.n3, ...), custom_call_target="tpu_custom_call" | custom-call | flops 1000 | bytes 1000 | tf_op jit(solution)/shard_map/pallas_call | solution.py:274
  45.7 0.0 collective-permute-done.1.b0.m0
  45.7 0.0 collective-permute-done.5.b1.m1
  45.7 0.0 collective-permute-done.6.b2.m2
  45.7 0.2 collective-permute-done.7.b3.m3
  45.9 4.7 %shard_map.79 = (f32[512,1000]{1,0:T(8,128)S(1)}, f32[8,128]{1,0:T(8,128)S(1)}, bf16[512,1000]{1,0:T(8,128)(2,1)S(1)}) custom-call(s32[35]{0:T(128)S(1)} %concatenate.3.core, bf16[128,2304]{1,0:T(8,128)(2,1)S(1)} %collective-permute-done.1.b0.m0, bf16[128,2304]{1,0:T(8,128)(2,1)S(1)} %collective-permute-done.5.b1.m1, ...), custom_call_target="tpu_custom_call" | custom-call | flops 1000 | bytes 1000 | tf_op jit(solution)/shard_map/pallas_call | solution.py:274
  50.6 0.4 collective-permute-start.8
  51.0 0.3 collective-permute-start.10
  51.3 3.2 %shard_map.80 = bf16[512,2304]{1,0:T(8,128)(2,1)S(1)} custom-call(s32[35]{0:T(128)S(1)} %concatenate.3.core, bf16[512,1000]{1,0:T(8,128)(2,1)S(1)} %get-tuple-element.48.others, bf16[1000,4608]{1,0:T(8,128)(2,1)S(1)} %copy-done.1), custom_call_target="tpu_custom_call" | custom-call | flops 1000 | bytes 1000 | tf_op jit(solution)/shard_map/pallas_call | solution.py:274
  54.5 0.0 collective-permute-done.8
  54.5 0.3 collective-permute-start.9
  54.8 17.1 %all_to_all.16.stats = f32[64,8,128]{2,1,0:T(8,128)S(1)} all-to-all(f32[64,8,128]{2,1,0:T(8,128)S(1)} %broadcast_in_dim.22), channel_id=1, replica_groups=mesh['x'=4,'c'=2,'y'=4,'z'=4] {'x','y','z'}, dimensions={0} | all-to-all | bytes 524288 | tf_op jit(solution)/shard_map/all_to_all | solution.py:361
  71.9 0.0 collective-permute-done.10.target
  71.9 0.0 collective-permute-done.9.received
  72.0 5.0 %shard_map.81 = (bf16[128,2432]{1,0:T(8,128)(2,1)S(1)}, bf16[128,2432]{1,0:T(8,128)(2,1)S(1)}, bf16[128,2432]{1,0:T(8,128)(2,1)S(1)}, bf16[128,2432]{1,0:T(8,128...) custom-call(s32[35]{0:T(128)S(1)} %concatenate.3.core, f32[512,1000]{1,0:T(8,128)S(1)} %get-tuple-element.46.others, ...), custom_call_target="tpu_custom_call" | custom-call | flops 1000 | bytes 1000 | tf_op jit(solution)/shard_map/pallas_call | solution.py:274
  76.9 0.3 collective-permute-start.11
  77.2 2.4 %collective-permute-start.12 = (bf16[128,2432]{1,0:T(8,128)(2,1)S(1)}, bf16[128,2432]{1,0:T(8,128)(2,1)S(1)}, u32[]{:S(2)}, u32[]{:S(2)}) collective-permute-start(bf16[128,2432]{1,0:T(8,128)(2,1)S(1)} %get-tuple-element.57), channel_id=1, source_target_pairs={{0,96},{1,97},{2,98},{3,99},{4,100},{5,101},{6,102},{7,103},{8,104... | collective-permute-start | bytes 1867784 | tf_op jit(solution)/shard_map/ppermute | solution.py:48
  79.7 0.0 collective-permute-start.13
  79.7 8.7 %shard_map.82 = bf16[1000,4608]{1,0:T(8,128)(2,1)} custom-call(s32[35]{0:T(128)S(1)} %concatenate.3.core, f32[512,1000]{1,0:T(8,128)S(1)} %get-tuple-element.46.others, f32[8,128]{1,0:T(8,128)S(1)} %get-tuple-element.53.marks, s32[4,128]{1,0:T(4,128)S(1)} %sub.28.labels, bf16[128,2304]{1,0:T(8,128)(2,1)S(1)} %bitcast.12, ...), custom_call_target="tpu_custom_call" | custom-call | flops 1000 | bytes 1000 | tf_op jit(solution)/shard_map/pallas_call | solution.py:274
  88.4 5.8 %collective-permute-done.11.b1 = bf16[128,2432]{1,0:T(8,128)(2,1)S(1)} collective-permute-done((bf16[128,2432]{1,0:T(8,128)(2,1)S(1)}, bf16[128,2432]{1,0:T(8,128)(2,1)S(1)}, u32[]{:S(2)}, u32[]{:S(2)}) %collective-permute-start.11) | collective-permute-done | bytes 622624 | tf_op jit(solution)/shard_map/ppermute | solution.py:48
  94.3 0.0 collective-permute-done.12.b2
  94.3 0.0 collective-permute-done.13.b3
  94.3 0.8 shard_map.83
  95.1 12.8 %all_to_all.17.blocks = bf16[16,8,2688]{2,1,0:T(8,128)(2,1)S(1)} all-to-all(bf16[16,8,2688]{2,1,0:T(8,128)(2,1)S(1)} %bitcast.13), channel_id=1, replica_groups={{0,1,2,3,4,5,6,7,8,9,10,11,12,13,14,15},{32,33,34,35,36,37,38,39,40,41,..., dimensions={0} | all-to-all | bytes 1376256 | tf_op jit(solution)/shard_map/all_to_all | solution.py:52
  108.0 0.6 shard_map.84
  108.6 3.7 %collective-permute-start.14 = (f32[8,2304]{1,0:T(8,128)S(1)}, f32[8,2304]{1,0:T(8,128)S(1)}, u32[]{:S(2)}, u32[]{:S(2)}) collective-permute-start(f32[8,2304]{1,0:T(8,128)S(1)} %get-tuple-element.60), channel_id=1, source_target_pairs={{0,16},{1,17},{2,18},{3,19},{4,20},{5,21},{6,22},{7,23},{8,24},{9,... | collective-permute-start | bytes 221192 | tf_op jit(solution)/shard_map/ppermute | solution.py:41
  112.3 0.9 collective-permute-done.14.received
  113.2 1.3 %shard_map.85 = (f32[4]{0:T(128)}, f32[4,4608]{1,0:T(4,128)}, f32[4608]{0:T(1024)}) custom-call(s32[35]{0:T(128)S(1)} %concatenate.3.core, f32[8,2304]{1,0:T(8,128)S(1)} %get-tuple-element.59.keep, f32[8,2304]{1,0:T(8,128)S(1)} %collective-permute-done.14.received, f32[4,4608]{1,0:T(4,128)S(1)} %get-tuple-element.61.unit, ...), custom_call_target="tpu_custom_call" | custom-call | flops 1000 | bytes 1000 | tf_op jit(solution)/shard_map/pallas_call | solution.py:274
  (5 shorter events, 0.1 us)
Async XLA Ops:
  0.6 2.8 %collective-permute-start = (bf16[4,4608]{1,0:T(4,128)(2,1)}, bf16[4,4608]{1,0:T(4,128)(2,1)S(1)}, u32[]{:S(2)}, u32[]{:S(2)}) collective-permute-start(bf16[4,4608]{1,0:T(4,128)(2,1)} %mine.1), channel_id=1, source_target_pairs={{0,16},{1,17},{2,18},{3,19},{4,20},{5,21},{6,22},{7,23},{8,24},{9,... | collective-permute-start | bytes 110600 | tf_op jit(solution)/shard_map/ppermute | solution.py:41
  3.5 0.8 copy-start.2
  4.2 0.7 copy-start.3
  23.7 14.9 %collective-permute-start.4 = (bf16[128,2304]{1,0:T(8,128)(2,1)S(1)}, bf16[128,2304]{1,0:T(8,128)(2,1)S(1)}, u32[]{:S(2)}, u32[]{:S(2)}) collective-permute-start(bf16[128,2304]{1,0:T(8,128)(2,1)S(1)} %bitcast.6), channel_id=1, source_target_pairs={{0,32},{1,33},{2,34},{3,35},{4,36},{5,37},{6,38},{7,39},{8,40},{9,... | collective-permute-start | bytes 1769480 | tf_op jit(solution)/shard_map/ppermute | solution.py:48
  24.9 13.7 %collective-permute-start.3 = (bf16[128,2304]{1,0:T(8,128)(2,1)S(1)}, bf16[128,2304]{1,0:T(8,128)(2,1)S(1)}, u32[]{:S(2)}, u32[]{:S(2)}) collective-permute-start(bf16[128,2304]{1,0:T(8,128)(2,1)S(1)} %bitcast.7), channel_id=1, source_target_pairs={{0,96},{1,97},{2,98},{3,99},{4,100},{5,101},{6,102},{7,103},{8,104... | collective-permute-start | bytes 1769480 | tf_op jit(solution)/shard_map/ppermute | solution.py:48
  26.3 14.7 %collective-permute-start.2 = (bf16[128,2304]{1,0:T(8,128)(2,1)S(1)}, bf16[128,2304]{1,0:T(8,128)(2,1)S(1)}, u32[]{:S(2)}, u32[]{:S(2)}) collective-permute-start(bf16[128,2304]{1,0:T(8,128)(2,1)S(1)} %bitcast.8), channel_id=1, source_target_pairs={{0,64},{1,65},{2,66},{3,67},{4,68},{5,69},{6,70},{7,71},{8,72},{9,... | collective-permute-start | bytes 1769480 | tf_op jit(solution)/shard_map/ppermute | solution.py:48
  27.7 18.0 %collective-permute-start.1 = (bf16[128,2304]{1,0:T(8,128)(2,1)S(1)}, bf16[128,2304]{1,0:T(8,128)(2,1)S(1)}, u32[]{:S(2)}, u32[]{:S(2)}) collective-permute-start(bf16[128,2304]{1,0:T(8,128)(2,1)S(1)} %bitcast.9), channel_id=1, source_target_pairs={{0,16},{1,17},{2,18},{3,19},{4,20},{5,21},{6,22},{7,23},{8,24},{9,... | collective-permute-start | bytes 1769480 | tf_op jit(solution)/shard_map/ppermute | solution.py:41
  29.3 3.6 %copy-start = (bf16[1000,4608]{1,0:T(8,128)(2,1)S(1)}, bf16[1000,4608]{1,0:T(8,128)(2,1)}, u32[]{:S(2)}) copy-start(bf16[1000,4608]{1,0:T(8,128)(2,1)} %weight.7) | copy-start | bytes 27648004
  32.9 3.6 %copy-start.1 = (bf16[1000,4608]{1,0:T(8,128)(2,1)S(1)}, bf16[1000,4608]{1,0:T(8,128)(2,1)}, u32[]{:S(2)}) copy-start(bf16[1000,4608]{1,0:T(8,128)(2,1)} %weight.7) | copy-start | bytes 27648004
  41.0 4.7 %collective-permute-start.5 = (bf16[128,2304]{1,0:T(8,128)(2,1)S(1)}, bf16[128,2304]{1,0:T(8,128)(2,1)S(1)}, u32[]{:S(2)}, u32[]{:S(2)}) collective-permute-start(bf16[128,2304]{1,0:T(8,128)(2,1)S(1)} %collective-permute-done.3.refs_0_.n1), channel_id=1, source_target_pairs={{0,16},{1,17},{2,18},{3,19},{4,20},{5,21},{6,22},{7,23},{8,24},{9,... | collective-permute-start | bytes 1769480 | tf_op jit(solution)/shard_map/ppermute | solution.py:41
  42.6 3.1 %collective-permute-start.6 = (bf16[128,2304]{1,0:T(8,128)(2,1)S(1)}, bf16[128,2304]{1,0:T(8,128)(2,1)S(1)}, u32[]{:S(2)}, u32[]{:S(2)}) collective-permute-start(bf16[128,2304]{1,0:T(8,128)(2,1)S(1)} %collective-permute-done.2.refs_1_.n2), channel_id=1, source_target_pairs={{0,16},{1,17},{2,18},{3,19},{4,20},{5,21},{6,22},{7,23},{8,24},{9,... | collective-permute-start | bytes 1769480 | tf_op jit(solution)/shard_map/ppermute | solution.py:41
  42.6 3.3 %collective-permute-start.7 = (bf16[128,2304]{1,0:T(8,128)(2,1)S(1)}, bf16[128,2304]{1,0:T(8,128)(2,1)S(1)}, u32[]{:S(2)}, u32[]{:S(2)}) collective-permute-start(bf16[128,2304]{1,0:T(8,128)(2,1)S(1)} %collective-permute-done.4.refs_2_.n3), channel_id=1, source_target_pairs={{0,16},{1,17},{2,18},{3,19},{4,20},{5,21},{6,22},{7,23},{8,24},{9,... | collective-permute-start | bytes 1769480 | tf_op jit(solution)/shard_map/ppermute | solution.py:41
  50.6 3.9 %collective-permute-start.8 = (f32[8,128]{1,0:T(8,128)S(1)}, f32[8,128]{1,0:T(8,128)S(1)}, u32[]{:S(2)}, u32[]{:S(2)}) collective-permute-start(f32[8,128]{1,0:T(8,128)S(1)} %get-tuple-element.47), channel_id=1, source_target_pairs={{0,16},{1,17},{2,18},{3,19},{4,20},{5,21},{6,22},{7,23},{8,24},{9,... | collective-permute-start | bytes 12296 | tf_op jit(solution)/shard_map/ppermute | solution.py:41
  51.0 20.9 %collective-permute-start.10 = (bf16[512,2304]{1,0:T(8,128)(2,1)S(1)}, bf16[512,2304]{1,0:T(8,128)(2,1)S(1)}, u32[]{:S(2)}, u32[]{:S(2)}) collective-permute-start(bf16[512,2304]{1,0:T(8,128)(2,1)S(1)} %shard_map.76), channel_id=1, source_target_pairs={{0,16},{1,17},{2,18},{3,19},{4,20},{5,21},{6,22},{7,23},{8,24},{9,... | collective-permute-start | bytes 7077896 | tf_op jit(solution)/shard_map/ppermute | solution.py:41
  54.5 17.5 %collective-permute-start.9 = (bf16[512,2304]{1,0:T(8,128)(2,1)S(1)}, bf16[512,2304]{1,0:T(8,128)(2,1)S(1)}, u32[]{:S(2)}, u32[]{:S(2)}) collective-permute-start(bf16[512,2304]{1,0:T(8,128)(2,1)S(1)} %shard_map.80), channel_id=1, source_target_pairs={{0,16},{1,17},{2,18},{3,19},{4,20},{5,21},{6,22},{7,23},{8,24},{9,... | collective-permute-start | bytes 7077896 | tf_op jit(solution)/shard_map/ppermute | solution.py:41
  76.9 17.3 %collective-permute-start.11 = (bf16[128,2432]{1,0:T(8,128)(2,1)S(1)}, bf16[128,2432]{1,0:T(8,128)(2,1)S(1)}, u32[]{:S(2)}, u32[]{:S(2)}) collective-permute-start(bf16[128,2432]{1,0:T(8,128)(2,1)S(1)} %get-tuple-element.56), channel_id=1, source_target_pairs={{0,32},{1,33},{2,34},{3,35},{4,36},{5,37},{6,38},{7,39},{8,40},{9,... | collective-permute-start | bytes 1867784 | tf_op jit(solution)/shard_map/ppermute | solution.py:48
  77.2 17.0 %collective-permute-start.12 = (bf16[128,2432]{1,0:T(8,128)(2,1)S(1)}, bf16[128,2432]{1,0:T(8,128)(2,1)S(1)}, u32[]{:S(2)}, u32[]{:S(2)}) collective-permute-start(bf16[128,2432]{1,0:T(8,128)(2,1)S(1)} %get-tuple-element.57), channel_id=1, source_target_pairs={{0,96},{1,97},{2,98},{3,99},{4,100},{5,101},{6,102},{7,103},{8,104... | collective-permute-start | bytes 1867784 | tf_op jit(solution)/shard_map/ppermute | solution.py:48
  79.7 14.6 %collective-permute-start.13 = (bf16[128,2432]{1,0:T(8,128)(2,1)S(1)}, bf16[128,2432]{1,0:T(8,128)(2,1)S(1)}, u32[]{:S(2)}, u32[]{:S(2)}) collective-permute-start(bf16[128,2432]{1,0:T(8,128)(2,1)S(1)} %get-tuple-element.58), channel_id=1, source_target_pairs={{0,64},{1,65},{2,66},{3,67},{4,68},{5,69},{6,70},{7,71},{8,72},{9,... | collective-permute-start | bytes 1867784 | tf_op jit(solution)/shard_map/ppermute | solution.py:48
  108.6 4.6 %collective-permute-start.14 = (f32[8,2304]{1,0:T(8,128)S(1)}, f32[8,2304]{1,0:T(8,128)S(1)}, u32[]{:S(2)}, u32[]{:S(2)}) collective-permute-start(f32[8,2304]{1,0:T(8,128)S(1)} %get-tuple-element.60), channel_id=1, source_target_pairs={{0,16},{1,17},{2,18},{3,19},{4,20},{5,21},{6,22},{7,23},{8,24},{9,... | collective-permute-start | bytes 221192 | tf_op jit(solution)/shard_map/ppermute | solution.py:41

commit v5 on v4

--- a/solution.py
+++ b/solution.py
@@ -104,11 +104,20 @@
     return jnp.concatenate(rows, axis=0)
 
 
-def far_target_kernel(core, weight, labels, out):
+def first_logits_kernel(core, weight, targets, b0, out, labels, part):
+    to = lax.broadcasted_iota(jnp.int32, (128, 128), 1)
+    source = ((to >> 2) & 1) * 64 + (to >> 3) * 4 + (to & 3)
+    order = (lax.broadcasted_iota(jnp.int32, (128, 128), 0) == source).astype(f32)
+    ids = jnp.concatenate([targets[...].astype(f32), jnp.zeros((4, 128), f32)], axis=0)
+    ids = jnp.dot(ids, order, precision=lax.Precision.HIGHEST, preferred_element_type=f32)
+    labels[...] = ids[:4].astype(jnp.int32) - core[3 + 2 * chunks]
     onehot = onehot_rows(labels, weight.shape[0])
     out[...] = jnp.dot(
         onehot, half_of(weight, 1 - core[0]), preferred_element_type=f32
     ).astype(bf16)
+    part[...] = lax.dot_general(
+        b0[...], half_of(weight, core[0]), (((1,), (1,)), ((), ())), preferred_element_type=f32
+    )
 
 
 def near_logits_kernel(core, *refs):
@@ -156,8 +165,7 @@
 
 
 def far_grad_kernel(core, others, weight, out):
-    grad = jnp.dot(others[...], half_of(weight, 1 - core[0]), preferred_element_type=f32)
-    out[...] = grad.astype(bf16)
+    out[...] = jnp.dot(others[...], half_of(weight, 1 - core[0]), preferred_element_type=f32)
 
 
 def combine_kernel(
@@ -189,7 +197,7 @@
             for k in range(4):
                 at = pl.ds(pl.multiple_of(core[1 + 4 * d + k] * chunk, chunk), chunk)
                 rows = slice(chunk * k, chunk * (k + 1))
-                value = held[j, at, :] + received[at, lanes].astype(f32) * inverse[at, :]
+                value = held[j, at, :] + received[at, lanes] * inverse[at, :]
                 value += target[at, lanes].astype(f32) * factor[at, :]
                 out[rows, lanes] = value.astype(bf16)
                 value = value * normed[rows, lanes].astype(f32)
@@ -305,11 +313,11 @@
             jnp.where(first, by_y, by_x).reshape(chunks),
             (token // 128)[None],
             ((128 - token % 128) % 128)[None],
+            (device * vocab)[None],
         ]
     )
     gain = norm_gain
 
-    labels = targets.reshape(4, 2, 16, 4).transpose(0, 2, 1, 3).reshape(4, 128) - device * vocab
     spread, unit, root, gain = call(
         norm_kernel,
         core,
@@ -321,31 +329,28 @@
             shape((1, width), f32),
         ],
     )
-    spread, labels = lax.optimization_barrier((spread, labels))
     near = over_plane(spread).reshape(block, half)
     sent = {d: along_line(near, -d) for d in (2, 1, 3)}
     near = [near, sent[1], sent[2], sent[3]]
-    local, late = lax.optimization_barrier((near[0], labels))
-    target = call(far_target_kernel, core, (weight, late), shape((tokens, half), bf16))
-    local, target = lax.optimization_barrier((local, target))
+    target, labels, part = call(
+        first_logits_kernel,
+        core,
+        (weight, targets.reshape(4, 128), near[0]),
+        [shape((tokens, half), bf16), shape((4, 128), jnp.int32), shape((block, vocab), f32)],
+    )
+    far = [other_core(near[0])]
+    part, near[2], near[1], near[3] = lax.optimization_barrier((part, near[2], near[1], near[3]))
     target = other_core(target)
-    parts = []
-    far = [None] * 4
-    for group in ((0,), (1, 2, 3)):
-        for d in (0,) if group == (0,) else (2, 1, 3):
-            far[d] = other_core(near[d])
-        part = call(
-            near_logits_kernel,
-            core,
-            (*(near[d] if d else local for d in group), weight),
-            shape((len(group) * block, vocab), f32),
-            [pltpu.VMEM((len(group) * block, half), bf16)],
-        )
-        if group[0] == 0:
-            part, near[2], near[1], near[3] = lax.optimization_barrier(
-                (part, near[2], near[1], near[3])
-            )
-        parts.append(part)
+    sent = {d: other_core(near[d]) for d in (2, 1, 3)}
+    far += [sent[1], sent[2], sent[3]]
+    late_part = call(
+        near_logits_kernel,
+        core,
+        (*near[1:], weight),
+        shape((3 * block, vocab), f32),
+        [pltpu.VMEM((3 * block, half), bf16)],
+    )
+    parts = [part, late_part]
     rest, stats, others = call(
         logits_kernel,
         core,
@@ -354,7 +359,7 @@
         [pltpu.VMEM((tokens, half), bf16)],
     )
     stats = stats + other_core(stats)
-    far_grad = call(far_grad_kernel, core, (others, weight), shape((tokens, half), bf16))
+    far_grad = call(far_grad_kernel, core, (others, weight), shape((tokens, half), f32))
     stats, far_grad = lax.optimization_barrier((stats, far_grad))
     received = other_core(far_grad)
     stats = jnp.broadcast_to(stats[None], (n_chips, 8, 128))

time: 115 us -> 115 us (level)
    unnamed x8 -> x14, local copies, waits for them, and re-layouts: 5.24 us -> 5.8 us
    pallas_call x11 -> x10, Pallas kernels: 33.2 us -> 32.9 us  [call(): pl.pallas_call(kernel, grid_spec=pltpu.PrefetchScalarGridSpec(num_scalar_...]
  transfers between devices with their start and end apart: 15 -> 15, of which waited for: 4 -> 5; matrix products, arithmetic and copies ran while one was open for 1% -> 0% of each run, Pallas kernels for 17% -> 17%
where the time goes in v5:
time: 115 us
  blocking collectives  47.9 us (42%)
  Pallas kernels  32.9 us (29%)
  starting transfers between devices  17.4 us (15%)
  waiting for transfers between devices  9.51 us (8%)
  local copies, waits for them, and re-layouts  6.07 us (5%)
    pallas_call x10, Pallas kernels, call(): pl.pallas_call(kernel, grid_spec=pltpu.PrefetchScalarGridSpec(num_scalar_...  32.9 us
    all_to_all x2, blocking collectives, over_plane(): lax.all_to_all(array, every, 0, 0, axis_index_groups=planes, tiled=True)  30.8 us
    all_to_all x1, blocking collectives, body(): stats = lax.all_to_all(stats, chips, 0, 0, tiled=True)  17.1 us
    ppermute x9, starting transfers between devices, other_core(): return lax.ppermute(array, every, swap_cores)  10.4 us
    ppermute x6, waiting for transfers between devices, along_line(): return lax.ppermute(array, every, pairs)  7.64 us
    ppermute x6, starting transfers between devices, along_line(): return lax.ppermute(array, every, pairs)  7.05 us
    unnamed x14, local copies, waits for them, and re-layouts  5.8 us
  transfers between devices with their start and end apart: 15, of which 5 were waited for; matrix products, arithmetic and copies ran while one was open for 0% of the time, Pallas kernels for 17%

profile of v5, /device:TPU:1, one launch (start us, length us, event | category | flops | bytes accessed | tf_op | source)
XLA Modules:
  0.0 114.7 jit_solution(7159054384350163198)
XLA Ops:
  0.6 1.5 %collective-permute-start = (bf16[4,4608]{1,0:T(4,128)(2,1)}, bf16[4,4608]{1,0:T(4,128)(2,1)S(1)}, u32[]{:S(2)}, u32[]{:S(2)}) collective-permute-start(bf16[4,4608]{1,0:T(4,128)(2,1)} %mine.1), channel_id=1, source_target_pairs={{0,16},{1,17},{2,18},{3,19},{4,20},{5,21},{6,22},{7,23},{8,24},{9,... | collective-permute-start | bytes 110600 | tf_op jit(solution)/shard_map/ppermute | solution.py:41
  2.2 0.1 add_select_fusion
  2.2 0.1 select_n.57
  2.3 0.1 select_n.59
  2.4 0.1 concatenate.3.core
  2.5 0.7 collective-permute-done.theirs
  3.2 0.0 copy-start.1
  3.2 0.8 copy-done.1
  4.0 0.0 copy-start.2
  4.0 0.7 copy-done.2
  4.7 0.7 shard_map.75
  5.5 17.9 %all_to_all.15 = bf16[16,8,2304]{2,1,0:T(8,128)(2,1)S(1)} all-to-all(bf16[16,8,2304]{2,1,0:T(8,128)(2,1)S(1)} %get-tuple-element.33), channel_id=1, replica_groups={{0,1,2,3,4,5,6,7,8,9,10,11,12,13,14,15},{32,33,34,35,36,37,38,39,40,41,..., dimensions={0} | all-to-all | bytes 1179648 | tf_op jit(solution)/shard_map/all_to_all | solution.py:52
  23.4 2.8 %collective-permute-start.2 = (bf16[128,2304]{1,0:T(8,128)(2,1)S(1)}, bf16[128,2304]{1,0:T(8,128)(2,1)S(1)}, u32[]{:S(2)}, u32[]{:S(2)}) collective-permute-start(bf16[128,2304]{1,0:T(8,128)(2,1)S(1)} %bitcast.9), channel_id=1, source_target_pairs={{0,64},{1,65},{2,66},{3,67},{4,68},{5,69},{6,70},{7,71},{8,72},{9,... | collective-permute-start | bytes 1769480 | tf_op jit(solution)/shard_map/ppermute | solution.py:48
  26.2 0.9 collective-permute-start.3
  27.1 0.6 collective-permute-start.4
  27.7 1.6 %collective-permute-start.1 = (bf16[128,2304]{1,0:T(8,128)(2,1)S(1)}, bf16[128,2304]{1,0:T(8,128)(2,1)S(1)}, u32[]{:S(2)}, u32[]{:S(2)}) collective-permute-start(bf16[128,2304]{1,0:T(8,128)(2,1)S(1)} %bitcast.12), channel_id=1, source_target_pairs={{0,16},{1,17},{2,18},{3,19},{4,20},{5,21},{6,22},{7,23},{8,24},{9,... | collective-permute-start | bytes 1769480 | tf_op jit(solution)/shard_map/ppermute | solution.py:41
  29.3 0.0 copy-start
  29.3 3.6 %copy-done = bf16[1000,4608]{1,0:T(8,128)(2,1)S(1)} copy-done((bf16[1000,4608]{1,0:T(8,128)(2,1)S(1)}, bf16[1000,4608]{1,0:T(8,128)(2,1)}, u32[]{:S(2)}) %copy-start) | copy-done | bytes 9216024
  32.9 0.0 copy-start.3
  32.9 0.7 copy-done.3
  33.6 5.1 %shard_map.76 = (bf16[512,2304]{1,0:T(8,128)(2,1)S(1)}, s32[4,128]{1,0:T(4,128)S(1)}, f32[128,1000]{1,0:T(8,128)S(1)}) custom-call(s32[36]{0:T(128)S(1)} %concatenate.3.core, bf16[1000,4608]{1,0:T(8,128)(2,1)S(1)} %copy-done, s32[4,128]{1,0:T(4,128)S(1)} %bitcast.17, bf16[128,2304]{1,0:T(8,128)(2,1)S(1)} %bitcast.13), custom_call_target="tpu_custom_call" | custom-call | flops 1000 | bytes 1000 | tf_op jit(solution)/shard_map/pallas_call | solution.py:282
  38.7 0.0 collective-permute-done.2.refs_1_.n2
  38.7 1.8 %collective-permute-done.3.refs_0_.n1 = bf16[128,2304]{1,0:T(8,128)(2,1)S(1)} collective-permute-done((bf16[128,2304]{1,0:T(8,128)(2,1)S(1)}, bf16[128,2304]{1,0:T(8,128)(2,1)S(1)}, u32[]{:S(2)}, u32[]{:S(2)}) %collective-permute-start.3) | collective-permute-done | bytes 589856 | tf_op jit(solution)/shard_map/ppermute | solution.py:48
  40.5 0.0 collective-permute-done.4.refs_2_.n3
  40.5 2.0 %collective-permute-start.5 = (bf16[128,2304]{1,0:T(8,128)(2,1)S(1)}, bf16[128,2304]{1,0:T(8,128)(2,1)S(1)}, u32[]{:S(2)}, u32[]{:S(2)}) collective-permute-start(bf16[128,2304]{1,0:T(8,128)(2,1)S(1)} %collective-permute-done.3.refs_0_.n1), channel_id=1, source_target_pairs={{0,16},{1,17},{2,18},{3,19},{4,20},{5,21},{6,22},{7,23},{8,24},{9,... | collective-permute-start | bytes 1769480 | tf_op jit(solution)/shard_map/ppermute | solution.py:41
  42.5 0.0 collective-permute-start.6
  42.5 0.5 collective-permute-start.7
  43.0 2.6 %shard_map.77.part1 = f32[384,1000]{1,0:T(8,128)S(1)} custom-call(s32[36]{0:T(128)S(1)} %concatenate.3.core, bf16[128,2304]{1,0:T(8,128)(2,1)S(1)} %collective-permute-done.3.refs_0_.n1, bf16[128,2304]{1,0:T(8,128)(2,1)S(1)} %collective-permute-done.2.refs_1_.n2, bf16[128,2304]{1,0:T(8,128)(2,1)S(1)} %collective-permute-done.4.refs_2_.n3, ...), custom_call_target="tpu_custom_call" | custom-call | flops 1000 | bytes 1000 | tf_op jit(solution)/shard_map/pallas_call | solution.py:282
  45.6 0.0 collective-permute-done.1.b0.m0
  45.6 0.0 collective-permute-done.5.b1.m1
  45.6 0.0 collective-permute-done.6.b2.m2
  45.6 0.2 collective-permute-done.7.b3.m3
  45.8 0.0 slice-start
  45.8 0.0 slice-start.1
  45.8 4.7 %shard_map.78 = (f32[512,1000]{1,0:T(8,128)S(1)}, f32[8,128]{1,0:T(8,128)S(1)}, bf16[512,1000]{1,0:T(8,128)(2,1)S(1)}) custom-call(s32[36]{0:T(128)S(1)} %concatenate.3.core, bf16[128,2304]{1,0:T(8,128)(2,1)S(1)} %collective-permute-done.1.b0.m0, bf16[128,2304]{1,0:T(8,128)(2,1)S(1)} %collective-permute-done.5.b1.m1, ...), custom_call_target="tpu_custom_call" | custom-call | flops 1000 | bytes 1000 | tf_op jit(solution)/shard_map/pallas_call | solution.py:282
  50.5 0.6 collective-permute-start.8
  51.1 0.0 slice-start.2
  51.1 3.2 %shard_map.79 = f32[512,2304]{1,0:T(8,128)S(1)} custom-call(s32[36]{0:T(128)S(1)} %concatenate.3.core, bf16[512,1000]{1,0:T(8,128)(2,1)S(1)} %get-tuple-element.42.others, bf16[1000,4608]{1,0:T(8,128)(2,1)S(1)} %copy-done), custom_call_target="tpu_custom_call" | custom-call | flops 1000 | bytes 1000 | tf_op jit(solution)/shard_map/pallas_call | solution.py:282
  54.3 0.0 collective-permute-done.8
  54.3 0.2 collective-permute-start.9
  54.5 0.4 collective-permute-start.10
  54.9 17.1 %all_to_all.16.stats = f32[64,8,128]{2,1,0:T(8,128)S(1)} all-to-all(f32[64,8,128]{2,1,0:T(8,128)S(1)} %broadcast_in_dim.26), channel_id=1, replica_groups=mesh['x'=4,'c'=2,'y'=4,'z'=4] {'x','y','z'}, dimensions={0} | all-to-all | bytes 524288 | tf_op jit(solution)/shard_map/all_to_all | solution.py:366
  72.0 0.0 collective-permute-done.10.target
  72.0 0.0 collective-permute-done.9.received
  72.0 0.0 slice-done
  72.0 0.0 slice-done.1
  72.0 0.0 slice-done.2
  72.0 5.1 %shard_map.80 = (bf16[128,2432]{1,0:T(8,128)(2,1)S(1)}, bf16[128,2432]{1,0:T(8,128)(2,1)S(1)}, bf16[128,2432]{1,0:T(8,128)(2,1)S(1)}, bf16[128,2432]{1,0:T(8,128...) custom-call(s32[36]{0:T(128)S(1)} %concatenate.3.core, f32[512,1000]{1,0:T(8,128)S(1)} %get-tuple-element.40.others, ...), custom_call_target="tpu_custom_call" | custom-call | flops 1000 | bytes 1000 | tf_op jit(solution)/shard_map/pallas_call | solution.py:282
  77.1 0.4 collective-permute-start.11
  77.5 2.4 %collective-permute-start.12 = (bf16[128,2432]{1,0:T(8,128)(2,1)S(1)}, bf16[128,2432]{1,0:T(8,128)(2,1)S(1)}, u32[]{:S(2)}, u32[]{:S(2)}) collective-permute-start(bf16[128,2432]{1,0:T(8,128)(2,1)S(1)} %get-tuple-element.51), channel_id=1, source_target_pairs={{0,96},{1,97},{2,98},{3,99},{4,100},{5,101},{6,102},{7,103},{8,104... | collective-permute-start | bytes 1867784 | tf_op jit(solution)/shard_map/ppermute | solution.py:48
  79.9 0.0 collective-permute-start.13
  79.9 8.7 %shard_map.81 = bf16[1000,4608]{1,0:T(8,128)(2,1)} custom-call(s32[36]{0:T(128)S(1)} %concatenate.3.core, f32[512,1000]{1,0:T(8,128)S(1)} %get-tuple-element.40.others, f32[8,128]{1,0:T(8,128)S(1)} %get-tuple-element.47.marks, s32[4,128]{1,0:T(4,128)S(1)} %get-tuple-element.39.labels, bf16[128,2304]{1,0:T(8,128)(2,1)S(1)} %bitcast.15, ...), custom_call_target="tpu_custom_call" | custom-call | flops 1000 | bytes 1000 | tf_op jit(solution)/shard_map/pallas_call | solution.py:282
  88.6 5.8 %collective-permute-done.11.b1 = bf16[128,2432]{1,0:T(8,128)(2,1)S(1)} collective-permute-done((bf16[128,2432]{1,0:T(8,128)(2,1)S(1)}, bf16[128,2432]{1,0:T(8,128)(2,1)S(1)}, u32[]{:S(2)}, u32[]{:S(2)}) %collective-permute-start.11) | collective-permute-done | bytes 622624 | tf_op jit(solution)/shard_map/ppermute | solution.py:48
  94.5 0.0 collective-permute-done.12.b2
  94.5 0.0 collective-permute-done.13.b3
  94.5 0.9 shard_map.82
  95.3 12.9 %all_to_all.17.blocks = bf16[16,8,2688]{2,1,0:T(8,128)(2,1)S(1)} all-to-all(bf16[16,8,2688]{2,1,0:T(8,128)(2,1)S(1)} %bitcast.16), channel_id=1, replica_groups={{0,1,2,3,4,5,6,7,8,9,10,11,12,13,14,15},{32,33,34,35,36,37,38,39,40,41,..., dimensions={0} | all-to-all | bytes 1376256 | tf_op jit(solution)/shard_map/all_to_all | solution.py:52
  108.2 0.6 shard_map.83
  108.9 3.6 %collective-permute-start.14 = (f32[8,2304]{1,0:T(8,128)S(1)}, f32[8,2304]{1,0:T(8,128)S(1)}, u32[]{:S(2)}, u32[]{:S(2)}) collective-permute-start(f32[8,2304]{1,0:T(8,128)S(1)} %get-tuple-element.54), channel_id=1, source_target_pairs={{0,16},{1,17},{2,18},{3,19},{4,20},{5,21},{6,22},{7,23},{8,24},{9,... | collective-permute-start | bytes 221192 | tf_op jit(solution)/shard_map/ppermute | solution.py:41
  112.4 0.9 collective-permute-done.14.received
  113.4 1.3 %shard_map.84 = (f32[4]{0:T(128)}, f32[4,4608]{1,0:T(4,128)}, f32[4608]{0:T(1024)}) custom-call(s32[36]{0:T(128)S(1)} %concatenate.3.core, f32[8,2304]{1,0:T(8,128)S(1)} %get-tuple-element.53.keep, f32[8,2304]{1,0:T(8,128)S(1)} %collective-permute-done.14.received, f32[4,4608]{1,0:T(4,128)S(1)} %get-tuple-element.55.unit, ...), custom_call_target="tpu_custom_call" | custom-call | flops 1000 | bytes 1000 | tf_op jit(solution)/shard_map/pallas_call | solution.py:282
  (5 shorter events, 0.0 us)
Async XLA Ops:
  0.6 2.6 %collective-permute-start = (bf16[4,4608]{1,0:T(4,128)(2,1)}, bf16[4,4608]{1,0:T(4,128)(2,1)S(1)}, u32[]{:S(2)}, u32[]{:S(2)}) collective-permute-start(bf16[4,4608]{1,0:T(4,128)(2,1)} %mine.1), channel_id=1, source_target_pairs={{0,16},{1,17},{2,18},{3,19},{4,20},{5,21},{6,22},{7,23},{8,24},{9,... | collective-permute-start | bytes 110600 | tf_op jit(solution)/shard_map/ppermute | solution.py:41
  3.2 0.8 copy-start.1
  4.0 0.7 copy-start.2
  23.4 15.3 %collective-permute-start.2 = (bf16[128,2304]{1,0:T(8,128)(2,1)S(1)}, bf16[128,2304]{1,0:T(8,128)(2,1)S(1)}, u32[]{:S(2)}, u32[]{:S(2)}) collective-permute-start(bf16[128,2304]{1,0:T(8,128)(2,1)S(1)} %bitcast.9), channel_id=1, source_target_pairs={{0,64},{1,65},{2,66},{3,67},{4,68},{5,69},{6,70},{7,71},{8,72},{9,... | collective-permute-start | bytes 1769480 | tf_op jit(solution)/shard_map/ppermute | solution.py:48
  26.2 14.2 %collective-permute-start.3 = (bf16[128,2304]{1,0:T(8,128)(2,1)S(1)}, bf16[128,2304]{1,0:T(8,128)(2,1)S(1)}, u32[]{:S(2)}, u32[]{:S(2)}) collective-permute-start(bf16[128,2304]{1,0:T(8,128)(2,1)S(1)} %bitcast.10), channel_id=1, source_target_pairs={{0,96},{1,97},{2,98},{3,99},{4,100},{5,101},{6,102},{7,103},{8,104... | collective-permute-start | bytes 1769480 | tf_op jit(solution)/shard_map/ppermute | solution.py:48
  27.1 13.4 %collective-permute-start.4 = (bf16[128,2304]{1,0:T(8,128)(2,1)S(1)}, bf16[128,2304]{1,0:T(8,128)(2,1)S(1)}, u32[]{:S(2)}, u32[]{:S(2)}) collective-permute-start(bf16[128,2304]{1,0:T(8,128)(2,1)S(1)} %bitcast.11), channel_id=1, source_target_pairs={{0,32},{1,33},{2,34},{3,35},{4,36},{5,37},{6,38},{7,39},{8,40},{9,... | collective-permute-start | bytes 1769480 | tf_op jit(solution)/shard_map/ppermute | solution.py:48
  27.7 17.9 %collective-permute-start.1 = (bf16[128,2304]{1,0:T(8,128)(2,1)S(1)}, bf16[128,2304]{1,0:T(8,128)(2,1)S(1)}, u32[]{:S(2)}, u32[]{:S(2)}) collective-permute-start(bf16[128,2304]{1,0:T(8,128)(2,1)S(1)} %bitcast.12), channel_id=1, source_target_pairs={{0,16},{1,17},{2,18},{3,19},{4,20},{5,21},{6,22},{7,23},{8,24},{9,... | collective-permute-start | bytes 1769480 | tf_op jit(solution)/shard_map/ppermute | solution.py:41
  29.3 3.6 %copy-start = (bf16[1000,4608]{1,0:T(8,128)(2,1)S(1)}, bf16[1000,4608]{1,0:T(8,128)(2,1)}, u32[]{:S(2)}) copy-start(bf16[1000,4608]{1,0:T(8,128)(2,1)} %weight.7) | copy-start | bytes 27648004
  32.9 0.7 copy-start.3
  40.5 5.1 %collective-permute-start.5 = (bf16[128,2304]{1,0:T(8,128)(2,1)S(1)}, bf16[128,2304]{1,0:T(8,128)(2,1)S(1)}, u32[]{:S(2)}, u32[]{:S(2)}) collective-permute-start(bf16[128,2304]{1,0:T(8,128)(2,1)S(1)} %collective-permute-done.3.refs_0_.n1), channel_id=1, source_target_pairs={{0,16},{1,17},{2,18},{3,19},{4,20},{5,21},{6,22},{7,23},{8,24},{9,... | collective-permute-start | bytes 1769480 | tf_op jit(solution)/shard_map/ppermute | solution.py:41
  42.5 3.1 %collective-permute-start.6 = (bf16[128,2304]{1,0:T(8,128)(2,1)S(1)}, bf16[128,2304]{1,0:T(8,128)(2,1)S(1)}, u32[]{:S(2)}, u32[]{:S(2)}) collective-permute-start(bf16[128,2304]{1,0:T(8,128)(2,1)S(1)} %collective-permute-done.2.refs_1_.n2), channel_id=1, source_target_pairs={{0,16},{1,17},{2,18},{3,19},{4,20},{5,21},{6,22},{7,23},{8,24},{9,... | collective-permute-start | bytes 1769480 | tf_op jit(solution)/shard_map/ppermute | solution.py:41
  42.5 3.3 %collective-permute-start.7 = (bf16[128,2304]{1,0:T(8,128)(2,1)S(1)}, bf16[128,2304]{1,0:T(8,128)(2,1)S(1)}, u32[]{:S(2)}, u32[]{:S(2)}) collective-permute-start(bf16[128,2304]{1,0:T(8,128)(2,1)S(1)} %collective-permute-done.4.refs_2_.n3), channel_id=1, source_target_pairs={{0,16},{1,17},{2,18},{3,19},{4,20},{5,21},{6,22},{7,23},{8,24},{9,... | collective-permute-start | bytes 1769480 | tf_op jit(solution)/shard_map/ppermute | solution.py:41
  45.8 26.2 %slice-start = ((s8[9216000]{0:T(1024)(128)(4,1)}), s8[4194304]{0:T(1024)(128)(4,1)S(1)}, s32[]{:S(2)}) async-start(s8[9216000]{0:T(1024)(128)(4,1)} %bitcast.7), calls=%async_computation.3 | async-start | bytes 8388608
  45.8 26.2 %slice-start.1 = ((s8[9216000]{0:T(1024)(128)(4,1)}), s8[4194304]{0:T(1024)(128)(4,1)S(1)}, s32[]{:S(2)}) async-start(s8[9216000]{0:T(1024)(128)(4,1)} %bitcast.7), calls=%async_computation.4 | async-start | bytes 8388608
  50.5 3.8 %collective-permute-start.8 = (f32[8,128]{1,0:T(8,128)S(1)}, f32[8,128]{1,0:T(8,128)S(1)}, u32[]{:S(2)}, u32[]{:S(2)}) collective-permute-start(f32[8,128]{1,0:T(8,128)S(1)} %get-tuple-element.41), channel_id=1, source_target_pairs={{0,16},{1,17},{2,18},{3,19},{4,20},{5,21},{6,22},{7,23},{8,24},{9,... | collective-permute-start | bytes 12296 | tf_op jit(solution)/shard_map/ppermute | solution.py:41
  51.1 20.9 %slice-start.2 = ((s8[9216000]{0:T(1024)(128)(4,1)}), s8[827392]{0:T(1024)(128)(4,1)S(1)}, s32[]{:S(2)}) async-start(s8[9216000]{0:T(1024)(128)(4,1)} %bitcast.7), calls=%async_computation.5 | async-start | bytes 1654784
  54.3 17.7 %collective-permute-start.9 = (f32[512,2304]{1,0:T(8,128)S(1)}, f32[512,2304]{1,0:T(8,128)S(1)}, u32[]{:S(2)}, u32[]{:S(2)}) collective-permute-start(f32[512,2304]{1,0:T(8,128)S(1)} %shard_map.79), channel_id=1, source_target_pairs={{0,16},{1,17},{2,18},{3,19},{4,20},{5,21},{6,22},{7,23},{8,24},{9,... | collective-permute-start | bytes 14155784 | tf_op jit(solution)/shard_map/ppermute | solution.py:41
  54.5 17.5 %collective-permute-start.10 = (bf16[512,2304]{1,0:T(8,128)(2,1)S(1)}, bf16[512,2304]{1,0:T(8,128)(2,1)S(1)}, u32[]{:S(2)}, u32[]{:S(2)}) collective-permute-start(bf16[512,2304]{1,0:T(8,128)(2,1)S(1)} %get-tuple-element.45), channel_id=1, source_target_pairs={{0,16},{1,17},{2,18},{3,19},{4,20},{5,21},{6,22},{7,23},{8,24},{9,... | collective-permute-start | bytes 7077896 | tf_op jit(solution)/shard_map/ppermute | solution.py:41
  77.1 17.3 %collective-permute-start.11 = (bf16[128,2432]{1,0:T(8,128)(2,1)S(1)}, bf16[128,2432]{1,0:T(8,128)(2,1)S(1)}, u32[]{:S(2)}, u32[]{:S(2)}) collective-permute-start(bf16[128,2432]{1,0:T(8,128)(2,1)S(1)} %get-tuple-element.50), channel_id=1, source_target_pairs={{0,32},{1,33},{2,34},{3,35},{4,36},{5,37},{6,38},{7,39},{8,40},{9,... | collective-permute-start | bytes 1867784 | tf_op jit(solution)/shard_map/ppermute | solution.py:48
  77.5 16.9 %collective-permute-start.12 = (bf16[128,2432]{1,0:T(8,128)(2,1)S(1)}, bf16[128,2432]{1,0:T(8,128)(2,1)S(1)}, u32[]{:S(2)}, u32[]{:S(2)}) collective-permute-start(bf16[128,2432]{1,0:T(8,128)(2,1)S(1)} %get-tuple-element.51), channel_id=1, source_target_pairs={{0,96},{1,97},{2,98},{3,99},{4,100},{5,101},{6,102},{7,103},{8,104... | collective-permute-start | bytes 1867784 | tf_op jit(solution)/shard_map/ppermute | solution.py:48
  79.9 14.6 %collective-permute-start.13 = (bf16[128,2432]{1,0:T(8,128)(2,1)S(1)}, bf16[128,2432]{1,0:T(8,128)(2,1)S(1)}, u32[]{:S(2)}, u32[]{:S(2)}) collective-permute-start(bf16[128,2432]{1,0:T(8,128)(2,1)S(1)} %get-tuple-element.52), channel_id=1, source_target_pairs={{0,64},{1,65},{2,66},{3,67},{4,68},{5,69},{6,70},{7,71},{8,72},{9,... | collective-permute-start | bytes 1867784 | tf_op jit(solution)/shard_map/ppermute | solution.py:48
  108.9 4.5 %collective-permute-start.14 = (f32[8,2304]{1,0:T(8,128)S(1)}, f32[8,2304]{1,0:T(8,128)S(1)}, u32[]{:S(2)}, u32[]{:S(2)}) collective-permute-start(f32[8,2304]{1,0:T(8,128)S(1)} %get-tuple-element.54), channel_id=1, source_target_pairs={{0,16},{1,17},{2,18},{3,19},{4,20},{5,21},{6,22},{7,23},{8,24},{9,... | collective-permute-start | bytes 221192 | tf_op jit(solution)/shard_map/ppermute | solution.py:41

commit v6 on v5

--- a/solution.py
+++ b/solution.py
@@ -330,7 +330,7 @@
         ],
     )
     near = over_plane(spread).reshape(block, half)
-    sent = {d: along_line(near, -d) for d in (2, 1, 3)}
+    sent = {d: along_line(near, -d) for d in (3, 1, 2)}
     near = [near, sent[1], sent[2], sent[3]]
     target, labels, part = call(
         first_logits_kernel,

time: 115 us -> 115 us (level)
  no operation moved by 1% of the time
where the time goes in v6:
time: 115 us
  blocking collectives  47.9 us (42%)
  Pallas kernels  32.9 us (29%)
  starting transfers between devices  17.4 us (15%)
  waiting for transfers between devices  9.51 us (8%)
  local copies, waits for them, and re-layouts  6.07 us (5%)
    pallas_call x10, Pallas kernels, call(): pl.pallas_call(kernel, grid_spec=pltpu.PrefetchScalarGridSpec(num_scalar_...  32.9 us
    all_to_all x2, blocking collectives, over_plane(): lax.all_to_all(array, every, 0, 0, axis_index_groups=planes, tiled=True)  30.8 us
    all_to_all x1, blocking collectives, body(): stats = lax.all_to_all(stats, chips, 0, 0, tiled=True)  17.1 us
    ppermute x9, starting transfers between devices, other_core(): return lax.ppermute(array, every, swap_cores)  10.4 us
    ppermute x6, waiting for transfers between devices, along_line(): return lax.ppermute(array, every, pairs)  7.64 us
    ppermute x6, starting transfers between devices, along_line(): return lax.ppermute(array, every, pairs)  7.05 us
    unnamed x14, local copies, waits for them, and re-layouts  5.8 us
  transfers between devices with their start and end apart: 15, of which 5 were waited for; matrix products, arithmetic and copies ran while one was open for 0% of the time, Pallas kernels for 17%

profile of v6, /device:TPU:1, one launch (start us, length us, event | category | flops | bytes accessed | tf_op | source)
XLA Modules:
  0.0 114.7 jit_solution(7159054384350163198)
XLA Ops:
  0.6 1.5 %collective-permute-start = (bf16[4,4608]{1,0:T(4,128)(2,1)}, bf16[4,4608]{1,0:T(4,128)(2,1)S(1)}, u32[]{:S(2)}, u32[]{:S(2)}) collective-permute-start(bf16[4,4608]{1,0:T(4,128)(2,1)} %mine.1), channel_id=1, source_target_pairs={{0,16},{1,17},{2,18},{3,19},{4,20},{5,21},{6,22},{7,23},{8,24},{9,... | collective-permute-start | bytes 110600 | tf_op jit(solution)/shard_map/ppermute | solution.py:41
  2.2 0.1 add_select_fusion
  2.2 0.1 select_n.57
  2.3 0.1 select_n.59
  2.4 0.1 concatenate.3.core
  2.5 0.7 collective-permute-done.theirs
  3.2 0.0 copy-start.1
  3.2 0.8 copy-done.1
  4.0 0.0 copy-start.2
  4.0 0.7 copy-done.2
  4.7 0.7 shard_map.75
  5.5 17.9 %all_to_all.15 = bf16[16,8,2304]{2,1,0:T(8,128)(2,1)S(1)} all-to-all(bf16[16,8,2304]{2,1,0:T(8,128)(2,1)S(1)} %get-tuple-element.33), channel_id=1, replica_groups={{0,1,2,3,4,5,6,7,8,9,10,11,12,13,14,15},{32,33,34,35,36,37,38,39,40,41,..., dimensions={0} | all-to-all | bytes 1179648 | tf_op jit(solution)/shard_map/all_to_all | solution.py:52
  23.4 2.8 %collective-permute-start.2 = (bf16[128,2304]{1,0:T(8,128)(2,1)S(1)}, bf16[128,2304]{1,0:T(8,128)(2,1)S(1)}, u32[]{:S(2)}, u32[]{:S(2)}) collective-permute-start(bf16[128,2304]{1,0:T(8,128)(2,1)S(1)} %bitcast.9), channel_id=1, source_target_pairs={{0,64},{1,65},{2,66},{3,67},{4,68},{5,69},{6,70},{7,71},{8,72},{9,... | collective-permute-start | bytes 1769480 | tf_op jit(solution)/shard_map/ppermute | solution.py:48
  26.2 0.9 collective-permute-start.3
  27.1 0.6 collective-permute-start.4
  27.7 1.6 %collective-permute-start.1 = (bf16[128,2304]{1,0:T(8,128)(2,1)S(1)}, bf16[128,2304]{1,0:T(8,128)(2,1)S(1)}, u32[]{:S(2)}, u32[]{:S(2)}) collective-permute-start(bf16[128,2304]{1,0:T(8,128)(2,1)S(1)} %bitcast.12), channel_id=1, source_target_pairs={{0,16},{1,17},{2,18},{3,19},{4,20},{5,21},{6,22},{7,23},{8,24},{9,... | collective-permute-start | bytes 1769480 | tf_op jit(solution)/shard_map/ppermute | solution.py:41
  29.3 0.0 copy-start
  29.3 3.6 %copy-done = bf16[1000,4608]{1,0:T(8,128)(2,1)S(1)} copy-done((bf16[1000,4608]{1,0:T(8,128)(2,1)S(1)}, bf16[1000,4608]{1,0:T(8,128)(2,1)}, u32[]{:S(2)}) %copy-start) | copy-done | bytes 9216024
  32.9 0.0 copy-start.3
  32.9 0.7 copy-done.3
  33.6 5.1 %shard_map.76 = (bf16[512,2304]{1,0:T(8,128)(2,1)S(1)}, s32[4,128]{1,0:T(4,128)S(1)}, f32[128,1000]{1,0:T(8,128)S(1)}) custom-call(s32[36]{0:T(128)S(1)} %concatenate.3.core, bf16[1000,4608]{1,0:T(8,128)(2,1)S(1)} %copy-done, s32[4,128]{1,0:T(4,128)S(1)} %bitcast.17, bf16[128,2304]{1,0:T(8,128)(2,1)S(1)} %bitcast.13), custom_call_target="tpu_custom_call" | custom-call | flops 1000 | bytes 1000 | tf_op jit(solution)/shard_map/pallas_call | solution.py:282
  38.7 0.0 collective-permute-done.2.refs_1_.n2
  38.7 1.8 %collective-permute-done.3.refs_0_.n1 = bf16[128,2304]{1,0:T(8,128)(2,1)S(1)} collective-permute-done((bf16[128,2304]{1,0:T(8,128)(2,1)S(1)}, bf16[128,2304]{1,0:T(8,128)(2,1)S(1)}, u32[]{:S(2)}, u32[]{:S(2)}) %collective-permute-start.3) | collective-permute-done | bytes 589856 | tf_op jit(solution)/shard_map/ppermute | solution.py:48
  40.5 0.0 collective-permute-done.4.refs_2_.n3
  40.5 2.0 %collective-permute-start.5 = (bf16[128,2304]{1,0:T(8,128)(2,1)S(1)}, bf16[128,2304]{1,0:T(8,128)(2,1)S(1)}, u32[]{:S(2)}, u32[]{:S(2)}) collective-permute-start(bf16[128,2304]{1,0:T(8,128)(2,1)S(1)} %collective-permute-done.3.refs_0_.n1), channel_id=1, source_target_pairs={{0,16},{1,17},{2,18},{3,19},{4,20},{5,21},{6,22},{7,23},{8,24},{9,... | collective-permute-start | bytes 1769480 | tf_op jit(solution)/shard_map/ppermute | solution.py:41
  42.5 0.0 collective-permute-start.6
  42.5 0.5 collective-permute-start.7
  43.0 2.6 %shard_map.77.part1 = f32[384,1000]{1,0:T(8,128)S(1)} custom-call(s32[36]{0:T(128)S(1)} %concatenate.3.core, bf16[128,2304]{1,0:T(8,128)(2,1)S(1)} %collective-permute-done.3.refs_0_.n1, bf16[128,2304]{1,0:T(8,128)(2,1)S(1)} %collective-permute-done.2.refs_1_.n2, bf16[128,2304]{1,0:T(8,128)(2,1)S(1)} %collective-permute-done.4.refs_2_.n3, ...), custom_call_target="tpu_custom_call" | custom-call | flops 1000 | bytes 1000 | tf_op jit(solution)/shard_map/pallas_call | solution.py:282
  45.6 0.0 collective-permute-done.1.b0.m0
  45.6 0.0 collective-permute-done.5.b1.m1
  45.6 0.0 collective-permute-done.6.b2.m2
  45.6 0.2 collective-permute-done.7.b3.m3
  45.8 0.0 slice-start
  45.8 0.0 slice-start.1
  45.8 4.7 %shard_map.78 = (f32[512,1000]{1,0:T(8,128)S(1)}, f32[8,128]{1,0:T(8,128)S(1)}, bf16[512,1000]{1,0:T(8,128)(2,1)S(1)}) custom-call(s32[36]{0:T(128)S(1)} %concatenate.3.core, bf16[128,2304]{1,0:T(8,128)(2,1)S(1)} %collective-permute-done.1.b0.m0, bf16[128,2304]{1,0:T(8,128)(2,1)S(1)} %collective-permute-done.5.b1.m1, ...), custom_call_target="tpu_custom_call" | custom-call | flops 1000 | bytes 1000 | tf_op jit(solution)/shard_map/pallas_call | solution.py:282
  50.5 0.6 collective-permute-start.8
  51.1 0.0 slice-start.2
  51.1 3.2 %shard_map.79 = f32[512,2304]{1,0:T(8,128)S(1)} custom-call(s32[36]{0:T(128)S(1)} %concatenate.3.core, bf16[512,1000]{1,0:T(8,128)(2,1)S(1)} %get-tuple-element.42.others, bf16[1000,4608]{1,0:T(8,128)(2,1)S(1)} %copy-done), custom_call_target="tpu_custom_call" | custom-call | flops 1000 | bytes 1000 | tf_op jit(solution)/shard_map/pallas_call | solution.py:282
  54.3 0.0 collective-permute-done.8
  54.3 0.2 collective-permute-start.9
  54.5 0.4 collective-permute-start.10
  54.9 17.1 %all_to_all.16.stats = f32[64,8,128]{2,1,0:T(8,128)S(1)} all-to-all(f32[64,8,128]{2,1,0:T(8,128)S(1)} %broadcast_in_dim.26), channel_id=1, replica_groups=mesh['x'=4,'c'=2,'y'=4,'z'=4] {'x','y','z'}, dimensions={0} | all-to-all | bytes 524288 | tf_op jit(solution)/shard_map/all_to_all | solution.py:366
  72.0 0.0 collective-permute-done.10.target
  72.0 0.0 collective-permute-done.9.received
  72.0 0.0 slice-done
  72.0 0.0 slice-done.1
  72.0 0.0 slice-done.2
  72.0 5.1 %shard_map.80 = (bf16[128,2432]{1,0:T(8,128)(2,1)S(1)}, bf16[128,2432]{1,0:T(8,128)(2,1)S(1)}, bf16[128,2432]{1,0:T(8,128)(2,1)S(1)}, bf16[128,2432]{1,0:T(8,128...) custom-call(s32[36]{0:T(128)S(1)} %concatenate.3.core, f32[512,1000]{1,0:T(8,128)S(1)} %get-tuple-element.40.others, ...), custom_call_target="tpu_custom_call" | custom-call | flops 1000 | bytes 1000 | tf_op jit(solution)/shard_map/pallas_call | solution.py:282
  77.1 0.4 collective-permute-start.11
  77.5 2.4 %collective-permute-start.12 = (bf16[128,2432]{1,0:T(8,128)(2,1)S(1)}, bf16[128,2432]{1,0:T(8,128)(2,1)S(1)}, u32[]{:S(2)}, u32[]{:S(2)}) collective-permute-start(bf16[128,2432]{1,0:T(8,128)(2,1)S(1)} %get-tuple-element.51), channel_id=1, source_target_pairs={{0,96},{1,97},{2,98},{3,99},{4,100},{5,101},{6,102},{7,103},{8,104... | collective-permute-start | bytes 1867784 | tf_op jit(solution)/shard_map/ppermute | solution.py:48
  79.9 0.0 collective-permute-start.13
  79.9 8.7 %shard_map.81 = bf16[1000,4608]{1,0:T(8,128)(2,1)} custom-call(s32[36]{0:T(128)S(1)} %concatenate.3.core, f32[512,1000]{1,0:T(8,128)S(1)} %get-tuple-element.40.others, f32[8,128]{1,0:T(8,128)S(1)} %get-tuple-element.47.marks, s32[4,128]{1,0:T(4,128)S(1)} %get-tuple-element.39.labels, bf16[128,2304]{1,0:T(8,128)(2,1)S(1)} %bitcast.15, ...), custom_call_target="tpu_custom_call" | custom-call | flops 1000 | bytes 1000 | tf_op jit(solution)/shard_map/pallas_call | solution.py:282
  88.6 5.8 %collective-permute-done.11.b1 = bf16[128,2432]{1,0:T(8,128)(2,1)S(1)} collective-permute-done((bf16[128,2432]{1,0:T(8,128)(2,1)S(1)}, bf16[128,2432]{1,0:T(8,128)(2,1)S(1)}, u32[]{:S(2)}, u32[]{:S(2)}) %collective-permute-start.11) | collective-permute-done | bytes 622624 | tf_op jit(solution)/shard_map/ppermute | solution.py:48
  94.5 0.0 collective-permute-done.12.b2
  94.5 0.0 collective-permute-done.13.b3
  94.5 0.9 shard_map.82
  95.3 12.9 %all_to_all.17.blocks = bf16[16,8,2688]{2,1,0:T(8,128)(2,1)S(1)} all-to-all(bf16[16,8,2688]{2,1,0:T(8,128)(2,1)S(1)} %bitcast.16), channel_id=1, replica_groups={{0,1,2,3,4,5,6,7,8,9,10,11,12,13,14,15},{32,33,34,35,36,37,38,39,40,41,..., dimensions={0} | all-to-all | bytes 1376256 | tf_op jit(solution)/shard_map/all_to_all | solution.py:52
  108.2 0.6 shard_map.83
  108.9 3.6 %collective-permute-start.14 = (f32[8,2304]{1,0:T(8,128)S(1)}, f32[8,2304]{1,0:T(8,128)S(1)}, u32[]{:S(2)}, u32[]{:S(2)}) collective-permute-start(f32[8,2304]{1,0:T(8,128)S(1)} %get-tuple-element.54), channel_id=1, source_target_pairs={{0,16},{1,17},{2,18},{3,19},{4,20},{5,21},{6,22},{7,23},{8,24},{9,... | collective-permute-start | bytes 221192 | tf_op jit(solution)/shard_map/ppermute | solution.py:41
  112.4 0.9 collective-permute-done.14.received
  113.4 1.3 %shard_map.84 = (f32[4]{0:T(128)}, f32[4,4608]{1,0:T(4,128)}, f32[4608]{0:T(1024)}) custom-call(s32[36]{0:T(128)S(1)} %concatenate.3.core, f32[8,2304]{1,0:T(8,128)S(1)} %get-tuple-element.53.keep, f32[8,2304]{1,0:T(8,128)S(1)} %collective-permute-done.14.received, f32[4,4608]{1,0:T(4,128)S(1)} %get-tuple-element.55.unit, ...), custom_call_target="tpu_custom_call" | custom-call | flops 1000 | bytes 1000 | tf_op jit(solution)/shard_map/pallas_call | solution.py:282
  (5 shorter events, 0.0 us)
Async XLA Ops:
  0.6 2.6 %collective-permute-start = (bf16[4,4608]{1,0:T(4,128)(2,1)}, bf16[4,4608]{1,0:T(4,128)(2,1)S(1)}, u32[]{:S(2)}, u32[]{:S(2)}) collective-permute-start(bf16[4,4608]{1,0:T(4,128)(2,1)} %mine.1), channel_id=1, source_target_pairs={{0,16},{1,17},{2,18},{3,19},{4,20},{5,21},{6,22},{7,23},{8,24},{9,... | collective-permute-start | bytes 110600 | tf_op jit(solution)/shard_map/ppermute | solution.py:41
  3.2 0.8 copy-start.1
  4.0 0.7 copy-start.2
  23.4 15.3 %collective-permute-start.2 = (bf16[128,2304]{1,0:T(8,128)(2,1)S(1)}, bf16[128,2304]{1,0:T(8,128)(2,1)S(1)}, u32[]{:S(2)}, u32[]{:S(2)}) collective-permute-start(bf16[128,2304]{1,0:T(8,128)(2,1)S(1)} %bitcast.9), channel_id=1, source_target_pairs={{0,64},{1,65},{2,66},{3,67},{4,68},{5,69},{6,70},{7,71},{8,72},{9,... | collective-permute-start | bytes 1769480 | tf_op jit(solution)/shard_map/ppermute | solution.py:48
  26.2 14.2 %collective-permute-start.3 = (bf16[128,2304]{1,0:T(8,128)(2,1)S(1)}, bf16[128,2304]{1,0:T(8,128)(2,1)S(1)}, u32[]{:S(2)}, u32[]{:S(2)}) collective-permute-start(bf16[128,2304]{1,0:T(8,128)(2,1)S(1)} %bitcast.10), channel_id=1, source_target_pairs={{0,96},{1,97},{2,98},{3,99},{4,100},{5,101},{6,102},{7,103},{8,104... | collective-permute-start | bytes 1769480 | tf_op jit(solution)/shard_map/ppermute | solution.py:48
  27.1 13.4 %collective-permute-start.4 = (bf16[128,2304]{1,0:T(8,128)(2,1)S(1)}, bf16[128,2304]{1,0:T(8,128)(2,1)S(1)}, u32[]{:S(2)}, u32[]{:S(2)}) collective-permute-start(bf16[128,2304]{1,0:T(8,128)(2,1)S(1)} %bitcast.11), channel_id=1, source_target_pairs={{0,32},{1,33},{2,34},{3,35},{4,36},{5,37},{6,38},{7,39},{8,40},{9,... | collective-permute-start | bytes 1769480 | tf_op jit(solution)/shard_map/ppermute | solution.py:48
  27.7 17.9 %collective-permute-start.1 = (bf16[128,2304]{1,0:T(8,128)(2,1)S(1)}, bf16[128,2304]{1,0:T(8,128)(2,1)S(1)}, u32[]{:S(2)}, u32[]{:S(2)}) collective-permute-start(bf16[128,2304]{1,0:T(8,128)(2,1)S(1)} %bitcast.12), channel_id=1, source_target_pairs={{0,16},{1,17},{2,18},{3,19},{4,20},{5,21},{6,22},{7,23},{8,24},{9,... | collective-permute-start | bytes 1769480 | tf_op jit(solution)/shard_map/ppermute | solution.py:41
  29.3 3.6 %copy-start = (bf16[1000,4608]{1,0:T(8,128)(2,1)S(1)}, bf16[1000,4608]{1,0:T(8,128)(2,1)}, u32[]{:S(2)}) copy-start(bf16[1000,4608]{1,0:T(8,128)(2,1)} %weight.7) | copy-start | bytes 27648004
  32.9 0.7 copy-start.3
  40.5 5.1 %collective-permute-start.5 = (bf16[128,2304]{1,0:T(8,128)(2,1)S(1)}, bf16[128,2304]{1,0:T(8,128)(2,1)S(1)}, u32[]{:S(2)}, u32[]{:S(2)}) collective-permute-start(bf16[128,2304]{1,0:T(8,128)(2,1)S(1)} %collective-permute-done.3.refs_0_.n1), channel_id=1, source_target_pairs={{0,16},{1,17},{2,18},{3,19},{4,20},{5,21},{6,22},{7,23},{8,24},{9,... | collective-permute-start | bytes 1769480 | tf_op jit(solution)/shard_map/ppermute | solution.py:41
  42.5 3.1 %collective-permute-start.6 = (bf16[128,2304]{1,0:T(8,128)(2,1)S(1)}, bf16[128,2304]{1,0:T(8,128)(2,1)S(1)}, u32[]{:S(2)}, u32[]{:S(2)}) collective-permute-start(bf16[128,2304]{1,0:T(8,128)(2,1)S(1)} %collective-permute-done.2.refs_1_.n2), channel_id=1, source_target_pairs={{0,16},{1,17},{2,18},{3,19},{4,20},{5,21},{6,22},{7,23},{8,24},{9,... | collective-permute-start | bytes 1769480 | tf_op jit(solution)/shard_map/ppermute | solution.py:41
  42.5 3.3 %collective-permute-start.7 = (bf16[128,2304]{1,0:T(8,128)(2,1)S(1)}, bf16[128,2304]{1,0:T(8,128)(2,1)S(1)}, u32[]{:S(2)}, u32[]{:S(2)}) collective-permute-start(bf16[128,2304]{1,0:T(8,128)(2,1)S(1)} %collective-permute-done.4.refs_2_.n3), channel_id=1, source_target_pairs={{0,16},{1,17},{2,18},{3,19},{4,20},{5,21},{6,22},{7,23},{8,24},{9,... | collective-permute-start | bytes 1769480 | tf_op jit(solution)/shard_map/ppermute | solution.py:41
  45.8 26.2 %slice-start = ((s8[9216000]{0:T(1024)(128)(4,1)}), s8[4194304]{0:T(1024)(128)(4,1)S(1)}, s32[]{:S(2)}) async-start(s8[9216000]{0:T(1024)(128)(4,1)} %bitcast.7), calls=%async_computation.3 | async-start | bytes 8388608
  45.8 26.2 %slice-start.1 = ((s8[9216000]{0:T(1024)(128)(4,1)}), s8[4194304]{0:T(1024)(128)(4,1)S(1)}, s32[]{:S(2)}) async-start(s8[9216000]{0:T(1024)(128)(4,1)} %bitcast.7), calls=%async_computation.4 | async-start | bytes 8388608
  50.5 3.8 %collective-permute-start.8 = (f32[8,128]{1,0:T(8,128)S(1)}, f32[8,128]{1,0:T(8,128)S(1)}, u32[]{:S(2)}, u32[]{:S(2)}) collective-permute-start(f32[8,128]{1,0:T(8,128)S(1)} %get-tuple-element.41), channel_id=1, source_target_pairs={{0,16},{1,17},{2,18},{3,19},{4,20},{5,21},{6,22},{7,23},{8,24},{9,... | collective-permute-start | bytes 12296 | tf_op jit(solution)/shard_map/ppermute | solution.py:41
  51.1 20.9 %slice-start.2 = ((s8[9216000]{0:T(1024)(128)(4,1)}), s8[827392]{0:T(1024)(128)(4,1)S(1)}, s32[]{:S(2)}) async-start(s8[9216000]{0:T(1024)(128)(4,1)} %bitcast.7), calls=%async_computation.5 | async-start | bytes 1654784
  54.3 17.7 %collective-permute-start.9 = (f32[512,2304]{1,0:T(8,128)S(1)}, f32[512,2304]{1,0:T(8,128)S(1)}, u32[]{:S(2)}, u32[]{:S(2)}) collective-permute-start(f32[512,2304]{1,0:T(8,128)S(1)} %shard_map.79), channel_id=1, source_target_pairs={{0,16},{1,17},{2,18},{3,19},{4,20},{5,21},{6,22},{7,23},{8,24},{9,... | collective-permute-start | bytes 14155784 | tf_op jit(solution)/shard_map/ppermute | solution.py:41
  54.5 17.5 %collective-permute-start.10 = (bf16[512,2304]{1,0:T(8,128)(2,1)S(1)}, bf16[512,2304]{1,0:T(8,128)(2,1)S(1)}, u32[]{:S(2)}, u32[]{:S(2)}) collective-permute-start(bf16[512,2304]{1,0:T(8,128)(2,1)S(1)} %get-tuple-element.45), channel_id=1, source_target_pairs={{0,16},{1,17},{2,18},{3,19},{4,20},{5,21},{6,22},{7,23},{8,24},{9,... | collective-permute-start | bytes 7077896 | tf_op jit(solution)/shard_map/ppermute | solution.py:41
  77.1 17.3 %collective-permute-start.11 = (bf16[128,2432]{1,0:T(8,128)(2,1)S(1)}, bf16[128,2432]{1,0:T(8,128)(2,1)S(1)}, u32[]{:S(2)}, u32[]{:S(2)}) collective-permute-start(bf16[128,2432]{1,0:T(8,128)(2,1)S(1)} %get-tuple-element.50), channel_id=1, source_target_pairs={{0,32},{1,33},{2,34},{3,35},{4,36},{5,37},{6,38},{7,39},{8,40},{9,... | collective-permute-start | bytes 1867784 | tf_op jit(solution)/shard_map/ppermute | solution.py:48
  77.5 16.9 %collective-permute-start.12 = (bf16[128,2432]{1,0:T(8,128)(2,1)S(1)}, bf16[128,2432]{1,0:T(8,128)(2,1)S(1)}, u32[]{:S(2)}, u32[]{:S(2)}) collective-permute-start(bf16[128,2432]{1,0:T(8,128)(2,1)S(1)} %get-tuple-element.51), channel_id=1, source_target_pairs={{0,96},{1,97},{2,98},{3,99},{4,100},{5,101},{6,102},{7,103},{8,104... | collective-permute-start | bytes 1867784 | tf_op jit(solution)/shard_map/ppermute | solution.py:48
  79.9 14.6 %collective-permute-start.13 = (bf16[128,2432]{1,0:T(8,128)(2,1)S(1)}, bf16[128,2432]{1,0:T(8,128)(2,1)S(1)}, u32[]{:S(2)}, u32[]{:S(2)}) collective-permute-start(bf16[128,2432]{1,0:T(8,128)(2,1)S(1)} %get-tuple-element.52), channel_id=1, source_target_pairs={{0,64},{1,65},{2,66},{3,67},{4,68},{5,69},{6,70},{7,71},{8,72},{9,... | collective-permute-start | bytes 1867784 | tf_op jit(solution)/shard_map/ppermute | solution.py:48
  108.9 4.5 %collective-permute-start.14 = (f32[8,2304]{1,0:T(8,128)S(1)}, f32[8,2304]{1,0:T(8,128)S(1)}, u32[]{:S(2)}, u32[]{:S(2)}) collective-permute-start(f32[8,2304]{1,0:T(8,128)S(1)} %get-tuple-element.54), channel_id=1, source_target_pairs={{0,16},{1,17},{2,18},{3,19},{4,20},{5,21},{6,22},{7,23},{8,24},{9,... | collective-permute-start | bytes 221192 | tf_op jit(solution)/shard_map/ppermute | solution.py:41

commit v7 on v4

--- a/solution.py
+++ b/solution.py
@@ -140,10 +140,11 @@
             out[pl.ds(row, chunk), some] += part[chunk * at : chunk * (at + 1), some]
         for j in range(4):
             lines = slice(128 * j, 128 * (j + 1))
-            capped = soft_cap * jnp.tanh(out[lines, some] / soft_cap)
+            level = jnp.tanh(out[lines, some] * (1.0 / soft_cap))
+            capped = soft_cap * level
             hit = lax.broadcasted_iota(jnp.int32, capped.shape, 1) + start == marks[j]
             exps = jnp.exp(capped)
-            slope = 1.0 - (capped / soft_cap) ** 2
+            slope = 1.0 - level * level
             rest = jnp.where(hit, 0.0, exps * slope)
             out[lines, some] = rest
             others[lines, some] = rest.astype(bf16)

time: 115 us -> 115 us (level)
  no operation moved by 1% of the time
where the time goes in v7:
time: 115 us; the launch traced here: 114 us
  blocking collectives  47.9 us (42%)
  Pallas kernels  33.2 us (29%)
  starting transfers between devices  16.6 us (14%)
  waiting for transfers between devices  9.42 us (8%)
  local copies, waits for them, and re-layouts  5.78 us (5%)
    pallas_call x11, Pallas kernels, call(): pl.pallas_call(kernel, grid_spec=pltpu.PrefetchScalarGridSpec(num_scalar_...  33.2 us
    all_to_all x2, blocking collectives, over_plane(): lax.all_to_all(array, every, 0, 0, axis_index_groups=planes, tiled=True)  30.8 us
    all_to_all x1, blocking collectives, body(): stats = lax.all_to_all(stats, chips, 0, 0, tiled=True)  17.1 us
    ppermute x9, starting transfers between devices, other_core(): return lax.ppermute(array, every, swap_cores)  9.82 us
    ppermute x6, waiting for transfers between devices, along_line(): return lax.ppermute(array, every, pairs)  8.28 us
    ppermute x6, starting transfers between devices, along_line(): return lax.ppermute(array, every, pairs)  6.77 us
    unnamed x8, local copies, waits for them, and re-layouts  5.24 us
  transfers between devices with their start and end apart: 15, of which 4 were waited for; matrix products, arithmetic and copies ran while one was open for 1% of the time, Pallas kernels for 17%

profile of v7, /device:TPU:1, one launch (start us, length us, event | category | flops | bytes accessed | tf_op | source)
XLA Modules:
  0.0 114.5 jit_solution(16543045004789276313)
XLA Ops:
  0.6 1.5 %collective-permute-start = (bf16[4,4608]{1,0:T(4,128)(2,1)}, bf16[4,4608]{1,0:T(4,128)(2,1)S(1)}, u32[]{:S(2)}, u32[]{:S(2)}) collective-permute-start(bf16[4,4608]{1,0:T(4,128)(2,1)} %mine.1), channel_id=1, source_target_pairs={{0,16},{1,17},{2,18},{3,19},{4,20},{5,21},{6,22},{7,23},{8,24},{9,... | collective-permute-start | bytes 110600 | tf_op jit(solution)/shard_map/ppermute | solution.py:41
  2.2 0.1 add_select_fusion
  2.2 0.7 broadcast_subtract_fusion
  2.9 0.1 select_n.59
  3.0 0.1 select_n.57
  3.1 0.1 sub.26
  3.2 0.1 sub.28.labels
  3.4 0.1 concatenate.3.core
  3.5 0.0 collective-permute-done.theirs
  3.5 0.0 copy-start.2
  3.5 0.8 copy-done.2
  4.2 0.0 copy-start.3
  4.2 0.7 copy-done.3
  5.0 0.7 shard_map.75
  5.7 17.9 %all_to_all.15 = bf16[16,8,2304]{2,1,0:T(8,128)(2,1)S(1)} all-to-all(bf16[16,8,2304]{2,1,0:T(8,128)(2,1)S(1)} %get-tuple-element.37), channel_id=1, replica_groups={{0,1,2,3,4,5,6,7,8,9,10,11,12,13,14,15},{32,33,34,35,36,37,38,39,40,41,..., dimensions={0} | all-to-all | bytes 1179648 | tf_op jit(solution)/shard_map/all_to_all | solution.py:52
  23.7 1.2 %collective-permute-start.4 = (bf16[128,2304]{1,0:T(8,128)(2,1)S(1)}, bf16[128,2304]{1,0:T(8,128)(2,1)S(1)}, u32[]{:S(2)}, u32[]{:S(2)}) collective-permute-start(bf16[128,2304]{1,0:T(8,128)(2,1)S(1)} %bitcast.6), channel_id=1, source_target_pairs={{0,32},{1,33},{2,34},{3,35},{4,36},{5,37},{6,38},{7,39},{8,40},{9,... | collective-permute-start | bytes 1769480 | tf_op jit(solution)/shard_map/ppermute | solution.py:48
  24.9 1.5 %collective-permute-start.3 = (bf16[128,2304]{1,0:T(8,128)(2,1)S(1)}, bf16[128,2304]{1,0:T(8,128)(2,1)S(1)}, u32[]{:S(2)}, u32[]{:S(2)}) collective-permute-start(bf16[128,2304]{1,0:T(8,128)(2,1)S(1)} %bitcast.7), channel_id=1, source_target_pairs={{0,96},{1,97},{2,98},{3,99},{4,100},{5,101},{6,102},{7,103},{8,104... | collective-permute-start | bytes 1769480 | tf_op jit(solution)/shard_map/ppermute | solution.py:48
  26.3 1.3 %collective-permute-start.2 = (bf16[128,2304]{1,0:T(8,128)(2,1)S(1)}, bf16[128,2304]{1,0:T(8,128)(2,1)S(1)}, u32[]{:S(2)}, u32[]{:S(2)}) collective-permute-start(bf16[128,2304]{1,0:T(8,128)(2,1)S(1)} %bitcast.8), channel_id=1, source_target_pairs={{0,64},{1,65},{2,66},{3,67},{4,68},{5,69},{6,70},{7,71},{8,72},{9,... | collective-permute-start | bytes 1769480 | tf_op jit(solution)/shard_map/ppermute | solution.py:48
  27.7 1.6 %collective-permute-start.1 = (bf16[128,2304]{1,0:T(8,128)(2,1)S(1)}, bf16[128,2304]{1,0:T(8,128)(2,1)S(1)}, u32[]{:S(2)}, u32[]{:S(2)}) collective-permute-start(bf16[128,2304]{1,0:T(8,128)(2,1)S(1)} %bitcast.9), channel_id=1, source_target_pairs={{0,16},{1,17},{2,18},{3,19},{4,20},{5,21},{6,22},{7,23},{8,24},{9,... | collective-permute-start | bytes 1769480 | tf_op jit(solution)/shard_map/ppermute | solution.py:41
  29.3 0.0 copy-start
  29.3 3.6 %copy-done = bf16[1000,4608]{1,0:T(8,128)(2,1)S(1)} copy-done((bf16[1000,4608]{1,0:T(8,128)(2,1)S(1)}, bf16[1000,4608]{1,0:T(8,128)(2,1)}, u32[]{:S(2)}) %copy-start) | copy-done | bytes 9216024
  32.9 0.0 copy-start.1
  32.9 3.5 %shard_map.76 = bf16[512,2304]{1,0:T(8,128)(2,1)S(1)} custom-call(s32[35]{0:T(128)S(1)} %concatenate.3.core, bf16[1000,4608]{1,0:T(8,128)(2,1)S(1)} %copy-done, s32[4,128]{1,0:T(4,128)S(1)} %sub.28.labels), custom_call_target="tpu_custom_call" | custom-call | flops 1000 | bytes 1000 | tf_op jit(solution)/shard_map/pallas_call | solution.py:275
  36.4 0.1 copy-done.1
  36.5 2.1 %shard_map.77.part0 = f32[128,1000]{1,0:T(8,128)S(1)} custom-call(s32[35]{0:T(128)S(1)} %concatenate.3.core, bf16[128,2304]{1,0:T(8,128)(2,1)S(1)} %bitcast.10, bf16[1000,4608]{1,0:T(8,128)(2,1)S(1)} %copy-done.1), custom_call_target="tpu_custom_call" | custom-call | flops 1000 | bytes 1000 | tf_op jit(solution)/shard_map/pallas_call | solution.py:275
  38.6 0.0 collective-permute-done.4.refs_2_.n3
  38.6 0.0 collective-permute-done.3.refs_0_.n1
  38.6 2.4 %collective-permute-done.2.refs_1_.n2 = bf16[128,2304]{1,0:T(8,128)(2,1)S(1)} collective-permute-done((bf16[128,2304]{1,0:T(8,128)(2,1)S(1)}, bf16[128,2304]{1,0:T(8,128)(2,1)S(1)}, u32[]{:S(2)}, u32[]{:S(2)}) %collective-permute-start.2) | collective-permute-done | bytes 589856 | tf_op jit(solution)/shard_map/ppermute | solution.py:48
  41.0 1.6 %collective-permute-start.5 = (bf16[128,2304]{1,0:T(8,128)(2,1)S(1)}, bf16[128,2304]{1,0:T(8,128)(2,1)S(1)}, u32[]{:S(2)}, u32[]{:S(2)}) collective-permute-start(bf16[128,2304]{1,0:T(8,128)(2,1)S(1)} %collective-permute-done.3.refs_0_.n1), channel_id=1, source_target_pairs={{0,16},{1,17},{2,18},{3,19},{4,20},{5,21},{6,22},{7,23},{8,24},{9,... | collective-permute-start | bytes 1769480 | tf_op jit(solution)/shard_map/ppermute | solution.py:41
  42.6 0.0 collective-permute-start.6
  42.6 0.5 collective-permute-start.7
  43.1 2.6 %shard_map.78.part1 = f32[384,1000]{1,0:T(8,128)S(1)} custom-call(s32[35]{0:T(128)S(1)} %concatenate.3.core, bf16[128,2304]{1,0:T(8,128)(2,1)S(1)} %collective-permute-done.3.refs_0_.n1, bf16[128,2304]{1,0:T(8,128)(2,1)S(1)} %collective-permute-done.2.refs_1_.n2, bf16[128,2304]{1,0:T(8,128)(2,1)S(1)} %collective-permute-done.4.refs_2_.n3, ...), custom_call_target="tpu_custom_call" | custom-call | flops 1000 | bytes 1000 | tf_op jit(solution)/shard_map/pallas_call | solution.py:275
  45.7 0.0 collective-permute-done.1.b0.m0
  45.7 0.0 collective-permute-done.5.b1.m1
  45.7 0.0 collective-permute-done.6.b2.m2
  45.7 0.2 collective-permute-done.7.b3.m3
  45.9 4.6 %shard_map.79 = (f32[512,1000]{1,0:T(8,128)S(1)}, f32[8,128]{1,0:T(8,128)S(1)}, bf16[512,1000]{1,0:T(8,128)(2,1)S(1)}) custom-call(s32[35]{0:T(128)S(1)} %concatenate.3.core, bf16[128,2304]{1,0:T(8,128)(2,1)S(1)} %collective-permute-done.1.b0.m0, bf16[128,2304]{1,0:T(8,128)(2,1)S(1)} %collective-permute-done.5.b1.m1, ...), custom_call_target="tpu_custom_call" | custom-call | flops 1000 | bytes 1000 | tf_op jit(solution)/shard_map/pallas_call | solution.py:275
  50.5 0.4 collective-permute-start.8
  51.0 0.3 collective-permute-start.10
  51.2 3.2 %shard_map.80 = bf16[512,2304]{1,0:T(8,128)(2,1)S(1)} custom-call(s32[35]{0:T(128)S(1)} %concatenate.3.core, bf16[512,1000]{1,0:T(8,128)(2,1)S(1)} %get-tuple-element.48.others, bf16[1000,4608]{1,0:T(8,128)(2,1)S(1)} %copy-done.1), custom_call_target="tpu_custom_call" | custom-call | flops 1000 | bytes 1000 | tf_op jit(solution)/shard_map/pallas_call | solution.py:275
  54.4 0.0 collective-permute-done.8
  54.4 0.3 collective-permute-start.9
  54.8 17.1 %all_to_all.16.stats = f32[64,8,128]{2,1,0:T(8,128)S(1)} all-to-all(f32[64,8,128]{2,1,0:T(8,128)S(1)} %broadcast_in_dim.22), channel_id=1, replica_groups=mesh['x'=4,'c'=2,'y'=4,'z'=4] {'x','y','z'}, dimensions={0} | all-to-all | bytes 524288 | tf_op jit(solution)/shard_map/all_to_all | solution.py:362
  71.9 0.0 collective-permute-done.10.target
  71.9 0.0 collective-permute-done.9.received
  71.9 5.0 %shard_map.81 = (bf16[128,2432]{1,0:T(8,128)(2,1)S(1)}, bf16[128,2432]{1,0:T(8,128)(2,1)S(1)}, bf16[128,2432]{1,0:T(8,128)(2,1)S(1)}, bf16[128,2432]{1,0:T(8,128...) custom-call(s32[35]{0:T(128)S(1)} %concatenate.3.core, f32[512,1000]{1,0:T(8,128)S(1)} %get-tuple-element.46.others, ...), custom_call_target="tpu_custom_call" | custom-call | flops 1000 | bytes 1000 | tf_op jit(solution)/shard_map/pallas_call | solution.py:275
  76.9 0.3 collective-permute-start.11
  77.2 2.4 %collective-permute-start.12 = (bf16[128,2432]{1,0:T(8,128)(2,1)S(1)}, bf16[128,2432]{1,0:T(8,128)(2,1)S(1)}, u32[]{:S(2)}, u32[]{:S(2)}) collective-permute-start(bf16[128,2432]{1,0:T(8,128)(2,1)S(1)} %get-tuple-element.57), channel_id=1, source_target_pairs={{0,96},{1,97},{2,98},{3,99},{4,100},{5,101},{6,102},{7,103},{8,104... | collective-permute-start | bytes 1867784 | tf_op jit(solution)/shard_map/ppermute | solution.py:48
  79.6 0.0 collective-permute-start.13
  79.6 8.7 %shard_map.82 = bf16[1000,4608]{1,0:T(8,128)(2,1)} custom-call(s32[35]{0:T(128)S(1)} %concatenate.3.core, f32[512,1000]{1,0:T(8,128)S(1)} %get-tuple-element.46.others, f32[8,128]{1,0:T(8,128)S(1)} %get-tuple-element.53.marks, s32[4,128]{1,0:T(4,128)S(1)} %sub.28.labels, bf16[128,2304]{1,0:T(8,128)(2,1)S(1)} %bitcast.12, ...), custom_call_target="tpu_custom_call" | custom-call | flops 1000 | bytes 1000 | tf_op jit(solution)/shard_map/pallas_call | solution.py:275
  88.4 5.8 %collective-permute-done.11.b1 = bf16[128,2432]{1,0:T(8,128)(2,1)S(1)} collective-permute-done((bf16[128,2432]{1,0:T(8,128)(2,1)S(1)}, bf16[128,2432]{1,0:T(8,128)(2,1)S(1)}, u32[]{:S(2)}, u32[]{:S(2)}) %collective-permute-start.11) | collective-permute-done | bytes 622624 | tf_op jit(solution)/shard_map/ppermute | solution.py:48
  94.2 0.0 collective-permute-done.12.b2
  94.2 0.0 collective-permute-done.13.b3
  94.2 0.8 shard_map.83
  95.1 12.8 %all_to_all.17.blocks = bf16[16,8,2688]{2,1,0:T(8,128)(2,1)S(1)} all-to-all(bf16[16,8,2688]{2,1,0:T(8,128)(2,1)S(1)} %bitcast.13), channel_id=1, replica_groups={{0,1,2,3,4,5,6,7,8,9,10,11,12,13,14,15},{32,33,34,35,36,37,38,39,40,41,..., dimensions={0} | all-to-all | bytes 1376256 | tf_op jit(solution)/shard_map/all_to_all | solution.py:52
  107.9 0.6 shard_map.84
  108.6 3.7 %collective-permute-start.14 = (f32[8,2304]{1,0:T(8,128)S(1)}, f32[8,2304]{1,0:T(8,128)S(1)}, u32[]{:S(2)}, u32[]{:S(2)}) collective-permute-start(f32[8,2304]{1,0:T(8,128)S(1)} %get-tuple-element.60), channel_id=1, source_target_pairs={{0,16},{1,17},{2,18},{3,19},{4,20},{5,21},{6,22},{7,23},{8,24},{9,... | collective-permute-start | bytes 221192 | tf_op jit(solution)/shard_map/ppermute | solution.py:41
  112.2 0.9 collective-permute-done.14.received
  113.1 1.3 %shard_map.85 = (f32[4]{0:T(128)}, f32[4,4608]{1,0:T(4,128)}, f32[4608]{0:T(1024)}) custom-call(s32[35]{0:T(128)S(1)} %concatenate.3.core, f32[8,2304]{1,0:T(8,128)S(1)} %get-tuple-element.59.keep, f32[8,2304]{1,0:T(8,128)S(1)} %collective-permute-done.14.received, f32[4,4608]{1,0:T(4,128)S(1)} %get-tuple-element.61.unit, ...), custom_call_target="tpu_custom_call" | custom-call | flops 1000 | bytes 1000 | tf_op jit(solution)/shard_map/pallas_call | solution.py:275
  (5 shorter events, 0.1 us)
Async XLA Ops:
  0.6 2.8 %collective-permute-start = (bf16[4,4608]{1,0:T(4,128)(2,1)}, bf16[4,4608]{1,0:T(4,128)(2,1)S(1)}, u32[]{:S(2)}, u32[]{:S(2)}) collective-permute-start(bf16[4,4608]{1,0:T(4,128)(2,1)} %mine.1), channel_id=1, source_target_pairs={{0,16},{1,17},{2,18},{3,19},{4,20},{5,21},{6,22},{7,23},{8,24},{9,... | collective-permute-start | bytes 110600 | tf_op jit(solution)/shard_map/ppermute | solution.py:41
  3.5 0.8 copy-start.2
  4.2 0.7 copy-start.3
  23.7 14.9 %collective-permute-start.4 = (bf16[128,2304]{1,0:T(8,128)(2,1)S(1)}, bf16[128,2304]{1,0:T(8,128)(2,1)S(1)}, u32[]{:S(2)}, u32[]{:S(2)}) collective-permute-start(bf16[128,2304]{1,0:T(8,128)(2,1)S(1)} %bitcast.6), channel_id=1, source_target_pairs={{0,32},{1,33},{2,34},{3,35},{4,36},{5,37},{6,38},{7,39},{8,40},{9,... | collective-permute-start | bytes 1769480 | tf_op jit(solution)/shard_map/ppermute | solution.py:48
  24.9 13.7 %collective-permute-start.3 = (bf16[128,2304]{1,0:T(8,128)(2,1)S(1)}, bf16[128,2304]{1,0:T(8,128)(2,1)S(1)}, u32[]{:S(2)}, u32[]{:S(2)}) collective-permute-start(bf16[128,2304]{1,0:T(8,128)(2,1)S(1)} %bitcast.7), channel_id=1, source_target_pairs={{0,96},{1,97},{2,98},{3,99},{4,100},{5,101},{6,102},{7,103},{8,104... | collective-permute-start | bytes 1769480 | tf_op jit(solution)/shard_map/ppermute | solution.py:48
  26.3 14.7 %collective-permute-start.2 = (bf16[128,2304]{1,0:T(8,128)(2,1)S(1)}, bf16[128,2304]{1,0:T(8,128)(2,1)S(1)}, u32[]{:S(2)}, u32[]{:S(2)}) collective-permute-start(bf16[128,2304]{1,0:T(8,128)(2,1)S(1)} %bitcast.8), channel_id=1, source_target_pairs={{0,64},{1,65},{2,66},{3,67},{4,68},{5,69},{6,70},{7,71},{8,72},{9,... | collective-permute-start | bytes 1769480 | tf_op jit(solution)/shard_map/ppermute | solution.py:48
  27.7 18.0 %collective-permute-start.1 = (bf16[128,2304]{1,0:T(8,128)(2,1)S(1)}, bf16[128,2304]{1,0:T(8,128)(2,1)S(1)}, u32[]{:S(2)}, u32[]{:S(2)}) collective-permute-start(bf16[128,2304]{1,0:T(8,128)(2,1)S(1)} %bitcast.9), channel_id=1, source_target_pairs={{0,16},{1,17},{2,18},{3,19},{4,20},{5,21},{6,22},{7,23},{8,24},{9,... | collective-permute-start | bytes 1769480 | tf_op jit(solution)/shard_map/ppermute | solution.py:41
  29.3 3.6 %copy-start = (bf16[1000,4608]{1,0:T(8,128)(2,1)S(1)}, bf16[1000,4608]{1,0:T(8,128)(2,1)}, u32[]{:S(2)}) copy-start(bf16[1000,4608]{1,0:T(8,128)(2,1)} %weight.7) | copy-start | bytes 27648004
  32.9 3.6 %copy-start.1 = (bf16[1000,4608]{1,0:T(8,128)(2,1)S(1)}, bf16[1000,4608]{1,0:T(8,128)(2,1)}, u32[]{:S(2)}) copy-start(bf16[1000,4608]{1,0:T(8,128)(2,1)} %weight.7) | copy-start | bytes 27648004
  41.0 4.7 %collective-permute-start.5 = (bf16[128,2304]{1,0:T(8,128)(2,1)S(1)}, bf16[128,2304]{1,0:T(8,128)(2,1)S(1)}, u32[]{:S(2)}, u32[]{:S(2)}) collective-permute-start(bf16[128,2304]{1,0:T(8,128)(2,1)S(1)} %collective-permute-done.3.refs_0_.n1), channel_id=1, source_target_pairs={{0,16},{1,17},{2,18},{3,19},{4,20},{5,21},{6,22},{7,23},{8,24},{9,... | collective-permute-start | bytes 1769480 | tf_op jit(solution)/shard_map/ppermute | solution.py:41
  42.6 3.1 %collective-permute-start.6 = (bf16[128,2304]{1,0:T(8,128)(2,1)S(1)}, bf16[128,2304]{1,0:T(8,128)(2,1)S(1)}, u32[]{:S(2)}, u32[]{:S(2)}) collective-permute-start(bf16[128,2304]{1,0:T(8,128)(2,1)S(1)} %collective-permute-done.2.refs_1_.n2), channel_id=1, source_target_pairs={{0,16},{1,17},{2,18},{3,19},{4,20},{5,21},{6,22},{7,23},{8,24},{9,... | collective-permute-start | bytes 1769480 | tf_op jit(solution)/shard_map/ppermute | solution.py:41
  42.6 3.3 %collective-permute-start.7 = (bf16[128,2304]{1,0:T(8,128)(2,1)S(1)}, bf16[128,2304]{1,0:T(8,128)(2,1)S(1)}, u32[]{:S(2)}, u32[]{:S(2)}) collective-permute-start(bf16[128,2304]{1,0:T(8,128)(2,1)S(1)} %collective-permute-done.4.refs_2_.n3), channel_id=1, source_target_pairs={{0,16},{1,17},{2,18},{3,19},{4,20},{5,21},{6,22},{7,23},{8,24},{9,... | collective-permute-start | bytes 1769480 | tf_op jit(solution)/shard_map/ppermute | solution.py:41
  50.5 3.9 %collective-permute-start.8 = (f32[8,128]{1,0:T(8,128)S(1)}, f32[8,128]{1,0:T(8,128)S(1)}, u32[]{:S(2)}, u32[]{:S(2)}) collective-permute-start(f32[8,128]{1,0:T(8,128)S(1)} %get-tuple-element.47), channel_id=1, source_target_pairs={{0,16},{1,17},{2,18},{3,19},{4,20},{5,21},{6,22},{7,23},{8,24},{9,... | collective-permute-start | bytes 12296 | tf_op jit(solution)/shard_map/ppermute | solution.py:41
  51.0 20.9 %collective-permute-start.10 = (bf16[512,2304]{1,0:T(8,128)(2,1)S(1)}, bf16[512,2304]{1,0:T(8,128)(2,1)S(1)}, u32[]{:S(2)}, u32[]{:S(2)}) collective-permute-start(bf16[512,2304]{1,0:T(8,128)(2,1)S(1)} %shard_map.76), channel_id=1, source_target_pairs={{0,16},{1,17},{2,18},{3,19},{4,20},{5,21},{6,22},{7,23},{8,24},{9,... | collective-permute-start | bytes 7077896 | tf_op jit(solution)/shard_map/ppermute | solution.py:41
  54.4 17.4 %collective-permute-start.9 = (bf16[512,2304]{1,0:T(8,128)(2,1)S(1)}, bf16[512,2304]{1,0:T(8,128)(2,1)S(1)}, u32[]{:S(2)}, u32[]{:S(2)}) collective-permute-start(bf16[512,2304]{1,0:T(8,128)(2,1)S(1)} %shard_map.80), channel_id=1, source_target_pairs={{0,16},{1,17},{2,18},{3,19},{4,20},{5,21},{6,22},{7,23},{8,24},{9,... | collective-permute-start | bytes 7077896 | tf_op jit(solution)/shard_map/ppermute | solution.py:41
  76.9 17.3 %collective-permute-start.11 = (bf16[128,2432]{1,0:T(8,128)(2,1)S(1)}, bf16[128,2432]{1,0:T(8,128)(2,1)S(1)}, u32[]{:S(2)}, u32[]{:S(2)}) collective-permute-start(bf16[128,2432]{1,0:T(8,128)(2,1)S(1)} %get-tuple-element.56), channel_id=1, source_target_pairs={{0,32},{1,33},{2,34},{3,35},{4,36},{5,37},{6,38},{7,39},{8,40},{9,... | collective-permute-start | bytes 1867784 | tf_op jit(solution)/shard_map/ppermute | solution.py:48
  77.2 17.0 %collective-permute-start.12 = (bf16[128,2432]{1,0:T(8,128)(2,1)S(1)}, bf16[128,2432]{1,0:T(8,128)(2,1)S(1)}, u32[]{:S(2)}, u32[]{:S(2)}) collective-permute-start(bf16[128,2432]{1,0:T(8,128)(2,1)S(1)} %get-tuple-element.57), channel_id=1, source_target_pairs={{0,96},{1,97},{2,98},{3,99},{4,100},{5,101},{6,102},{7,103},{8,104... | collective-permute-start | bytes 1867784 | tf_op jit(solution)/shard_map/ppermute | solution.py:48
  79.6 14.6 %collective-permute-start.13 = (bf16[128,2432]{1,0:T(8,128)(2,1)S(1)}, bf16[128,2432]{1,0:T(8,128)(2,1)S(1)}, u32[]{:S(2)}, u32[]{:S(2)}) collective-permute-start(bf16[128,2432]{1,0:T(8,128)(2,1)S(1)} %get-tuple-element.58), channel_id=1, source_target_pairs={{0,64},{1,65},{2,66},{3,67},{4,68},{5,69},{6,70},{7,71},{8,72},{9,... | collective-permute-start | bytes 1867784 | tf_op jit(solution)/shard_map/ppermute | solution.py:48
  108.6 4.6 %collective-permute-start.14 = (f32[8,2304]{1,0:T(8,128)S(1)}, f32[8,2304]{1,0:T(8,128)S(1)}, u32[]{:S(2)}, u32[]{:S(2)}) collective-permute-start(f32[8,2304]{1,0:T(8,128)S(1)} %get-tuple-element.60), channel_id=1, source_target_pairs={{0,16},{1,17},{2,18},{3,19},{4,20},{5,21},{6,22},{7,23},{8,24},{9,... | collective-permute-start | bytes 221192 | tf_op jit(solution)/shard_map/ppermute | solution.py:41
